TPU v7x, 128 devices: a whole 4x4x4 slice. The times are simulated.
128 devices in a mesh: base: 8 (over z, x_lo), inst: 16 (over y, x_hi, core).
Axes of the slice: x: 4 (x_hi: 2, x_lo: 2; x = x_hi * 2 + x_lo), y: 4, z: 4, core: 2. Of those that a mesh axis runs over, the one named last changes fastest.
Arguments:
- base_pre: bfloat16 [4096, 16384], P(('base', 'inst'))
- inst_pre: bfloat16 [4096, 16384], P(('base', 'inst'))
- base_support: int32 [4096, 128], P(('base', 'inst')), may hold values from 0 to 16383, all different within a row
- inst_support: int32 [4096, 128], P(('base', 'inst')), may hold values from 0 to 16383, all different within a row
Outputs:
- scores: float32 [16384, 16384], P('base', 'inst')
Inputs may be any that keep to these rules, and one draw needn't show every extreme that they name: `base_support`: the 128 indices of a row are distinct latents. `inst_support`: the 128 indices of a row are distinct latents.
All inputs are finite; a program needn't handle non-finite values.
Results may differ from a plain program's by a relative error of at most 0.004.
Values may be sent and summed in bfloat16 or wider, within the bound.
No kernel may reach another device: no remote copies, remote signals or barrier semaphores. Data moves between devices by JAX's collectives and lax.ppermute only.
A program may use at most 128 MiB of HBM per device.

v0:
```python
import jax
import jax.numpy as jnp
from jax import lax
from jax.sharding import PartitionSpec as P


def emphasize(pre, support):
    pre32 = pre.astype(jnp.float32)
    scale = lax.rsqrt(jnp.mean(pre32 * pre32, axis=1, keepdims=True) + 1e-06)
    rows = jnp.arange(pre.shape[0], dtype=jnp.int32)[:, None]
    active = jnp.zeros(pre.shape, jnp.float32).at[rows, support].set(1.0)
    return (pre32 * scale * (1.0 + 3.0 * active)).astype(jnp.bfloat16)


def squared_sums(codes):
    wide = codes.astype(jnp.float32)
    return jnp.sum(wide * wide, axis=0)


def per_device(base_pre, inst_pre, base_support, inst_support):
    tok_rows = base_pre.shape[0]
    base_count = lax.axis_size("base")
    inst_count = lax.axis_size("inst")
    base_codes = emphasize(base_pre, base_support)
    inst_codes = emphasize(inst_pre, inst_support)
    base_rows = lax.all_to_all(base_codes, "base", split_axis=1, concat_axis=0, tiled=True)
    column_part = lax.all_to_all(inst_codes, "inst", split_axis=1, concat_axis=0, tiled=True)
    gathered = lax.all_gather(column_part, "base", axis=0, tiled=True)
    inst_block = (
        gathered.reshape(base_count, inst_count, tok_rows, -1)
        .transpose(1, 0, 2, 3)
        .reshape(base_count * inst_count * tok_rows, -1)
    )
    total = inst_block.shape[0]
    inst_sq = squared_sums(inst_block)
    base_block = lax.all_gather(base_rows, "inst", axis=0, tiled=True)
    gram = lax.dot_general(
        base_block, inst_block, (((0,), (0,)), ((), ())), preferred_element_type=jnp.float32
    )
    base_sq = squared_sums(base_block)
    base_rms = jnp.sqrt(base_sq / total + 1e-06)
    inst_rms = jnp.sqrt(inst_sq / total + 1e-06)
    return gram / (jnp.sqrt(jnp.float32(total)) * base_rms[:, None] * inst_rms[None, :])


def solution(mesh):
    in_specs = (
        P(("base", "inst"), None),
        P(("base", "inst"), None),
        P(("base", "inst"), None),
        P(("base", "inst"), None),
    )
    out_specs = P("base", "inst")
    return jax.shard_map(
        per_device, mesh=mesh, in_specs=in_specs, out_specs=out_specs, check_vma=False
    )
```

profile of v0, /device:TPU:1, one launch (start us, length us, event | category | flops | bytes accessed | tf_op | source)
XLA Modules:
  0.0 394.9 jit_solution(7022140366967942130)
XLA Ops:
  6.5 1.5 fusion.3
  8.1 0.7 fusion.10
  8.8 0.7 fusion.11
  9.5 0.7 and_reduce_fusion
  10.3 0.7 multiply_reduce_fusion.2
  11.0 16.0 %scatter_custom_fusion.1 = f32[524288]{0:T(1024)S(1)} fusion(s32[4096]{0:T(1024)S(1)} %get-tuple-element.9, f32[4096]{0:T(1024)S(1)} %broadcast.104, f32[]{:T(128)} %constant.9.clone.1), kind=kCustom, calls=%fused_computation.19 | custom fusion | bytes 2097156
  27.1 1.5 multiply_add_fusion
  28.6 1.8 reshape.59
  30.4 0.0 copy-done.1
  30.4 0.3 fusion.5
  30.7 1.0 copy.17
  31.8 8.4 %all-to-all-start.1 = ((bf16[32,16,1024]{2,0,1:T(8,128)(2,1)}), bf16[32,16,1024]{2,0,1:T(8,128)(2,1)S(1)}, u32[]{:S(2)}, u32[]{:S(2)}) async-start(bf16[32,16,1024]{2,0,1:T(8,128)(2,1)} %bitcast.27), calls=%async_computation.1 | async-start | bytes 2097152 | tf_op jit(solution)/shard_map/all_to_all | solution.py:27
  40.2 0.0 all-gather.5.cloned.1.call-start
  40.3 16.0 %scatter_custom_fusion = f32[524288]{0:T(1024)S(1)} fusion(s32[4096]{0:T(1024)S(1)} %get-tuple-element.10, f32[4096]{0:T(1024)S(1)} %broadcast.104, f32[]{:T(128)} %constant.9.clone.1), kind=kCustom, calls=%fused_computation.21 | custom fusion | bytes 2097156
  56.3 1.1 all-to-all-done.1
  57.4 1.1 copy-done.3
  58.5 0.0 all-gather.5.cloned.1.call-update
  58.5 0.0 all-gather.3.cloned.1.call-start
  58.6 1.5 multiply_add_fusion.1
  60.1 1.8 reshape.57
  61.9 0.3 fusion
  62.3 0.3 fusion.2
  62.6 0.1 copy.18
  62.7 31.4 %all_to_all.38 = bf16[32,8,2048]{2,0,1:T(8,128)(2,1)} all-to-all(bf16[32,8,2048]{2,0,1:T(8,128)(2,1)S(1)} %bitcast.38), channel_id=1, replica_groups=mesh['base'=8,'inst'=16] {'base'}, dimensions={1} | all-to-all | bytes 2097152 | tf_op jit(solution)/shard_map/all_to_all | solution.py:26
  94.1 0.0 all-gather.3.cloned.1.call-update
  94.1 145.2 %all-gather.5.cloned.1.call-done = bf16[4096,1024]{1,0:T(8,128)(2,1)} async-done(((bf16[512,1024]{1,0:T(8,128)(2,1)}), bf16[4096,1024]{1,0:T(8,128)(2,1)}) %all-gather.5.cloned.1.call-update) | async-done | bytes 8388624 | tf_op jit(solution)/shard_map/all_gather | solution.py:28
  239.3 8.5 %copy.11 = bf16[8,16,32,1024]{3,2,0,1:T(8,128)(2,1)} copy(bf16[8,16,32,1024]{3,2,1,0:T(8,128)(2,1)} %bitcast.31) | data formatting | bytes 16777216 | tf_op jit(solution)/shard_map/reshape | solution.py:30
  247.8 5.1 %multiply_reduce_fusion.1 = f32[1024]{0:T(1024)S(1)} fusion(bf16[8,16,32,1024]{3,2,1,0:T(8,128)(2,1)} %bitcast.32), kind=kLoop, calls=%fused_computation.3 | loop fusion | flops 12581888 | bytes 8392704 | tf_op jit(solution)/shard_map/reduce_sum | solution.py:17
  252.9 99.2 %all-gather.3.cloned.1.call-done = bf16[4096,2048]{1,0:T(8,128)(2,1)} async-done(((bf16[256,2048]{1,0:T(8,128)(2,1)}), bf16[4096,2048]{1,0:T(8,128)(2,1)}) %all-gather.3.cloned.1.call-update) | async-done | bytes 16777232 | tf_op jit(solution)/shard_map/all_gather | solution.py:36
  352.1 7.7 %multiply_reduce_fusion = f32[2048]{0:T(1024)S(1)} fusion(bf16[4096,2048]{1,0:T(8,128)(2,1)} %all-gather.3.cloned.1.call-done), kind=kLoop, calls=%fused_computation.2 | loop fusion | flops 25163776 | bytes 16785408 | tf_op jit(solution)/shard_map/reduce_sum | solution.py:17
  359.8 3.1 copy-done
  362.9 25.2 %multiply_divide_fusion = f32[2048,1024]{1,0:T(8,128)} fusion(bf16[4096,2048]{1,0:T(8,128)(2,1)S(1)} %copy-done, bf16[4096,1024]{1,0:T(8,128)(2,1)} %bitcast.33, f32[1024]{0:T(1024)S(1)} %add_sqrt_fusion, f32[2048]{0:T(1024)S(1)} %sqrt_multiply_fusion), kind=kOutput, calls=%fused_computation.4 | convolution fusion | flops 17184063488 | bytes 33566720 | tf_op jit(solution)/shard_map/dot_general | solution.py:37
  (12 shorter events, 0.1 us)
Async XLA Ops:
  28.6 1.9 copy-start.1
  31.8 25.7 %all-to-all-start.1 = ((bf16[32,16,1024]{2,0,1:T(8,128)(2,1)}), bf16[32,16,1024]{2,0,1:T(8,128)(2,1)S(1)}, u32[]{:S(2)}, u32[]{:S(2)}) async-start(bf16[32,16,1024]{2,0,1:T(8,128)(2,1)} %bitcast.27), calls=%async_computation.1 | async-start | bytes 2097152 | tf_op jit(solution)/shard_map/all_to_all | solution.py:27
  40.2 199.1 %all-gather.5.cloned.1.call-start = ((), (), s32[]{:S(2)}) async-start(), calls=%async_computation.3 | async-start | bytes 9437184 | tf_op jit(solution)/shard_map/all_gather | solution.py:28
  57.4 1.1 copy-start.3
  58.5 293.5 %all-gather.3.cloned.1.call-start = ((), (), s32[]{:S(2)}) async-start(), calls=%async_computation.2 | async-start | bytes 17825792 | tf_op jit(solution)/shard_map/all_gather | solution.py:36
  60.1 1.9 copy-start.2
  352.1 10.8 %copy-start = (bf16[4096,2048]{1,0:T(8,128)(2,1)S(1)}, bf16[4096,2048]{1,0:T(8,128)(2,1)}, u32[]{:S(2)}) copy-start(bf16[4096,2048]{1,0:T(8,128)(2,1)} %all-gather.3.cloned.1.call-done) | copy-start | bytes 50331652
Sparse Core Ops, SparseCore 0:
  58.7 180.6 all-gather.4
  241.8 110.2 all-gather.2
where the time goes:
time: 395 us
  waiting for transfers between devices  246 us (62%)
  local copies, waits for them, and re-layouts  49.5 us (13%)
  blocking collectives  31.4 us (8%)
  matrix products  25.2 us (6%)
  other arithmetic  21.2 us (5%)
  between operations  13.5 us (3%)
  starting transfers between devices  8.53 us (2%)
    all_gather x1, waiting for transfers between devices, per_device(): gathered = lax.all_gather(column_part, 'base', axis=0, tiled=True)  145 us
    all_gather x1, waiting for transfers between devices, per_device(): base_block = lax.all_gather(base_rows, 'inst', axis=0, tiled=True)  99.2 us
    unnamed x11, local copies, waits for them, and re-layouts  36.3 us
    all_to_all x1, blocking collectives, per_device(): lax.all_to_all(base_codes, 'base', split_axis=1, concat_axis=0, tiled=True)  31.4 us
    dot_general x1, matrix products, per_device(): lax.dot_general(base_block, inst_block, (((0,), (0,)), ((), ())), preferr...  25.2 us
    reduce_sum x2, other arithmetic, squared_sums(): return jnp.sum(wide * wide, axis=0)  12.8 us
    reshape x1, local copies, waits for them, and re-layouts, per_device(): gathered.reshape(base_count, inst_count, tok_rows, -1).transpose(1, 0, 2, 3)  8.45 us
    all_to_all x1, starting transfers between devices, per_device(): lax.all_to_all(inst_codes, 'inst', split_axis=1, concat_axis=0, tiled=True)  8.45 us
  transfers between devices with their start and end apart: 3, of which 3 were waited for; matrix products, arithmetic and copies ran while one was open for 9% of the time, Pallas kernels for 0%

commit v1 on v0

v1 whole, which is shorter than its diff:
```python
import functools

import jax
import jax.numpy as jnp
from jax import lax
from jax.experimental import pallas as pl
from jax.experimental.pallas import tpu as pltpu
from jax.sharding import Mesh
from jax.sharding import PartitionSpec as P

AXES = ("z", "xl", "y", "xh", "c")
SIZES = (4, 2, 4, 2, 2)
TILE = 256


def emphasize_kernel(pre_ref, support_ref, out_ref, mask_ref):
    toks, latents = pre_ref.shape
    active = support_ref.shape[1]
    groups = latents // 128
    per_block = out_ref.shape[2] // 128
    rows = lax.broadcasted_iota(jnp.int32, (groups, active), 0)
    lanes = lax.broadcasted_iota(jnp.int32, (128, active), 0)

    def token(t, carry):
        picks = support_ref[pl.ds(t, 1), :]
        high = (rows == (picks >> 7)).astype(jnp.bfloat16)
        low = (lanes == (picks & 127)).astype(jnp.bfloat16)
        mask_ref[pl.ds(t * groups, groups), :] = lax.dot_general(
            high, low, (((1,), (1,)), ((), ())), preferred_element_type=jnp.float32
        )
        return carry

    lax.fori_loop(0, toks, token, 0, unroll=4)
    total = jnp.zeros((toks, 128), jnp.float32)
    for g in range(groups):
        wide = pre_ref[:, g * 128 : (g + 1) * 128].astype(jnp.float32)
        total = total + wide * wide
    scale = lax.rsqrt(jnp.sum(total, axis=1, keepdims=True) / latents + 1e-06)
    for g in range(groups):
        wide = pre_ref[:, g * 128 : (g + 1) * 128].astype(jnp.float32)
        on = mask_ref[pl.ds(g, toks, stride=groups), :]
        block, place = g // per_block, g % per_block * 128
        out_ref[block, :, place : place + 128] = (wide * scale * (1.0 + 3.0 * on)).astype(jnp.bfloat16)


def emphasize(pre, support, blocks):
    toks, latents = pre.shape
    return pl.pallas_call(
        emphasize_kernel,
        out_shape=jax.ShapeDtypeStruct((blocks, toks, latents // blocks), jnp.bfloat16),
        in_specs=[pl.BlockSpec(memory_space=pltpu.VMEM)] * 2,
        out_specs=pl.BlockSpec(memory_space=pltpu.VMEM),
        scratch_shapes=[pltpu.VMEM((toks * (latents // 128), 128), jnp.float32)],
        compiler_params=pltpu.CompilerParams(vmem_limit_bytes=24 << 20),
        cost_estimate=pl.CostEstimate(flops=1 << 30, bytes_accessed=4 << 20, transcendentals=0),
        name="emphasize",
    )(pre, support)


def dot_kernel(combos, base_keys, inst_keys, first, last, total, *refs):
    pos = refs[0]
    base = dict(zip(base_keys, refs[1 : 1 + len(base_keys)]))
    refs = refs[1 + len(base_keys) :]
    inst = dict(zip(inst_keys, refs[: len(inst_keys)]))
    refs = refs[len(inst_keys) :]
    if not first:
        acc_ref, bsq_ref, isq_ref, *refs = refs
    if last:
        out_ref, rhs_ref, isum_ref = refs
    else:
        out_ref, bsq_out, isq_out, rhs_ref, isum_ref = refs
    z, xl, y, xh, c = (pos[i] for i in range(5))
    order = [
        (dy, dz, dxl, dxh, dc)
        for dy, dz in combos
        for dxl in range(2)
        for dxh in range(2)
        for dc in range(2)
    ]

    @pl.when(pl.program_id(0) == 0)
    def _():
        sums = jnp.zeros((8, rhs_ref.shape[1]), jnp.float32)
        for n, (dy, dz, dxl, dxh, dc) in enumerate(order):
            place = ((y + dy) & 3) * 4 + (xh ^ dxh) * 2 + (c ^ dc)
            rows = inst[dz, dxl][place]
            rhs_ref[n * 32 : (n + 1) * 32, :] = rows
            wide = rows.astype(jnp.float32)
            sums = sums + jnp.sum((wide * wide).reshape(4, 8, -1), axis=0)
        sums = jnp.sum(sums, axis=0, keepdims=True)
        if not first:
            sums = sums + isq_ref[...]
        isum_ref[...] = sums

    blocks = []
    sums = jnp.zeros((8, TILE), jnp.float32)
    whole = base[base_keys[0]].shape[0] == 4
    for dy, dz, dxl, dxh, dc in order:
        rows = base[dy, dxh, dc][((z + dz) & 3) if whole else 0, xl ^ dxl]
        blocks.append(rows)
        wide = rows.astype(jnp.float32)
        sums = sums + jnp.sum((wide * wide).reshape(4, 8, -1), axis=0)
    sums = jnp.sum(sums, axis=0, keepdims=True)
    if not first:
        sums = sums + bsq_ref[...]
    gram = lax.dot_general(
        jnp.concatenate(blocks, axis=0),
        rhs_ref[...],
        (((0,), (0,)), ((), ())),
        preferred_element_type=jnp.float32,
    )
    if not first:
        gram = gram + acc_ref[...]
    if last:
        base_inv = 1.0 / (jnp.sqrt(sums / total + 1e-06) * jnp.sqrt(jnp.float32(total)))
        inst_inv = 1.0 / jnp.sqrt(isum_ref[...] / total + 1e-06)
        column = jnp.transpose(jnp.broadcast_to(base_inv, (8, TILE)))[:, :1]
        out_ref[...] = gram * column * inst_inv
    else:
        out_ref[...] = gram
        bsq_out[...] = sums
        isq_out[...] = isum_ref[...]


def partial_gram(pos, base, inst, combos, carry, last, total):
    base_keys = [k for k in base if k[0] in {dy for dy, _ in combos}]
    dzs = sorted({dz for _, dz in combos})
    inst_keys = [k for k in inst if k[0] in dzs]
    first = carry is None
    m = base[base_keys[0]].shape[-1]
    n = inst[inst_keys[0]].shape[-1]
    if len(dzs) == 1:
        base_spec = pl.BlockSpec((1, 2, 32, TILE), lambda i, p: ((p[0] + dzs[0]) & 3, 0, 0, i))
    else:
        base_spec = pl.BlockSpec((4, 2, 32, TILE), lambda i, p: (0, 0, 0, i))
    inst_spec = pl.BlockSpec((16, 32, n), lambda i, p: (0, 0, 0))
    gram_spec = pl.BlockSpec((TILE, n), lambda i, p: (i, 0))
    bsq_spec = pl.BlockSpec((1, TILE), lambda i, p: (0, i))
    isq_spec = pl.BlockSpec((1, n), lambda i, p: (0, 0))
    carry_specs = [gram_spec, bsq_spec, isq_spec]
    carry_shapes = [
        jax.ShapeDtypeStruct((m, n), jnp.float32),
        jax.ShapeDtypeStruct((1, m), jnp.float32),
        jax.ShapeDtypeStruct((1, n), jnp.float32),
    ]
    depth = len(combos) * 256
    return pl.pallas_call(
        functools.partial(dot_kernel, combos, base_keys, inst_keys, first, last, total),
        grid_spec=pltpu.PrefetchScalarGridSpec(
            num_scalar_prefetch=1,
            grid=(m // TILE,),
            in_specs=[base_spec] * len(base_keys)
            + [inst_spec] * len(inst_keys)
            + ([] if first else carry_specs),
            out_specs=gram_spec if last else carry_specs,
            scratch_shapes=[pltpu.VMEM((depth, n), jnp.bfloat16), pltpu.VMEM((1, n), jnp.float32)],
        ),
        out_shape=carry_shapes[0] if last else carry_shapes,
        compiler_params=pltpu.CompilerParams(vmem_limit_bytes=56 << 20),
        cost_estimate=pl.CostEstimate(
            flops=2 * depth * m * n, bytes_accessed=depth * (m + n) * 2 + 8 * m * n, transcendentals=0
        ),
        name="partial_gram",
    )(
        pos,
        *[base[k].reshape(4, 2, 32, m) for k in base_keys],
        *[inst[k] for k in inst_keys],
        *([] if first else carry),
    )


def shift(x, axis, step):
    size = lax.axis_size(axis)
    return lax.ppermute(x, axis, [(i, (i + step) % size) for i in range(size)])


def ring_gather(own, pair_axis, ring_axis):
    other = shift(own, pair_axis, 1)
    got = {(0, 0): own, (0, 1): other}
    for key, x in ((0, own), (1, other)):
        got[3, key] = shift(x, ring_axis, 1)
        got[1, key] = shift(x, ring_axis, -1)
    got[2, 0] = shift(got[3, 0], ring_axis, 1)
    got[2, 1] = shift(got[1, 1], ring_axis, -1)
    return got


def per_device(base_pre, inst_pre, base_support, inst_support):
    total = base_pre.shape[0] * 128
    pos = jnp.stack([lax.axis_index(a) for a in AXES]).astype(jnp.int32)
    base_codes = emphasize(base_pre, base_support, 8)
    base_own = lax.all_to_all(base_codes, ("z", "xl"), 0, 0, tiled=True)
    inst_codes = emphasize(inst_pre, inst_support, 16)
    inst_own = lax.all_to_all(inst_codes, ("y", "xh", "c"), 0, 0, tiled=True)
    base_got = ring_gather(base_own, "xh", "y")
    inst = ring_gather(inst_own, "xl", "z")
    base = {}
    for (dy, dxh), x in base_got.items():
        base[dy, dxh, 0] = x
        base[dy, dxh, 1] = shift(x, "c", 1)
    near = (0, 1, 3)
    carry = partial_gram(pos, base, inst, [(dy, dz) for dy in near for dz in near], None, False, total)
    carry = partial_gram(pos, base, inst, [(2, dz) for dz in near], carry, False, total)
    return partial_gram(pos, base, inst, [(dy, 2) for dy in range(4)], carry, True, total)


def solution(mesh):
    split = Mesh(mesh.devices.reshape(SIZES), AXES)
    spec = P(AXES, None)
    return jax.shard_map(
        per_device,
        mesh=split,
        in_specs=(spec,) * 4,
        out_specs=P(("z", "xl"), ("y", "xh", "c")),
        check_vma=False,
    )
```

time: 395 us -> 187 us (0.47)
  waiting for transfers between devices: 246 us -> 76.3 us
  Pallas kernels: 0 us -> 57.3 us
  local copies, waits for them, and re-layouts: 49.5 us -> 6.91 us
  starting transfers between devices: 8.53 us -> 44.5 us
  blocking collectives: 31.4 us -> 0 us
  matrix products: 25.2 us -> 0 us
  other arithmetic: 21.2 us -> 0 us
  between operations: 13.5 us -> 0.32 us
    all_gather x2 -> x0, waiting for transfers between devices: 244 us -> none  [the longest x1 145 us: per_device(): gathered = lax.all_gather(column_part, 'base', axis=0, tiled=True)]
    ppermute x0 -> x22, waiting for transfers between devices: none -> 57.7 us  [shift(): return lax.ppermute(x, axis, [(i, (i + step) % size) for i in range(size)])]
    pallas_call x0 -> x5, Pallas kernels: none -> 57.3 us  [the longest x3 48.5 us: partial_gram(): pl.pallas_call(functools.partial(dot_kernel, combos, base_keys, inst_keys...]
    all_to_all x1 -> x0, blocking collectives: 31.4 us -> none  [per_device(): lax.all_to_all(base_codes, 'base', split_axis=1, concat_axis=0, tiled=True)]
    unnamed x11 -> x36, local copies, waits for them, and re-layouts: 36.3 us -> 6.24 us
    ppermute x0 -> x22, starting transfers between devices: none -> 28.9 us  [shift(): return lax.ppermute(x, axis, [(i, (i + step) % size) for i in range(size)])]
    dot_general x1 -> x0, matrix products: 25.2 us -> none  [per_device(): lax.dot_general(base_block, inst_block, (((0,), (0,)), ((), ())), preferr...]
    all_to_all x1 -> x2, waiting for transfers between devices: 1.12 us -> 18.6 us  [the longest x1 10.4 us: per_device(): inst_own = lax.all_to_all(inst_codes, ('y', 'xh', 'c'), 0, 0, tiled=True)]
  transfers between devices with their start and end apart: 3 -> 24, of which waited for: 3 -> 8; matrix products, arithmetic and copies ran while one was open for 9% -> 0% of each run, Pallas kernels for 0% -> 21%
where the time goes in v1:
time: 187 us; the launch traced here: 185 us
  waiting for transfers between devices  76.3 us (41%)
  Pallas kernels  57.3 us (31%)
  starting transfers between devices  44.5 us (24%)
  local copies, waits for them, and re-layouts  6.91 us (4%)
    ppermute x22, waiting for transfers between devices, shift(): return lax.ppermute(x, axis, [(i, (i + step) % size) for i in range(size)])  57.7 us
    pallas_call x3, Pallas kernels, partial_gram(): pl.pallas_call(functools.partial(dot_kernel, combos, base_keys, inst_keys...  48.5 us
    ppermute x22, starting transfers between devices, shift(): return lax.ppermute(x, axis, [(i, (i + step) % size) for i in range(size)])  28.9 us
    all_to_all x1, waiting for transfers between devices, per_device(): inst_own = lax.all_to_all(inst_codes, ('y', 'xh', 'c'), 0, 0, tiled=True)  10.4 us
    all_to_all x1, starting transfers between devices, per_device(): inst_own = lax.all_to_all(inst_codes, ('y', 'xh', 'c'), 0, 0, tiled=True)  8.81 us
    pallas_call x2, Pallas kernels, emphasize(): pl.pallas_call(emphasize_kernel, out_shape=jax.ShapeDtypeStruct((blocks,...  8.74 us
    all_to_all x1, waiting for transfers between devices, per_device(): base_own = lax.all_to_all(base_codes, ('z', 'xl'), 0, 0, tiled=True)  8.17 us
    all_to_all x1, starting transfers between devices, per_device(): base_own = lax.all_to_all(base_codes, ('z', 'xl'), 0, 0, tiled=True)  6.79 us
  transfers between devices with their start and end apart: 24, of which 8 were waited for; matrix products, arithmetic and copies ran while one was open for 0% of the time, Pallas kernels for 21%

profile of v1, /device:TPU:1, one launch (start us, length us, event | category | flops | bytes accessed | tf_op | source)
XLA Modules:
  0.0 185.3 jit_solution(11740591224289698094)
XLA Ops:
  0.0 1.2 copy-done
  1.9 4.4 %emphasize.2 = bf16[8,32,2048]{2,1,0:T(8,128)(2,1)} custom-call(bf16[32,16384]{1,0:T(8,128)(2,1)S(1)} %copy-done, s32[32,128]{1,0:T(8,128)S(1)} %copy-done.2), custom_call_target="tpu_custom_call" | custom-call | flops 1073741824 | bytes 4194304 | tf_op jit(solution)/shard_map/emphasize/pallas_call | solution.py:48
  6.3 6.8 %all-to-all-start = ((bf16[8,32,2048]{2,1,0:T(8,128)(2,1)}), bf16[8,32,2048]{2,1,0:T(8,128)(2,1)S(1)}, u32[]{:S(2)}, u32[]{:S(2)}) async-start(bf16[8,32,2048]{2,1,0:T(8,128)(2,1)} %emphasize.2), calls=%async_computation | async-start | bytes 2097152 | tf_op jit(solution)/shard_map/all_to_all | solution.py:192
  13.1 1.2 copy-done.1
  15.0 4.4 %emphasize.3 = bf16[16,32,1024]{2,1,0:T(8,128)(2,1)} custom-call(bf16[32,16384]{1,0:T(8,128)(2,1)S(1)} %copy-done.1, s32[32,128]{1,0:T(8,128)S(1)} %copy-done.3), custom_call_target="tpu_custom_call" | custom-call | flops 1073741824 | bytes 4194304 | tf_op jit(solution)/shard_map/emphasize/pallas_call | solution.py:48
  19.4 8.2 %all-to-all-done = bf16[8,32,2048]{2,1,0:T(8,128)(2,1)S(1)} async-done(((bf16[8,32,2048]{2,1,0:T(8,128)(2,1)}), bf16[8,32,2048]{2,1,0:T(8,128)(2,1)S(1)}, u32[]{:S(2)}, u32[]{:S(2)}) %all-to-all-start) | async-done | bytes 1048608 | tf_op jit(solution)/shard_map/all_to_all | solution.py:192
  27.6 8.8 %all-to-all-start.1 = ((bf16[16,32,1024]{2,1,0:T(8,128)(2,1)}), bf16[16,32,1024]{2,1,0:T(8,128)(2,1)S(1)}, u32[]{:S(2)}, u32[]{:S(2)}) async-start(bf16[16,32,1024]{2,1,0:T(8,128)(2,1)} %emphasize.3), calls=%async_computation.1 | async-start | bytes 2097152 | tf_op jit(solution)/shard_map/all_to_all | solution.py:194
  36.4 2.9 %collective-permute-start.1 = (bf16[8,32,2048]{2,1,0:T(8,128)(2,1)S(1)}, bf16[8,32,2048]{2,1,0:T(8,128)(2,1)S(1)}, u32[]{:S(2)}, u32[]{:S(2)}) collective-permute-start(bf16[8,32,2048]{2,1,0:T(8,128)(2,1)S(1)} %all-to-all-done), channel_id=1, source_target_pairs={{0,2},{2,0},{1,3},{3,1},{4,6},{6,4},{5,7},{7,5},{8,10},{10,8},{9,1... | collective-permute-start | bytes 3145736 | tf_op jit(solution)/shard_map/ppermute | solution.py:174
  39.3 1.2 collective-permute-start.3
  40.5 1.5 collective-permute-start.5
  42.0 1.2 collective-permute-start
  43.2 10.4 %all-to-all-done.1.refs_13_.refs_5_ = bf16[16,32,1024]{2,1,0:T(8,128)(2,1)S(1)} async-done(((bf16[16,32,1024]{2,1,0:T(8,128)(2,1)}), bf16[16,32,1024]{2,1,0:T(8,128)(2,1)S(1)}, u32[]{:S(2)}, u32[]{:S(2)}) %all-to-all-start.1) | async-done | bytes 1048608 | tf_op jit(solution)/shard_map/all_to_all | solution.py:194
  53.6 20.3 %collective-permute-done.1 = bf16[8,32,2048]{2,1,0:T(8,128)(2,1)S(1)} collective-permute-done((bf16[8,32,2048]{2,1,0:T(8,128)(2,1)S(1)}, bf16[8,32,2048]{2,1,0:T(8,128)(2,1)S(1)}, u32[]{:S(2)}, u32[]{:S(2)}) %collective-permute-start.1) | collective-permute-done | bytes 1048608 | tf_op jit(solution)/shard_map/ppermute | solution.py:174
  74.0 2.7 %collective-permute-start.20 = (bf16[16,32,1024]{2,1,0:T(8,128)(2,1)S(1)}, bf16[16,32,1024]{2,1,0:T(8,128)(2,1)S(1)}, u32[]{:S(2)}, u32[]{:S(2)}) collective-permute-start(bf16[16,32,1024]{2,1,0:T(8,128)(2,1)S(1)} %all-to-all-done.1.refs_13_.refs_5_), channel_id=1, source_target_pairs={{0,96},{32,0},{64,32},{96,64},{1,97},{33,1},{65,33},{97,65},{2,98}... | collective-permute-start | bytes 3145736 | tf_op jit(solution)/shard_map/ppermute | solution.py:174
  76.6 2.4 %collective-permute-start.9 = (bf16[8,32,2048]{2,1,0:T(8,128)(2,1)S(1)}, bf16[8,32,2048]{2,1,0:T(8,128)(2,1)}, u32[]{:S(2)}, u32[]{:S(2)}) collective-permute-start(bf16[8,32,2048]{2,1,0:T(8,128)(2,1)S(1)} %collective-permute-done.1), channel_id=1, source_target_pairs={{0,12},{4,0},{8,4},{12,8},{1,13},{5,1},{9,5},{13,9},{2,14},{6,2},{... | collective-permute-start | bytes 3145736 | tf_op jit(solution)/shard_map/ppermute | solution.py:174
  79.1 14.9 %collective-permute-done.17.refs_14_.refs_6_ = bf16[16,32,1024]{2,1,0:T(8,128)(2,1)} collective-permute-done((bf16[16,32,1024]{2,1,0:T(8,128)(2,1)S(1)}, bf16[16,32,1024]{2,1,0:T(8,128)(2,1)}, u32[]{:S(2)}, u32[]{:S(2)}) %collective-permute-start.17) | collective-permute-done | bytes 1048608 | tf_op jit(solution)/shard_map/ppermute | solution.py:174
  94.5 4.1 %collective-permute-done.15.refs_15_.refs_7_ = bf16[16,32,1024]{2,1,0:T(8,128)(2,1)S(1)} collective-permute-done((bf16[16,32,1024]{2,1,0:T(8,128)(2,1)S(1)}, bf16[16,32,1024]{2,1,0:T(8,128)(2,1)S(1)}, u32[]{:S(2)}, u32[]{:S(2)}) %collective-permute-start.15) | collective-permute-done | bytes 1048608 | tf_op jit(solution)/shard_map/ppermute | solution.py:174
  98.6 2.2 %collective-permute-start.4 = (bf16[8,32,2048]{2,1,0:T(8,128)(2,1)}, bf16[8,32,2048]{2,1,0:T(8,128)(2,1)S(1)}, u32[]{:S(2)}, u32[]{:S(2)}) collective-permute-start(bf16[8,32,2048]{2,1,0:T(8,128)(2,1)} %collective-permute-done.3), channel_id=1, source_target_pairs={{0,1},{1,0},{2,3},{3,2},{4,5},{5,4},{6,7},{7,6},{8,9},{9,8},{10,11... | collective-permute-start | bytes 3145736 | tf_op jit(solution)/shard_map/ppermute | solution.py:174
  100.9 1.2 collective-permute-start.11
  102.0 0.8 collective-permute-done.7
  102.8 1.8 collective-permute-start.18
  104.6 1.6 collective-permute-start.13
  106.2 2.3 %collective-permute-start.10 = (bf16[8,32,2048]{2,1,0:T(8,128)(2,1)}, bf16[8,32,2048]{2,1,0:T(8,128)(2,1)}, u32[]{:S(2)}, u32[]{:S(2)}) collective-permute-start(bf16[8,32,2048]{2,1,0:T(8,128)(2,1)} %collective-permute-done.9), channel_id=1, source_target_pairs={{0,1},{1,0},{2,3},{3,2},{4,5},{5,4},{6,7},{7,6},{8,9},{9,8},{10,11... | collective-permute-start | bytes 3145736 | tf_op jit(solution)/shard_map/ppermute | solution.py:174
  108.5 17.3 %collective-permute-done.11 = bf16[8,32,2048]{2,1,0:T(8,128)(2,1)S(1)} collective-permute-done((bf16[8,32,2048]{2,1,0:T(8,128)(2,1)}, bf16[8,32,2048]{2,1,0:T(8,128)(2,1)S(1)}, u32[]{:S(2)}, u32[]{:S(2)}) %collective-permute-start.11) | collective-permute-done | bytes 1048608 | tf_op jit(solution)/shard_map/ppermute | solution.py:174
  125.8 2.5 %collective-permute-start.8 = (bf16[8,32,2048]{2,1,0:T(8,128)(2,1)}, bf16[8,32,2048]{2,1,0:T(8,128)(2,1)}, u32[]{:S(2)}, u32[]{:S(2)}) collective-permute-start(bf16[8,32,2048]{2,1,0:T(8,128)(2,1)} %collective-permute-done.7), channel_id=1, source_target_pairs={{0,1},{1,0},{2,3},{3,2},{4,5},{5,4},{6,7},{7,6},{8,9},{9,8},{10,11... | collective-permute-start | bytes 3145736 | tf_op jit(solution)/shard_map/ppermute | solution.py:174
  128.6 1.9 %collective-permute-start.14 = (bf16[8,32,2048]{2,1,0:T(8,128)(2,1)S(1)}, bf16[8,32,2048]{2,1,0:T(8,128)(2,1)}, u32[]{:S(2)}, u32[]{:S(2)}) collective-permute-start(bf16[8,32,2048]{2,1,0:T(8,128)(2,1)S(1)} %collective-permute-done.13), channel_id=1, source_target_pairs={{0,1},{1,0},{2,3},{3,2},{4,5},{5,4},{6,7},{7,6},{8,9},{9,8},{10,11... | collective-permute-start | bytes 3145736 | tf_op jit(solution)/shard_map/ppermute | solution.py:174
  131.5 2.7 %collective-permute-start.19 = (bf16[16,32,1024]{2,1,0:T(8,128)(2,1)}, bf16[16,32,1024]{2,1,0:T(8,128)(2,1)S(1)}, u32[]{:S(2)}, u32[]{:S(2)}) collective-permute-start(bf16[16,32,1024]{2,1,0:T(8,128)(2,1)} %copy-done.15), channel_id=1, source_target_pairs={{0,96},{32,0},{64,32},{96,64},{1,97},{33,1},{65,33},{97,65},{2,98}... | collective-permute-start | bytes 3145736 | tf_op jit(solution)/shard_map/ppermute | solution.py:174
  134.2 18.7 %partial_gram.3 = (f32[2048,1024]{1,0:T(8,128)}, f32[1,2048]{1,0:T(1,128)}, f32[1,1024]{1,0:T(1,128)}) custom-call(s32[5]{0:T(128)} %stack.23.refs_0_, bf16[4,2,32,2048]{3,2,1,0:T(8,128)(2,1)} %bitcast.27, bf16[4,2,32,2048]{3,2,1,0:T(8,128)(2,1)} %bitcast.6.refs_2_, bf16[4,2,32,2048]{3,2,1,0:T(8,128)(2,1)} %bitcast.29, bf16[4,2,32,2048]{3,2,1,0:T(8,128)(2,1)} %bitcast.31, ...), custom_call_target="tpu_custom_call" | custom-call | flops 9663676416 | bytes 30932992 | tf_op jit(solution)/shard_map/partial_gram/pallas_call | solution.py:147
  153.0 1.0 copy-done.6
  153.9 15.4 %partial_gram.4 = (f32[2048,1024]{1,0:T(8,128)}, f32[1,2048]{1,0:T(1,128)}, f32[1,1024]{1,0:T(1,128)}) custom-call(s32[5]{0:T(128)} %stack.23.refs_0_, bf16[4,2,32,2048]{3,2,1,0:T(8,128)(2,1)} %bitcast.21, bf16[4,2,32,2048]{3,2,1,0:T(8,128)(2,1)} %bitcast.25, bf16[4,2,32,2048]{3,2,1,0:T(8,128)(2,1)} %bitcast.23, ...), custom_call_target="tpu_custom_call" | custom-call | flops 3221225472 | bytes 21495808 | tf_op jit(solution)/shard_map/partial_gram/pallas_call | solution.py:147
  169.3 1.0 copy-done.16
  170.7 14.4 %partial_gram.5 = f32[2048,1024]{1,0:T(8,128)} custom-call(s32[5]{0:T(128)} %stack.23.refs_0_, bf16[4,2,32,2048]{3,2,1,0:T(8,128)(2,1)} %bitcast.28, bf16[4,2,32,2048]{3,2,1,0:T(8,128)(2,1)} %bitcast.6.refs_2_, bf16[4,2,32,2048]{3,2,1,0:T(8,128)(2,1)} %bitcast.30, bf16[4,2,32,2048]{3,2,1,0:T(8,128)(2,1)} %bitcast.32, ...), custom_call_target="tpu_custom_call" | custom-call | flops 4294967296 | bytes 23068672 | tf_op jit(solution)/shard_map/partial_gram/pallas_call | solution.py:147
  (58 shorter events, 3.9 us)
Async XLA Ops:
  6.3 21.3 %all-to-all-start = ((bf16[8,32,2048]{2,1,0:T(8,128)(2,1)}), bf16[8,32,2048]{2,1,0:T(8,128)(2,1)S(1)}, u32[]{:S(2)}, u32[]{:S(2)}) async-start(bf16[8,32,2048]{2,1,0:T(8,128)(2,1)} %emphasize.2), calls=%async_computation | async-start | bytes 2097152 | tf_op jit(solution)/shard_map/all_to_all | solution.py:192
  27.6 73.3 %copy-start.7 = (bf16[8,32,2048]{2,1,0:T(8,128)(2,1)}, bf16[8,32,2048]{2,1,0:T(8,128)(2,1)S(1)}, u32[]{:S(2)}) copy-start(bf16[8,32,2048]{2,1,0:T(8,128)(2,1)S(1)} %all-to-all-done) | copy-start | bytes 3145732
  27.6 26.0 %all-to-all-start.1 = ((bf16[16,32,1024]{2,1,0:T(8,128)(2,1)}), bf16[16,32,1024]{2,1,0:T(8,128)(2,1)S(1)}, u32[]{:S(2)}, u32[]{:S(2)}) async-start(bf16[16,32,1024]{2,1,0:T(8,128)(2,1)} %emphasize.3), calls=%async_computation.1 | async-start | bytes 2097152 | tf_op jit(solution)/shard_map/all_to_all | solution.py:194
  36.4 37.6 %collective-permute-start.1 = (bf16[8,32,2048]{2,1,0:T(8,128)(2,1)S(1)}, bf16[8,32,2048]{2,1,0:T(8,128)(2,1)S(1)}, u32[]{:S(2)}, u32[]{:S(2)}) collective-permute-start(bf16[8,32,2048]{2,1,0:T(8,128)(2,1)S(1)} %all-to-all-done), channel_id=1, source_target_pairs={{0,2},{2,0},{1,3},{3,1},{4,6},{6,4},{5,7},{7,5},{8,10},{10,8},{9,1... | collective-permute-start | bytes 3145736 | tf_op jit(solution)/shard_map/ppermute | solution.py:174
  39.3 34.7 %collective-permute-start.3 = (bf16[8,32,2048]{2,1,0:T(8,128)(2,1)S(1)}, bf16[8,32,2048]{2,1,0:T(8,128)(2,1)}, u32[]{:S(2)}, u32[]{:S(2)}) collective-permute-start(bf16[8,32,2048]{2,1,0:T(8,128)(2,1)S(1)} %all-to-all-done), channel_id=1, source_target_pairs={{0,4},{4,8},{8,12},{12,0},{1,5},{5,9},{9,13},{13,1},{2,6},{6,10},{... | collective-permute-start | bytes 3145736 | tf_op jit(solution)/shard_map/ppermute | solution.py:174
  40.5 36.2 %collective-permute-start.5 = (bf16[8,32,2048]{2,1,0:T(8,128)(2,1)S(1)}, bf16[8,32,2048]{2,1,0:T(8,128)(2,1)}, u32[]{:S(2)}, u32[]{:S(2)}) collective-permute-start(bf16[8,32,2048]{2,1,0:T(8,128)(2,1)S(1)} %all-to-all-done), channel_id=1, source_target_pairs={{0,12},{4,0},{8,4},{12,8},{1,13},{5,1},{9,5},{13,9},{2,14},{6,2},{... | collective-permute-start | bytes 3145736 | tf_op jit(solution)/shard_map/ppermute | solution.py:174
  42.0 37.1 %collective-permute-start = (bf16[8,32,2048]{2,1,0:T(8,128)(2,1)S(1)}, bf16[8,32,2048]{2,1,0:T(8,128)(2,1)}, u32[]{:S(2)}, u32[]{:S(2)}) collective-permute-start(bf16[8,32,2048]{2,1,0:T(8,128)(2,1)S(1)} %all-to-all-done), channel_id=1, source_target_pairs={{0,1},{1,0},{2,3},{3,2},{4,5},{5,4},{6,7},{7,6},{8,9},{9,8},{10,11... | collective-permute-start | bytes 3145736 | tf_op jit(solution)/shard_map/ppermute | solution.py:174
  53.6 51.0 %copy-start.8 = (bf16[16,32,1024]{2,1,0:T(8,128)(2,1)}, bf16[16,32,1024]{2,1,0:T(8,128)(2,1)S(1)}, u32[]{:S(2)}) copy-start(bf16[16,32,1024]{2,1,0:T(8,128)(2,1)S(1)} %all-to-all-done.1.refs_13_.refs_5_) | copy-start | bytes 3145732
  53.6 40.3 %collective-permute-start.17 = (bf16[16,32,1024]{2,1,0:T(8,128)(2,1)S(1)}, bf16[16,32,1024]{2,1,0:T(8,128)(2,1)}, u32[]{:S(2)}, u32[]{:S(2)}) collective-permute-start(bf16[16,32,1024]{2,1,0:T(8,128)(2,1)S(1)} %all-to-all-done.1.refs_13_.refs_5_), channel_id=1, source_target_pairs={{0,16},{16,0},{1,17},{17,1},{2,18},{18,2},{3,19},{19,3},{4,20},{20... | collective-permute-start | bytes 3145736 | tf_op jit(solution)/shard_map/ppermute | solution.py:174
  74.0 54.4 %copy-start.9 = (bf16[8,32,2048]{2,1,0:T(8,128)(2,1)}, bf16[8,32,2048]{2,1,0:T(8,128)(2,1)S(1)}, u32[]{:S(2)}) copy-start(bf16[8,32,2048]{2,1,0:T(8,128)(2,1)S(1)} %collective-permute-done.1) | copy-start | bytes 3145732
  74.0 24.6 %collective-permute-start.15 = (bf16[16,32,1024]{2,1,0:T(8,128)(2,1)S(1)}, bf16[16,32,1024]{2,1,0:T(8,128)(2,1)S(1)}, u32[]{:S(2)}, u32[]{:S(2)}) collective-permute-start(bf16[16,32,1024]{2,1,0:T(8,128)(2,1)S(1)} %all-to-all-done.1.refs_13_.refs_5_), channel_id=1, source_target_pairs={{0,32},{32,64},{64,96},{96,0},{1,33},{33,65},{65,97},{97,1},{2,34}... | collective-permute-start | bytes 3145736 | tf_op jit(solution)/shard_map/ppermute | solution.py:174
  74.0 26.8 %collective-permute-start.20 = (bf16[16,32,1024]{2,1,0:T(8,128)(2,1)S(1)}, bf16[16,32,1024]{2,1,0:T(8,128)(2,1)S(1)}, u32[]{:S(2)}, u32[]{:S(2)}) collective-permute-start(bf16[16,32,1024]{2,1,0:T(8,128)(2,1)S(1)} %all-to-all-done.1.refs_13_.refs_5_), channel_id=1, source_target_pairs={{0,96},{32,0},{64,32},{96,64},{1,97},{33,1},{65,33},{97,65},{2,98}... | collective-permute-start | bytes 3145736 | tf_op jit(solution)/shard_map/ppermute | solution.py:174
  76.6 24.2 %collective-permute-start.9 = (bf16[8,32,2048]{2,1,0:T(8,128)(2,1)S(1)}, bf16[8,32,2048]{2,1,0:T(8,128)(2,1)}, u32[]{:S(2)}, u32[]{:S(2)}) collective-permute-start(bf16[8,32,2048]{2,1,0:T(8,128)(2,1)S(1)} %collective-permute-done.1), channel_id=1, source_target_pairs={{0,12},{4,0},{8,4},{12,8},{1,13},{5,1},{9,5},{13,9},{2,14},{6,2},{... | collective-permute-start | bytes 3145736 | tf_op jit(solution)/shard_map/ppermute | solution.py:174
  79.0 23.8 %collective-permute-start.7 = (bf16[8,32,2048]{2,1,0:T(8,128)(2,1)S(1)}, bf16[8,32,2048]{2,1,0:T(8,128)(2,1)}, u32[]{:S(2)}, u32[]{:S(2)}) collective-permute-start(bf16[8,32,2048]{2,1,0:T(8,128)(2,1)S(1)} %collective-permute-done.1), channel_id=1, source_target_pairs={{0,4},{4,8},{8,12},{12,0},{1,5},{5,9},{9,13},{13,1},{2,6},{6,10},{... | collective-permute-start | bytes 3145736 | tf_op jit(solution)/shard_map/ppermute | solution.py:174
  93.9 10.7 %collective-permute-start.2 = (bf16[8,32,2048]{2,1,0:T(8,128)(2,1)S(1)}, bf16[8,32,2048]{2,1,0:T(8,128)(2,1)S(1)}, u32[]{:S(2)}, u32[]{:S(2)}) collective-permute-start(bf16[8,32,2048]{2,1,0:T(8,128)(2,1)S(1)} %collective-permute-done.1), channel_id=1, source_target_pairs={{0,1},{1,0},{2,3},{3,2},{4,5},{5,4},{6,7},{7,6},{8,9},{9,8},{10,11... | collective-permute-start | bytes 3145736 | tf_op jit(solution)/shard_map/ppermute | solution.py:174
  98.6 30.0 %copy-start.10 = (bf16[16,32,1024]{2,1,0:T(8,128)(2,1)}, bf16[16,32,1024]{2,1,0:T(8,128)(2,1)S(1)}, u32[]{:S(2)}) copy-start(bf16[16,32,1024]{2,1,0:T(8,128)(2,1)S(1)} %collective-permute-done.15.refs_15_.refs_7_) | copy-start | bytes 3145732
  98.6 7.6 %collective-permute-start.4 = (bf16[8,32,2048]{2,1,0:T(8,128)(2,1)}, bf16[8,32,2048]{2,1,0:T(8,128)(2,1)S(1)}, u32[]{:S(2)}, u32[]{:S(2)}) collective-permute-start(bf16[8,32,2048]{2,1,0:T(8,128)(2,1)} %collective-permute-done.3), channel_id=1, source_target_pairs={{0,1},{1,0},{2,3},{3,2},{4,5},{5,4},{6,7},{7,6},{8,9},{9,8},{10,11... | collective-permute-start | bytes 3145736 | tf_op jit(solution)/shard_map/ppermute | solution.py:174
  100.8 29.8 %copy-start.12 = (bf16[16,32,1024]{2,1,0:T(8,128)(2,1)}, bf16[16,32,1024]{2,1,0:T(8,128)(2,1)S(1)}, u32[]{:S(2)}) copy-start(bf16[16,32,1024]{2,1,0:T(8,128)(2,1)S(1)} %collective-permute-done.20.refs_16_.refs_8_) | copy-start | bytes 3145732
  100.8 5.5 %collective-permute-start.6 = (bf16[8,32,2048]{2,1,0:T(8,128)(2,1)}, bf16[8,32,2048]{2,1,0:T(8,128)(2,1)S(1)}, u32[]{:S(2)}, u32[]{:S(2)}) collective-permute-start(bf16[8,32,2048]{2,1,0:T(8,128)(2,1)} %collective-permute-done.5), channel_id=1, source_target_pairs={{0,1},{1,0},{2,3},{3,2},{4,5},{5,4},{6,7},{7,6},{8,9},{9,8},{10,11... | collective-permute-start | bytes 3145736 | tf_op jit(solution)/shard_map/ppermute | solution.py:174
  100.9 25.0 %collective-permute-start.11 = (bf16[8,32,2048]{2,1,0:T(8,128)(2,1)}, bf16[8,32,2048]{2,1,0:T(8,128)(2,1)S(1)}, u32[]{:S(2)}, u32[]{:S(2)}) collective-permute-start(bf16[8,32,2048]{2,1,0:T(8,128)(2,1)} %collective-permute-done.3), channel_id=1, source_target_pairs={{0,4},{4,8},{8,12},{12,0},{1,5},{5,9},{9,13},{13,1},{2,6},{6,10},{... | collective-permute-start | bytes 3145736 | tf_op jit(solution)/shard_map/ppermute | solution.py:174
  102.8 25.5 %collective-permute-start.18 = (bf16[16,32,1024]{2,1,0:T(8,128)(2,1)}, bf16[16,32,1024]{2,1,0:T(8,128)(2,1)S(1)}, u32[]{:S(2)}, u32[]{:S(2)}) collective-permute-start(bf16[16,32,1024]{2,1,0:T(8,128)(2,1)} %collective-permute-done.17.refs_14_.refs_6_), channel_id=1, source_target_pairs={{0,96},{32,0},{64,32},{96,64},{1,97},{33,1},{65,33},{97,65},{2,98}... | collective-permute-start | bytes 3145736 | tf_op jit(solution)/shard_map/ppermute | solution.py:174
  104.6 25.9 %copy-start.11 = (bf16[8,32,2048]{2,1,0:T(8,128)(2,1)}, bf16[8,32,2048]{2,1,0:T(8,128)(2,1)S(1)}, u32[]{:S(2)}) copy-start(bf16[8,32,2048]{2,1,0:T(8,128)(2,1)S(1)} %collective-permute-done.2) | copy-start | bytes 3145732
  104.6 24.0 %collective-permute-start.13 = (bf16[8,32,2048]{2,1,0:T(8,128)(2,1)}, bf16[8,32,2048]{2,1,0:T(8,128)(2,1)S(1)}, u32[]{:S(2)}, u32[]{:S(2)}) collective-permute-start(bf16[8,32,2048]{2,1,0:T(8,128)(2,1)} %collective-permute-done.9), channel_id=1, source_target_pairs={{0,12},{4,0},{8,4},{12,8},{1,13},{5,1},{9,5},{13,9},{2,14},{6,2},{... | collective-permute-start | bytes 3145736 | tf_op jit(solution)/shard_map/ppermute | solution.py:174
  106.2 24.3 %copy-start.13 = (bf16[8,32,2048]{2,1,0:T(8,128)(2,1)}, bf16[8,32,2048]{2,1,0:T(8,128)(2,1)S(1)}, u32[]{:S(2)}) copy-start(bf16[8,32,2048]{2,1,0:T(8,128)(2,1)S(1)} %collective-permute-done.4) | copy-start | bytes 3145732
  106.2 25.3 %collective-permute-start.21 = (bf16[16,32,1024]{2,1,0:T(8,128)(2,1)}, bf16[16,32,1024]{2,1,0:T(8,128)(2,1)}, u32[]{:S(2)}, u32[]{:S(2)}) collective-permute-start(bf16[16,32,1024]{2,1,0:T(8,128)(2,1)} %collective-permute-done.17.refs_14_.refs_6_), channel_id=1, source_target_pairs={{0,32},{32,64},{64,96},{96,0},{1,33},{33,65},{65,97},{97,1},{2,34}... | collective-permute-start | bytes 3145736 | tf_op jit(solution)/shard_map/ppermute | solution.py:174
  106.2 25.3 %collective-permute-start.10 = (bf16[8,32,2048]{2,1,0:T(8,128)(2,1)}, bf16[8,32,2048]{2,1,0:T(8,128)(2,1)}, u32[]{:S(2)}, u32[]{:S(2)}) collective-permute-start(bf16[8,32,2048]{2,1,0:T(8,128)(2,1)} %collective-permute-done.9), channel_id=1, source_target_pairs={{0,1},{1,0},{2,3},{3,2},{4,5},{5,4},{6,7},{7,6},{8,9},{9,8},{10,11... | collective-permute-start | bytes 3145736 | tf_op jit(solution)/shard_map/ppermute | solution.py:174
  125.8 27.1 %copy-start.4 = (bf16[8,32,2048]{2,1,0:T(8,128)(2,1)}, bf16[8,32,2048]{2,1,0:T(8,128)(2,1)S(1)}, u32[]{:S(2)}) copy-start(bf16[8,32,2048]{2,1,0:T(8,128)(2,1)S(1)} %collective-permute-done.11) | copy-start | bytes 3145732
  125.8 8.4 %collective-permute-start.8 = (bf16[8,32,2048]{2,1,0:T(8,128)(2,1)}, bf16[8,32,2048]{2,1,0:T(8,128)(2,1)}, u32[]{:S(2)}, u32[]{:S(2)}) collective-permute-start(bf16[8,32,2048]{2,1,0:T(8,128)(2,1)} %collective-permute-done.7), channel_id=1, source_target_pairs={{0,1},{1,0},{2,3},{3,2},{4,5},{5,4},{6,7},{7,6},{8,9},{9,8},{10,11... | collective-permute-start | bytes 3145736 | tf_op jit(solution)/shard_map/ppermute | solution.py:174
  128.3 24.6 %collective-permute-start.12 = (bf16[8,32,2048]{2,1,0:T(8,128)(2,1)S(1)}, bf16[8,32,2048]{2,1,0:T(8,128)(2,1)S(1)}, u32[]{:S(2)}, u32[]{:S(2)}) collective-permute-start(bf16[8,32,2048]{2,1,0:T(8,128)(2,1)S(1)} %collective-permute-done.11), channel_id=1, source_target_pairs={{0,1},{1,0},{2,3},{3,2},{4,5},{5,4},{6,7},{7,6},{8,9},{9,8},{10,11... | collective-permute-start | bytes 3145736 | tf_op jit(solution)/shard_map/ppermute | solution.py:174
  128.6 24.3 %collective-permute-start.14 = (bf16[8,32,2048]{2,1,0:T(8,128)(2,1)S(1)}, bf16[8,32,2048]{2,1,0:T(8,128)(2,1)}, u32[]{:S(2)}, u32[]{:S(2)}) collective-permute-start(bf16[8,32,2048]{2,1,0:T(8,128)(2,1)S(1)} %collective-permute-done.13), channel_id=1, source_target_pairs={{0,1},{1,0},{2,3},{3,2},{4,5},{5,4},{6,7},{7,6},{8,9},{9,8},{10,11... | collective-permute-start | bytes 3145736 | tf_op jit(solution)/shard_map/ppermute | solution.py:174
  131.5 37.8 %collective-permute-start.16 = (bf16[16,32,1024]{2,1,0:T(8,128)(2,1)}, bf16[16,32,1024]{2,1,0:T(8,128)(2,1)S(1)}, u32[]{:S(2)}, u32[]{:S(2)}) collective-permute-start(bf16[16,32,1024]{2,1,0:T(8,128)(2,1)} %copy-done.10), channel_id=1, source_target_pairs={{0,32},{32,64},{64,96},{96,0},{1,33},{33,65},{65,97},{97,1},{2,34}... | collective-permute-start | bytes 3145736 | tf_op jit(solution)/shard_map/ppermute | solution.py:174
  131.5 37.8 %collective-permute-start.19 = (bf16[16,32,1024]{2,1,0:T(8,128)(2,1)}, bf16[16,32,1024]{2,1,0:T(8,128)(2,1)S(1)}, u32[]{:S(2)}, u32[]{:S(2)}) collective-permute-start(bf16[16,32,1024]{2,1,0:T(8,128)(2,1)} %copy-done.15), channel_id=1, source_target_pairs={{0,96},{32,0},{64,32},{96,64},{1,97},{33,1},{65,33},{97,65},{2,98}... | collective-permute-start | bytes 3145736 | tf_op jit(solution)/shard_map/ppermute | solution.py:174
  (10 other events, 58.0 us)

commit v2 on v1

v2 whole, which is shorter than its diff:
```python
import functools

import jax
import jax.numpy as jnp
from jax import lax
from jax.experimental import pallas as pl
from jax.experimental.pallas import tpu as pltpu
from jax.sharding import PartitionSpec as P

AXES = ("base", "inst")
SIZES = (4, 2, 4, 2, 2)
TILE = 512
ROWS = 32


def device(z, xl, y, xh, c):
    return (((z % 4) * 2 + xl) * 4 + y % 4) * 4 + xh * 2 + c


def places():
    return [(z, xl, y, xh, c) for z in range(4) for xl in range(2) for y in range(4) for xh in range(2) for c in range(2)]


def emphasize_kernel(side, pos_ref, base_ref, inst_ref, base_sup_ref, inst_sup_ref, out_ref, pre_ref, support_ref, mask_ref, sem):
    for own, pre, sup in ((side, base_ref, base_sup_ref), (1 - side, inst_ref, inst_sup_ref)):

        @pl.when(pos_ref[4] == own)
        def _(pre=pre, sup=sup):
            pltpu.make_async_copy(sup, support_ref, sem.at[0]).start()
            pltpu.make_async_copy(pre, pre_ref, sem.at[1]).start()

    pltpu.make_async_copy(base_sup_ref, support_ref, sem.at[0]).wait()
    toks, latents = pre_ref.shape
    active = support_ref.shape[1]
    groups = latents // 128
    per_block = groups // 8
    rows = lax.broadcasted_iota(jnp.int32, (groups, active), 0)
    lanes = lax.broadcasted_iota(jnp.int32, (128, active), 0)

    def token(t, carry):
        picks = support_ref[pl.ds(t, 1), :]
        high = (rows == (picks >> 7)).astype(jnp.bfloat16)
        low = (lanes == (picks & 127)).astype(jnp.bfloat16)
        mask_ref[pl.ds(t * groups, groups), :] = lax.dot_general(
            high, low, (((1,), (1,)), ((), ())), preferred_element_type=jnp.float32
        )
        return carry

    lax.fori_loop(0, toks, token, 0, unroll=8)
    pltpu.make_async_copy(base_ref, pre_ref, sem.at[1]).wait()
    total = jnp.zeros((toks, 128), jnp.float32)
    for g in range(groups):
        wide = pre_ref[:, g * 128 : (g + 1) * 128].astype(jnp.float32)
        total = total + wide * wide
    scale = lax.rsqrt(jnp.sum(total, axis=1, keepdims=True) / latents + 1e-06)
    for g in range(groups):
        wide = pre_ref[:, g * 128 : (g + 1) * 128].astype(jnp.float32)
        on = mask_ref[pl.ds(g, toks, stride=groups), :]
        block, place = g // per_block, g % per_block * 128
        out_ref[block, :, place : place + 128] = (wide * scale * (1.0 + 3.0 * on)).astype(jnp.bfloat16)


def emphasize(side, pos, base_pre, inst_pre, base_support, inst_support):
    toks, latents = base_pre.shape
    return pl.pallas_call(
        functools.partial(emphasize_kernel, side),
        out_shape=jax.ShapeDtypeStruct((8, toks, latents // 8), jnp.bfloat16),
        in_specs=[pl.BlockSpec(memory_space=pltpu.SMEM)] + [pl.BlockSpec(memory_space=pl.ANY)] * 4,
        out_specs=pl.BlockSpec(memory_space=pltpu.VMEM),
        scratch_shapes=[
            pltpu.VMEM(base_pre.shape, base_pre.dtype),
            pltpu.VMEM(base_support.shape, base_support.dtype),
            pltpu.VMEM((toks * (latents // 128), 128), jnp.float32),
            pltpu.SemaphoreType.DMA((2,)),
        ],
        compiler_params=pltpu.CompilerParams(vmem_limit_bytes=56 << 20),
        cost_estimate=pl.CostEstimate(flops=1 << 30, bytes_accessed=4 << 20, transcendentals=0),
        name="emphasize",
    )(pos, base_pre, inst_pre, base_support, inst_support)


def dot_kernel(pairs, base_keys, inst_keys, first, last, total, *refs):
    pos, refs = refs[0], list(refs[1:])
    base = {key: refs.pop(0) for key in base_keys}
    inst = {key: refs.pop(0) for key in inst_keys}
    if not first:
        acc_ref, bsq_ref, isq_ref = refs[:3]
        del refs[:3]
    if last:
        out_ref, rhs_ref, isum_ref, sem = refs
    else:
        out_ref, bsq_out, isq_out, rhs_ref, isum_ref, sem = refs
    z, xl, y, xh, c = (pos[i] for i in range(5))
    n = rhs_ref.shape[1]

    @pl.when(pl.program_id(0) == 0)
    def _():
        columns = pl.ds(pl.multiple_of(c * n, n), n)
        copies = []
        for row, ((dy, dxh, _), key) in enumerate(pairs):
            source = inst[key].at[((y + dy) & 3) * 2 + (xh ^ dxh), :, columns]
            copies.append(pltpu.make_async_copy(source, rhs_ref.at[pl.ds(row * ROWS, ROWS)], sem))
        for copy in copies:
            copy.start()
        for copy in copies:
            copy.wait()
        sums = jnp.zeros((8, n), jnp.float32)
        for row in range(len(pairs)):
            wide = rhs_ref[row * ROWS : (row + 1) * ROWS, :].astype(jnp.float32)
            sums = sums + jnp.sum((wide * wide).reshape(4, 8, -1), axis=0)
        sums = jnp.sum(sums, axis=0, keepdims=True)
        isum_ref[...] = sums if first else sums + isq_ref[...]

    blocks = []
    sums = jnp.zeros((8, TILE), jnp.float32)
    for key, (dz, dxl, _) in pairs:
        rows = base[key][((z + dz) & 3) * 2 + (xl ^ dxl)]
        blocks.append(rows)
        wide = rows.astype(jnp.float32)
        sums = sums + jnp.sum((wide * wide).reshape(4, 8, -1), axis=0)
    sums = jnp.sum(sums, axis=0, keepdims=True)
    if not first:
        sums = sums + bsq_ref[...]
    gram = lax.dot_general(
        jnp.concatenate(blocks, axis=0),
        rhs_ref[...],
        (((0,), (0,)), ((), ())),
        preferred_element_type=jnp.float32,
    )
    if not first:
        gram = gram + acc_ref[...]
    if last:
        base_inv = 1.0 / (jnp.sqrt(sums / total + 1e-06) * jnp.sqrt(jnp.float32(total)))
        inst_inv = 1.0 / jnp.sqrt(isum_ref[...] / total + 1e-06)
        column = jnp.transpose(jnp.broadcast_to(base_inv, (8, TILE)))[:, :1]
        out_ref[...] = gram * column * inst_inv
    else:
        out_ref[...] = gram
        bsq_out[...] = sums
        isq_out[...] = isum_ref[...]


def partial_gram(pos, own, mate, pairs, carry, last, total):
    first = carry is None
    base_keys = sorted({key for key, _ in pairs})
    inst_keys = sorted({key for _, key in pairs})
    m = own[base_keys[0]].shape[-1]
    n = m // 2
    carry_specs = [
        pl.BlockSpec((TILE, n), lambda i, p: (i, 0)),
        pl.BlockSpec((1, TILE), lambda i, p: (0, i)),
        pl.BlockSpec((1, n), lambda i, p: (0, 0)),
    ]
    carry_shapes = [
        jax.ShapeDtypeStruct((m, n), jnp.float32),
        jax.ShapeDtypeStruct((1, m), jnp.float32),
        jax.ShapeDtypeStruct((1, n), jnp.float32),
    ]
    depth = len(pairs) * ROWS
    call = pl.pallas_call(
        functools.partial(dot_kernel, pairs, base_keys, inst_keys, first, last, total),
        grid_spec=pltpu.PrefetchScalarGridSpec(
            num_scalar_prefetch=1,
            grid=(m // TILE,),
            in_specs=[pl.BlockSpec((8, ROWS, TILE), lambda i, p: (0, 0, i))] * len(base_keys)
            + [pl.BlockSpec(memory_space=pl.ANY)] * len(inst_keys)
            + ([] if first else carry_specs),
            out_specs=carry_specs[0] if last else carry_specs,
            scratch_shapes=[
                pltpu.VMEM((depth, n), jnp.bfloat16),
                pltpu.VMEM((1, n), jnp.float32),
                pltpu.SemaphoreType.DMA,
            ],
        ),
        out_shape=carry_shapes[0] if last else carry_shapes,
        compiler_params=pltpu.CompilerParams(vmem_limit_bytes=56 << 20),
        cost_estimate=pl.CostEstimate(
            flops=2 * depth * m * n, bytes_accessed=depth * (m + n) * 2 + 8 * m * n, transcendentals=0
        ),
        name="partial_gram",
    )

    def run(pos, base, inst, carry):
        return call(pos, *[base[k] for k in base_keys], *[inst[k] for k in inst_keys], *(carry or ()))

    keys = set(base_keys + inst_keys)
    own, mate = ({key: pieces[key] for key in keys} for pieces in (own, mate))
    return lax.cond(
        pos[4] == 0,
        lambda pos, own, mate, carry: run(pos, own, mate, carry),
        lambda pos, own, mate, carry: run(pos, mate, own, carry),
        pos,
        own,
        mate,
        carry,
    )


def send(x, target):
    return lax.ppermute(x, AXES, [(device(*p), device(*target(*p))) for p in places()])


def ring(x, way):
    return send(x, lambda z, xl, y, xh, c: (z + way * c, xl, y + way * (1 - c), xh, c))


def across(x):
    return send(x, lambda z, xl, y, xh, c: (z, xl ^ c, y, xh ^ (1 - c), c))


def mated(x):
    return send(x, lambda z, xl, y, xh, c: (z, xl, y, xh, 1 - c))


def per_device(base_pre, inst_pre, base_support, inst_support):
    total = base_pre.shape[0] * 128
    tie = lax.optimization_barrier

    def after(x, *others):
        return tie((x, others))[0]

    row, column = lax.axis_index("base"), lax.axis_index("inst")
    pos = jnp.stack([row // 2, row % 2, column // 4, column // 2 % 2, column % 2]).astype(jnp.int32)
    codes = [base_pre, inst_pre, base_support, inst_support]
    groups = [
        [device(z, xl, y, xh, 0) for z in range(4) for xl in range(2)] for y in range(4) for xh in range(2)
    ] + [[device(z, xl, y, xh, 1) for y in range(4) for xh in range(2)] for z in range(4) for xl in range(2)]

    def spread(x):
        return lax.all_to_all(x, AXES, 0, 0, axis_index_groups=groups, tiled=True)

    staying = emphasize(0, pos, *codes)
    leaving = emphasize(1, after(pos, staying), *codes)
    a = spread(staying)
    leaving, a = tie((leaving, a))
    arriving = mated(leaving)
    a3, a1 = ring(a, 1), ring(a, -1)
    xa = across(a)
    b = spread(arriving)
    a2 = ring(a3, 1)
    b3, b1 = ring(b, 1), ring(b, -1)
    b2 = ring(b1, -1)
    xa = after(xa, b3, b1, a2)
    xb = across(after(b, xa))
    xa3, xa1 = ring(xa, 1), ring(xa, -1)
    xb = after(xb, xa3, xa1, b2)
    xb3, xb1 = ring(xb, 1), ring(xb, -1)
    xa2 = ring(xa3, 1)
    own = {(0, 0, 0): a, (1, 0, 0): a1, (2, 0, 0): a2, (3, 0, 0): a3}
    own |= {(0, 0, 1): b, (1, 0, 1): b1, (2, 0, 1): b2, (3, 0, 1): b3}
    mate = {key: mated(x) for key, x in own.items()}
    steps = [(k, dx) for k in range(4) for dx in range(2)]
    blocks = [(p + (t,), q + (1 - t,)) for t in range(2) for q in steps for p in steps]
    early = [(p, q) for p, q in blocks if p[1] == 0 and q[1] == 0]
    late = [(p, q) for p, q in blocks if (p, q) not in early]
    carry = partial_gram(after(pos, xb), own, mate, early, None, False, total)
    xb3, xb1, carry = tie((xb3, xb1, carry))
    xb2 = ring(xb1, -1)
    more = {(0, 1, 0): xa, (1, 1, 0): xa1, (2, 1, 0): xa2, (3, 1, 0): xa3}
    more |= {(0, 1, 1): xb, (1, 1, 1): xb1, (2, 1, 1): xb2, (3, 1, 1): xb3}
    own |= more
    mate |= {key: mated(x) for key, x in more.items()}
    return partial_gram(pos, own, mate, late, carry, True, total)


def solution(mesh):
    spec = P(AXES, None)
    return jax.shard_map(
        per_device, mesh=mesh, in_specs=(spec,) * 4, out_specs=P("base", "inst"), check_vma=False
    )
```

time: 187 us -> 168 us (0.90)
  Pallas kernels: 57.3 us -> 45.3 us
  starting transfers between devices: 44.5 us -> 36.9 us
  waiting for transfers between devices: 76.3 us -> 83.1 us
  local copies, waits for them, and re-layouts: 6.91 us -> 0.67 us
    pallas_call x5 -> x4, Pallas kernels: 57.3 us -> 45.3 us  [the longest x2 35 us: run(): call(pos, *[base[k] for k in base_keys], *[inst[k] for k in inst_keys], *...]
    ppermute x22 -> x31, waiting for transfers between devices: 57.7 us -> 64.7 us  [send(): lax.ppermute(x, AXES, [(device(*p), device(*target(*p))) for p in places()])]
    unnamed x36 -> x4, local copies, waits for them, and re-layouts: 6.24 us -> 0.01 us
    ppermute x22 -> x31, starting transfers between devices: 28.9 us -> 23.6 us  [send(): lax.ppermute(x, AXES, [(device(*p), device(*target(*p))) for p in places()])]
    all_to_all x2, starting transfers between devices: 15.6 us -> 13.4 us  [spread(): return lax.all_to_all(x, AXES, 0, 0, axis_index_groups=groups, tiled=True)]
  transfers between devices with their start and end apart: 24 -> 33, of which waited for: 8 -> 15; matrix products, arithmetic and copies ran while one was open for 0% -> 0% of each run, Pallas kernels for 21% -> 10%
where the time goes in v2:
time: 168 us; the launch traced here: 167 us
  waiting for transfers between devices  83.1 us (49%)
  Pallas kernels  45.3 us (27%)
  starting transfers between devices  36.9 us (22%)
    ppermute x31, waiting for transfers between devices, send(): lax.ppermute(x, AXES, [(device(*p), device(*target(*p))) for p in places()])  64.7 us
    pallas_call x2, Pallas kernels, run(): call(pos, *[base[k] for k in base_keys], *[inst[k] for k in inst_keys], *...  35 us
    ppermute x31, starting transfers between devices, send(): lax.ppermute(x, AXES, [(device(*p), device(*target(*p))) for p in places()])  23.6 us
    all_to_all x2, waiting for transfers between devices, spread(): return lax.all_to_all(x, AXES, 0, 0, axis_index_groups=groups, tiled=True)  18.4 us
    all_to_all x2, starting transfers between devices, spread(): return lax.all_to_all(x, AXES, 0, 0, axis_index_groups=groups, tiled=True)  13.4 us
    pallas_call x2, Pallas kernels, emphasize(): pl.pallas_call(functools.partial(emphasize_kernel, side), out_shape=jax.S...  10.3 us
  transfers between devices with their start and end apart: 33, of which 15 were waited for; matrix products, arithmetic and copies ran while one was open for 0% of the time, Pallas kernels for 10%

profile of v2, /device:TPU:1, one launch (start us, length us, event | category | flops | bytes accessed | tf_op | source)
XLA Modules:
  0.0 167.2 jit_solution(2453755982988014533)
XLA Ops:
  0.1 5.2 %emphasize.2 = bf16[8,32,2048]{2,1,0:T(8,128)(2,1)} custom-call(s32[5]{0:T(128)S(1)} %stack.23.pos_ref, bf16[32,16384]{1,0:T(8,128)(2,1)} %base_ref.3, bf16[32,16384]{1,0:T(8,128)(2,1)} %inst_ref.3, s32[32,128]{1,0:T(8,128)} %base_sup_ref.3, s32[32,128]{1,0:T(8,128)} %inst_sup_ref.3), custom_call_target="tpu_custom_call" | custom-call | flops 1073741824 | bytes 4194304 | tf_op jit(solution)/shard_map/emphasize/pallas_call | solution.py:65
  5.3 7.5 %all-to-all-start = ((bf16[8,32,2048]{2,1,0:T(8,128)(2,1)}), bf16[8,32,2048]{2,1,0:T(8,128)(2,1)S(1)}, u32[]{:S(2)}, u32[]{:S(2)}) async-start(bf16[8,32,2048]{2,1,0:T(8,128)(2,1)} %emphasize.2), calls=%async_computation | async-start | bytes 2097152 | tf_op jit(solution)/shard_map/all_to_all | solution.py:230
  12.8 5.2 %emphasize.3 = bf16[8,32,2048]{2,1,0:T(8,128)(2,1)} custom-call(s32[5]{0:T(128)S(1)} %stack.23.pos_ref, bf16[32,16384]{1,0:T(8,128)(2,1)} %base_ref.3, bf16[32,16384]{1,0:T(8,128)(2,1)} %inst_ref.3, s32[32,128]{1,0:T(8,128)} %base_sup_ref.3, s32[32,128]{1,0:T(8,128)} %inst_sup_ref.3), custom_call_target="tpu_custom_call" | custom-call | flops 1073741824 | bytes 4194304 | tf_op jit(solution)/shard_map/emphasize/pallas_call | solution.py:65
  17.9 12.0 %all-to-all-done = bf16[8,32,2048]{2,1,0:T(8,128)(2,1)S(1)} async-done(((bf16[8,32,2048]{2,1,0:T(8,128)(2,1)}), bf16[8,32,2048]{2,1,0:T(8,128)(2,1)S(1)}, u32[]{:S(2)}, u32[]{:S(2)}) %all-to-all-start) | async-done | bytes 1048608 | tf_op jit(solution)/shard_map/all_to_all | solution.py:230
  29.9 1.6 collective-permute-start.6
  31.6 1.4 collective-permute-done.1
  32.9 5.9 %all-to-all-start.1 = ((bf16[8,32,2048]{2,1,0:T(8,128)(2,1)}), bf16[8,32,2048]{2,1,0:T(8,128)(2,1)S(1)}, u32[]{:S(2)}, u32[]{:S(2)}) async-start(bf16[8,32,2048]{2,1,0:T(8,128)(2,1)} %collective-permute-done.1), calls=%async_computation.1 | async-start | bytes 2097152 | tf_op jit(solution)/shard_map/all_to_all | solution.py:230
  38.8 1.3 collective-permute-start.14
  40.7 9.3 %collective-permute-done.6 = bf16[8,32,2048]{2,1,0:T(8,128)(2,1)S(1)} collective-permute-done((bf16[8,32,2048]{2,1,0:T(8,128)(2,1)S(1)}, bf16[8,32,2048]{2,1,0:T(8,128)(2,1)S(1)}, u32[]{:S(2)}, u32[]{:S(2)}) %collective-permute-start.6) | collective-permute-done | bytes 1048608 | tf_op jit(solution)/shard_map/ppermute | solution.py:200
  50.0 6.4 %all-to-all-done.1 = bf16[8,32,2048]{2,1,0:T(8,128)(2,1)S(1)} async-done(((bf16[8,32,2048]{2,1,0:T(8,128)(2,1)}), bf16[8,32,2048]{2,1,0:T(8,128)(2,1)S(1)}, u32[]{:S(2)}, u32[]{:S(2)}) %all-to-all-start.1) | async-done | bytes 1048608 | tf_op jit(solution)/shard_map/all_to_all | solution.py:230
  56.4 1.0 collective-permute-start.5
  57.8 0.7 collective-permute-done.14
  59.0 14.1 %collective-permute-done.3 = bf16[8,32,2048]{2,1,0:T(8,128)(2,1)} collective-permute-done((bf16[8,32,2048]{2,1,0:T(8,128)(2,1)S(1)}, bf16[8,32,2048]{2,1,0:T(8,128)(2,1)}, u32[]{:S(2)}, u32[]{:S(2)}) %collective-permute-start.3) | collective-permute-done | bytes 1048608 | tf_op jit(solution)/shard_map/ppermute | solution.py:200
  73.6 2.6 %collective-permute-start.12 = (bf16[8,32,2048]{2,1,0:T(8,128)(2,1)S(1)}, bf16[8,32,2048]{2,1,0:T(8,128)(2,1)}, u32[]{:S(2)}, u32[]{:S(2)}) collective-permute-start(bf16[8,32,2048]{2,1,0:T(8,128)(2,1)S(1)} %collective-permute-done.5), channel_id=1, source_target_pairs={{0,12},{1,97},{2,14},{3,99},{4,0},{5,101},{6,2},{7,103},{8,4},{9,1... | collective-permute-start | bytes 3145736 | tf_op jit(solution)/shard_map/ppermute | solution.py:200
  76.2 1.0 collective-permute-done.4
  77.3 1.7 %collective-permute-start.11 = (bf16[8,32,2048]{2,1,0:T(8,128)(2,1)}, bf16[8,32,2048]{2,1,0:T(8,128)(2,1)}, u32[]{:S(2)}, u32[]{:S(2)}) collective-permute-start(bf16[8,32,2048]{2,1,0:T(8,128)(2,1)} %collective-permute-done.3), channel_id=1, source_target_pairs={{0,12},{1,97},{2,14},{3,99},{4,0},{5,101},{6,2},{7,103},{8,4},{9,1... | collective-permute-start | bytes 3145736 | tf_op jit(solution)/shard_map/ppermute | solution.py:200
  79.6 2.7 %collective-permute-start.2 = (bf16[8,32,2048]{2,1,0:T(8,128)(2,1)S(1)}, bf16[8,32,2048]{2,1,0:T(8,128)(2,1)}, u32[]{:S(2)}, u32[]{:S(2)}) collective-permute-start(bf16[8,32,2048]{2,1,0:T(8,128)(2,1)S(1)} %all-to-all-done.1), channel_id=1, source_target_pairs={{0,1},{1,0},{2,3},{3,2},{4,5},{5,4},{6,7},{7,6},{8,9},{9,8},{10,11... | collective-permute-start | bytes 3145736 | tf_op jit(solution)/shard_map/ppermute | solution.py:200
  82.3 6.0 %collective-permute-done.12 = bf16[8,32,2048]{2,1,0:T(8,128)(2,1)} collective-permute-done((bf16[8,32,2048]{2,1,0:T(8,128)(2,1)S(1)}, bf16[8,32,2048]{2,1,0:T(8,128)(2,1)}, u32[]{:S(2)}, u32[]{:S(2)}) %collective-permute-start.12) | collective-permute-done | bytes 1048608 | tf_op jit(solution)/shard_map/ppermute | solution.py:200
  88.6 13.2 %collective-permute-done.9 = bf16[8,32,2048]{2,1,0:T(8,128)(2,1)} collective-permute-done((bf16[8,32,2048]{2,1,0:T(8,128)(2,1)S(1)}, bf16[8,32,2048]{2,1,0:T(8,128)(2,1)}, u32[]{:S(2)}, u32[]{:S(2)}) %collective-permute-start.9) | collective-permute-done | bytes 1048608 | tf_op jit(solution)/shard_map/ppermute | solution.py:200
  101.8 2.3 %collective-permute-start.16 = (bf16[8,32,2048]{2,1,0:T(8,128)(2,1)S(1)}, bf16[8,32,2048]{2,1,0:T(8,128)(2,1)}, u32[]{:S(2)}, u32[]{:S(2)}) collective-permute-start(bf16[8,32,2048]{2,1,0:T(8,128)(2,1)S(1)} %collective-permute-done.5), channel_id=1, source_target_pairs={{0,1},{1,0},{2,3},{3,2},{4,5},{5,4},{6,7},{7,6},{8,9},{9,8},{10,11... | collective-permute-start | bytes 3145736 | tf_op jit(solution)/shard_map/ppermute | solution.py:200
  104.8 1.3 collective-permute-start.18
  107.3 0.6 collective-permute-done.16
  108.6 1.1 collective-permute-done.21
  110.1 11.5 %conditional.2 = ((f32[2048,1024]{1,0:T(8,128)}, f32[1,2048]{1,0:T(1,128)S(1)}, f32[1,1024]{1,0:T(1,128)S(1)})) conditional(s32[]{:T(128)} %bitcast.5, (s32[5]{0:T(128)S(1)}, bf16[8,32,2048]{2,1,0:T(8,128)(2,1)}, bf16[8,32,2048]{2,1,0:T(8,128)(2,1)}, bf16[8,32,2048]{2,1,0:T(8,128)(2,1)}, bf16[8,32,2048]{2,1,0:T(8,128)(2,1)}, ...), branch_computations={%region_0.1_spmd, %region_1.2_spmd} | conditional | flops 4294967296 | bytes 23068680 | solution.py:188
  110.1 11.5 %partial_gram.4 = (f32[2048,1024]{1,0:T(8,128)}, f32[1,2048]{1,0:T(1,128)S(1)}, f32[1,1024]{1,0:T(1,128)S(1)}) custom-call(s32[5]{0:T(128)S(1)} %get-tuple-element.220.refs_0_, bf16[8,32,2048]{2,1,0:T(8,128)(2,1)} %get-tuple-element.221.refs_1_, bf16[8,32,2048]{2,1,0:T(8,128)(2,1)} %get-tuple-element.222.refs_2_, ...), custom_call_target="tpu_custom_call" | custom-call | flops 4294967296 | bytes 23068672 | tf_op jit(solution)/shard_map/cond/branch_0_fun/partial_gram/pallas_call | solution.py:184
  121.7 2.7 %collective-permute-start.27 = (bf16[8,32,2048]{2,1,0:T(8,128)(2,1)}, bf16[8,32,2048]{2,1,0:T(8,128)(2,1)}, u32[]{:S(2)}, u32[]{:S(2)}) collective-permute-start(bf16[8,32,2048]{2,1,0:T(8,128)(2,1)} %collective-permute-done.19), channel_id=1, source_target_pairs={{0,12},{1,97},{2,14},{3,99},{4,0},{5,101},{6,2},{7,103},{8,4},{9,1... | collective-permute-start | bytes 3145736 | tf_op jit(solution)/shard_map/ppermute | solution.py:200
  124.9 12.3 %collective-permute-done.25 = bf16[8,32,2048]{2,1,0:T(8,128)(2,1)} collective-permute-done((bf16[8,32,2048]{2,1,0:T(8,128)(2,1)}, bf16[8,32,2048]{2,1,0:T(8,128)(2,1)}, u32[]{:S(2)}, u32[]{:S(2)}) %collective-permute-start.25) | collective-permute-done | bytes 1048608 | tf_op jit(solution)/shard_map/ppermute | solution.py:200
  138.2 2.1 %collective-permute-done.26 = bf16[8,32,2048]{2,1,0:T(8,128)(2,1)} collective-permute-done((bf16[8,32,2048]{2,1,0:T(8,128)(2,1)}, bf16[8,32,2048]{2,1,0:T(8,128)(2,1)}, u32[]{:S(2)}, u32[]{:S(2)}) %collective-permute-start.26) | collective-permute-done | bytes 1048608 | tf_op jit(solution)/shard_map/ppermute | solution.py:200
  140.3 1.5 collective-permute-done.30
  141.8 1.5 collective-permute-done.28
  143.3 23.7 %conditional.3 = (f32[2048,1024]{1,0:T(8,128)}) conditional(s32[]{:T(128)} %convert_element_type.9, (s32[5]{0:T(128)S(1)}, bf16[8,32,2048]{2,1,0:T(8,128)(2,1)}, bf16[8,32,2048]{2,1,0:T(8,128)(2,1)}, bf16[8,32,2048]{2,1,0:T(8,128)(2,1)}, bf16[8,32,2048]{2,1,0:T(8,128)(2,1)}, /*index=5*/bf16[8,32,2048]{2,1,0:T(8,128)(2,1)}, ...), branch_computations={%region_2.3_spmd, %region_3.4_spmd} | conditional | flops 12884901888 | bytes 35651592 | solution.py:188
  143.3 23.5 %partial_gram.6 = f32[2048,1024]{1,0:T(8,128)} custom-call(s32[5]{0:T(128)S(1)} %get-tuple-element.254.refs_0_, bf16[8,32,2048]{2,1,0:T(8,128)(2,1)} %get-tuple-element.255.refs_1_, bf16[8,32,2048]{2,1,0:T(8,128)(2,1)} %get-tuple-element.256.refs_2_, bf16[8,32,2048]{2,1,0:T(8,128)(2,1)} %get-tuple-element.257.refs_3_, ...), custom_call_target="tpu_custom_call" | custom-call | flops 12884901888 | bytes 35651584 | tf_op jit(solution)/shard_map/cond/branch_0_fun/partial_gram/pallas_call | solution.py:184
  (46 shorter events, 7.2 us)
Async XLA Ops:
  5.3 24.7 %all-to-all-start = ((bf16[8,32,2048]{2,1,0:T(8,128)(2,1)}), bf16[8,32,2048]{2,1,0:T(8,128)(2,1)S(1)}, u32[]{:S(2)}, u32[]{:S(2)}) async-start(bf16[8,32,2048]{2,1,0:T(8,128)(2,1)} %emphasize.2), calls=%async_computation | async-start | bytes 2097152 | tf_op jit(solution)/shard_map/all_to_all | solution.py:230
  29.9 20.0 %collective-permute-start.6 = (bf16[8,32,2048]{2,1,0:T(8,128)(2,1)S(1)}, bf16[8,32,2048]{2,1,0:T(8,128)(2,1)S(1)}, u32[]{:S(2)}, u32[]{:S(2)}) collective-permute-start(bf16[8,32,2048]{2,1,0:T(8,128)(2,1)S(1)} %all-to-all-done), channel_id=1, source_target_pairs={{0,4},{1,33},{2,6},{3,35},{4,8},{5,37},{6,10},{7,39},{8,12},{9,41}... | collective-permute-start | bytes 3145736 | tf_op jit(solution)/shard_map/ppermute | solution.py:200
  32.9 23.4 %all-to-all-start.1 = ((bf16[8,32,2048]{2,1,0:T(8,128)(2,1)}), bf16[8,32,2048]{2,1,0:T(8,128)(2,1)S(1)}, u32[]{:S(2)}, u32[]{:S(2)}) async-start(bf16[8,32,2048]{2,1,0:T(8,128)(2,1)} %collective-permute-done.1), calls=%async_computation.1 | async-start | bytes 2097152 | tf_op jit(solution)/shard_map/all_to_all | solution.py:230
  38.8 19.7 %collective-permute-start.14 = (bf16[8,32,2048]{2,1,0:T(8,128)(2,1)S(1)}, bf16[8,32,2048]{2,1,0:T(8,128)(2,1)}, u32[]{:S(2)}, u32[]{:S(2)}) collective-permute-start(bf16[8,32,2048]{2,1,0:T(8,128)(2,1)S(1)} %all-to-all-done), channel_id=1, source_target_pairs={{0,12},{1,97},{2,14},{3,99},{4,0},{5,101},{6,2},{7,103},{8,4},{9,1... | collective-permute-start | bytes 3145736 | tf_op jit(solution)/shard_map/ppermute | solution.py:200
  40.1 33.0 %collective-permute-start.3 = (bf16[8,32,2048]{2,1,0:T(8,128)(2,1)S(1)}, bf16[8,32,2048]{2,1,0:T(8,128)(2,1)}, u32[]{:S(2)}, u32[]{:S(2)}) collective-permute-start(bf16[8,32,2048]{2,1,0:T(8,128)(2,1)S(1)} %all-to-all-done), channel_id=1, source_target_pairs={{0,2},{1,17},{2,0},{3,19},{4,6},{5,21},{6,4},{7,23},{8,10},{9,25},... | collective-permute-start | bytes 3145736 | tf_op jit(solution)/shard_map/ppermute | solution.py:200
  50.0 23.3 %collective-permute-start.7 = (bf16[8,32,2048]{2,1,0:T(8,128)(2,1)S(1)}, bf16[8,32,2048]{2,1,0:T(8,128)(2,1)}, u32[]{:S(2)}, u32[]{:S(2)}) collective-permute-start(bf16[8,32,2048]{2,1,0:T(8,128)(2,1)S(1)} %collective-permute-done.6), channel_id=1, source_target_pairs={{0,4},{1,33},{2,6},{3,35},{4,8},{5,37},{6,10},{7,39},{8,12},{9,41}... | collective-permute-start | bytes 3145736 | tf_op jit(solution)/shard_map/ppermute | solution.py:200
  56.4 17.2 %collective-permute-start.5 = (bf16[8,32,2048]{2,1,0:T(8,128)(2,1)S(1)}, bf16[8,32,2048]{2,1,0:T(8,128)(2,1)S(1)}, u32[]{:S(2)}, u32[]{:S(2)}) collective-permute-start(bf16[8,32,2048]{2,1,0:T(8,128)(2,1)S(1)} %all-to-all-done.1), channel_id=1, source_target_pairs={{0,12},{1,97},{2,14},{3,99},{4,0},{5,101},{6,2},{7,103},{8,4},{9,1... | collective-permute-start | bytes 3145736 | tf_op jit(solution)/shard_map/ppermute | solution.py:200
  57.4 19.8 %collective-permute-start.4 = (bf16[8,32,2048]{2,1,0:T(8,128)(2,1)S(1)}, bf16[8,32,2048]{2,1,0:T(8,128)(2,1)}, u32[]{:S(2)}, u32[]{:S(2)}) collective-permute-start(bf16[8,32,2048]{2,1,0:T(8,128)(2,1)S(1)} %all-to-all-done.1), channel_id=1, source_target_pairs={{0,4},{1,33},{2,6},{3,35},{4,8},{5,37},{6,10},{7,39},{8,12},{9,41}... | collective-permute-start | bytes 3145736 | tf_op jit(solution)/shard_map/ppermute | solution.py:200
  58.5 18.8 %collective-permute-start = (bf16[8,32,2048]{2,1,0:T(8,128)(2,1)S(1)}, bf16[8,32,2048]{2,1,0:T(8,128)(2,1)}, u32[]{:S(2)}, u32[]{:S(2)}) collective-permute-start(bf16[8,32,2048]{2,1,0:T(8,128)(2,1)S(1)} %all-to-all-done), channel_id=1, source_target_pairs={{0,1},{1,0},{2,3},{3,2},{4,5},{5,4},{6,7},{7,6},{8,9},{9,8},{10,11... | collective-permute-start | bytes 3145736 | tf_op jit(solution)/shard_map/ppermute | solution.py:200
  73.0 5.9 %collective-permute-start.15 = (bf16[8,32,2048]{2,1,0:T(8,128)(2,1)}, bf16[8,32,2048]{2,1,0:T(8,128)(2,1)}, u32[]{:S(2)}, u32[]{:S(2)}) collective-permute-start(bf16[8,32,2048]{2,1,0:T(8,128)(2,1)} %collective-permute-done.14), channel_id=1, source_target_pairs={{0,1},{1,0},{2,3},{3,2},{4,5},{5,4},{6,7},{7,6},{8,9},{9,8},{10,11... | collective-permute-start | bytes 3145736 | tf_op jit(solution)/shard_map/ppermute | solution.py:200
  73.2 6.4 %collective-permute-start.22 = (bf16[8,32,2048]{2,1,0:T(8,128)(2,1)S(1)}, bf16[8,32,2048]{2,1,0:T(8,128)(2,1)}, u32[]{:S(2)}, u32[]{:S(2)}) collective-permute-start(bf16[8,32,2048]{2,1,0:T(8,128)(2,1)S(1)} %collective-permute-done.6), channel_id=1, source_target_pairs={{0,1},{1,0},{2,3},{3,2},{4,5},{5,4},{6,7},{7,6},{8,9},{9,8},{10,11... | collective-permute-start | bytes 3145736 | tf_op jit(solution)/shard_map/ppermute | solution.py:200
  73.6 14.7 %collective-permute-start.12 = (bf16[8,32,2048]{2,1,0:T(8,128)(2,1)S(1)}, bf16[8,32,2048]{2,1,0:T(8,128)(2,1)}, u32[]{:S(2)}, u32[]{:S(2)}) collective-permute-start(bf16[8,32,2048]{2,1,0:T(8,128)(2,1)S(1)} %collective-permute-done.5), channel_id=1, source_target_pairs={{0,12},{1,97},{2,14},{3,99},{4,0},{5,101},{6,2},{7,103},{8,4},{9,1... | collective-permute-start | bytes 3145736 | tf_op jit(solution)/shard_map/ppermute | solution.py:200
  77.1 24.7 %collective-permute-start.9 = (bf16[8,32,2048]{2,1,0:T(8,128)(2,1)S(1)}, bf16[8,32,2048]{2,1,0:T(8,128)(2,1)}, u32[]{:S(2)}, u32[]{:S(2)}) collective-permute-start(bf16[8,32,2048]{2,1,0:T(8,128)(2,1)S(1)} %all-to-all-done.1), channel_id=1, source_target_pairs={{0,2},{1,17},{2,0},{3,19},{4,6},{5,21},{6,4},{7,23},{8,10},{9,25},... | collective-permute-start | bytes 3145736 | tf_op jit(solution)/shard_map/ppermute | solution.py:200
  77.3 26.8 %collective-permute-start.11 = (bf16[8,32,2048]{2,1,0:T(8,128)(2,1)}, bf16[8,32,2048]{2,1,0:T(8,128)(2,1)}, u32[]{:S(2)}, u32[]{:S(2)}) collective-permute-start(bf16[8,32,2048]{2,1,0:T(8,128)(2,1)} %collective-permute-done.3), channel_id=1, source_target_pairs={{0,12},{1,97},{2,14},{3,99},{4,0},{5,101},{6,2},{7,103},{8,4},{9,1... | collective-permute-start | bytes 3145736 | tf_op jit(solution)/shard_map/ppermute | solution.py:200
  79.0 25.1 %collective-permute-start.10 = (bf16[8,32,2048]{2,1,0:T(8,128)(2,1)}, bf16[8,32,2048]{2,1,0:T(8,128)(2,1)S(1)}, u32[]{:S(2)}, u32[]{:S(2)}) collective-permute-start(bf16[8,32,2048]{2,1,0:T(8,128)(2,1)} %collective-permute-done.3), channel_id=1, source_target_pairs={{0,4},{1,33},{2,6},{3,35},{4,8},{5,37},{6,10},{7,39},{8,12},{9,41}... | collective-permute-start | bytes 3145736 | tf_op jit(solution)/shard_map/ppermute | solution.py:200
  79.6 25.0 %collective-permute-start.2 = (bf16[8,32,2048]{2,1,0:T(8,128)(2,1)S(1)}, bf16[8,32,2048]{2,1,0:T(8,128)(2,1)}, u32[]{:S(2)}, u32[]{:S(2)}) collective-permute-start(bf16[8,32,2048]{2,1,0:T(8,128)(2,1)S(1)} %all-to-all-done.1), channel_id=1, source_target_pairs={{0,1},{1,0},{2,3},{3,2},{4,5},{5,4},{6,7},{7,6},{8,9},{9,8},{10,11... | collective-permute-start | bytes 3145736 | tf_op jit(solution)/shard_map/ppermute | solution.py:200
  88.2 16.6 %collective-permute-start.20 = (bf16[8,32,2048]{2,1,0:T(8,128)(2,1)}, bf16[8,32,2048]{2,1,0:T(8,128)(2,1)}, u32[]{:S(2)}, u32[]{:S(2)}) collective-permute-start(bf16[8,32,2048]{2,1,0:T(8,128)(2,1)} %collective-permute-done.7), channel_id=1, source_target_pairs={{0,1},{1,0},{2,3},{3,2},{4,5},{5,4},{6,7},{7,6},{8,9},{9,8},{10,11... | collective-permute-start | bytes 3145736 | tf_op jit(solution)/shard_map/ppermute | solution.py:200
  101.8 6.1 %collective-permute-start.16 = (bf16[8,32,2048]{2,1,0:T(8,128)(2,1)S(1)}, bf16[8,32,2048]{2,1,0:T(8,128)(2,1)}, u32[]{:S(2)}, u32[]{:S(2)}) collective-permute-start(bf16[8,32,2048]{2,1,0:T(8,128)(2,1)S(1)} %collective-permute-done.5), channel_id=1, source_target_pairs={{0,1},{1,0},{2,3},{3,2},{4,5},{5,4},{6,7},{7,6},{8,9},{9,8},{10,11... | collective-permute-start | bytes 3145736 | tf_op jit(solution)/shard_map/ppermute | solution.py:200
  104.1 4.2 %collective-permute-start.23 = (bf16[8,32,2048]{2,1,0:T(8,128)(2,1)}, bf16[8,32,2048]{2,1,0:T(8,128)(2,1)}, u32[]{:S(2)}, u32[]{:S(2)}) collective-permute-start(bf16[8,32,2048]{2,1,0:T(8,128)(2,1)} %collective-permute-done.4), channel_id=1, source_target_pairs={{0,1},{1,0},{2,3},{3,2},{4,5},{5,4},{6,7},{7,6},{8,9},{9,8},{10,11... | collective-permute-start | bytes 3145736 | tf_op jit(solution)/shard_map/ppermute | solution.py:200
  104.1 5.6 %collective-permute-start.21 = (bf16[8,32,2048]{2,1,0:T(8,128)(2,1)}, bf16[8,32,2048]{2,1,0:T(8,128)(2,1)}, u32[]{:S(2)}, u32[]{:S(2)}) collective-permute-start(bf16[8,32,2048]{2,1,0:T(8,128)(2,1)} %collective-permute-done.12), channel_id=1, source_target_pairs={{0,1},{1,0},{2,3},{3,2},{4,5},{5,4},{6,7},{7,6},{8,9},{9,8},{10,11... | collective-permute-start | bytes 3145736 | tf_op jit(solution)/shard_map/ppermute | solution.py:200
  104.6 17.0 %collective-permute-start.19 = (bf16[8,32,2048]{2,1,0:T(8,128)(2,1)}, bf16[8,32,2048]{2,1,0:T(8,128)(2,1)}, u32[]{:S(2)}, u32[]{:S(2)}) collective-permute-start(bf16[8,32,2048]{2,1,0:T(8,128)(2,1)} %collective-permute-done.9), channel_id=1, source_target_pairs={{0,12},{1,97},{2,14},{3,99},{4,0},{5,101},{6,2},{7,103},{8,4},{9,1... | collective-permute-start | bytes 3145736 | tf_op jit(solution)/shard_map/ppermute | solution.py:200
  104.8 16.9 %collective-permute-start.18 = (bf16[8,32,2048]{2,1,0:T(8,128)(2,1)}, bf16[8,32,2048]{2,1,0:T(8,128)(2,1)}, u32[]{:S(2)}, u32[]{:S(2)}) collective-permute-start(bf16[8,32,2048]{2,1,0:T(8,128)(2,1)} %collective-permute-done.9), channel_id=1, source_target_pairs={{0,4},{1,33},{2,6},{3,35},{4,8},{5,37},{6,10},{7,39},{8,12},{9,41}... | collective-permute-start | bytes 3145736 | tf_op jit(solution)/shard_map/ppermute | solution.py:200
  107.9 16.5 %collective-permute-start.8 = (bf16[8,32,2048]{2,1,0:T(8,128)(2,1)}, bf16[8,32,2048]{2,1,0:T(8,128)(2,1)}, u32[]{:S(2)}, u32[]{:S(2)}) collective-permute-start(bf16[8,32,2048]{2,1,0:T(8,128)(2,1)} %collective-permute-done.3), channel_id=1, source_target_pairs={{0,1},{1,0},{2,3},{3,2},{4,5},{5,4},{6,7},{7,6},{8,9},{9,8},{10,11... | collective-permute-start | bytes 3145736 | tf_op jit(solution)/shard_map/ppermute | solution.py:200
  108.3 29.3 %collective-permute-start.13 = (bf16[8,32,2048]{2,1,0:T(8,128)(2,1)}, bf16[8,32,2048]{2,1,0:T(8,128)(2,1)}, u32[]{:S(2)}, u32[]{:S(2)}) collective-permute-start(bf16[8,32,2048]{2,1,0:T(8,128)(2,1)} %collective-permute-done.9), channel_id=1, source_target_pairs={{0,1},{1,0},{2,3},{3,2},{4,5},{5,4},{6,7},{7,6},{8,9},{9,8},{10,11... | collective-permute-start | bytes 3145736 | tf_op jit(solution)/shard_map/ppermute | solution.py:200
  109.7 14.9 %collective-permute-start.17 = (bf16[8,32,2048]{2,1,0:T(8,128)(2,1)}, bf16[8,32,2048]{2,1,0:T(8,128)(2,1)}, u32[]{:S(2)}, u32[]{:S(2)}) collective-permute-start(bf16[8,32,2048]{2,1,0:T(8,128)(2,1)} %collective-permute-done.11), channel_id=1, source_target_pairs={{0,1},{1,0},{2,3},{3,2},{4,5},{5,4},{6,7},{7,6},{8,9},{9,8},{10,11... | collective-permute-start | bytes 3145736 | tf_op jit(solution)/shard_map/ppermute | solution.py:200
  121.6 15.5 %collective-permute-start.25 = (bf16[8,32,2048]{2,1,0:T(8,128)(2,1)}, bf16[8,32,2048]{2,1,0:T(8,128)(2,1)}, u32[]{:S(2)}, u32[]{:S(2)}) collective-permute-start(bf16[8,32,2048]{2,1,0:T(8,128)(2,1)} %copy-done.1), channel_id=1, source_target_pairs={{0,4},{1,33},{2,6},{3,35},{4,8},{5,37},{6,10},{7,39},{8,12},{9,41}... | collective-permute-start | bytes 3145736 | tf_op jit(solution)/shard_map/ppermute | solution.py:200
  121.7 16.0 %collective-permute-start.27 = (bf16[8,32,2048]{2,1,0:T(8,128)(2,1)}, bf16[8,32,2048]{2,1,0:T(8,128)(2,1)}, u32[]{:S(2)}, u32[]{:S(2)}) collective-permute-start(bf16[8,32,2048]{2,1,0:T(8,128)(2,1)} %collective-permute-done.19), channel_id=1, source_target_pairs={{0,12},{1,97},{2,14},{3,99},{4,0},{5,101},{6,2},{7,103},{8,4},{9,1... | collective-permute-start | bytes 3145736 | tf_op jit(solution)/shard_map/ppermute | solution.py:200
  124.4 13.8 %collective-permute-start.29 = (bf16[8,32,2048]{2,1,0:T(8,128)(2,1)}, bf16[8,32,2048]{2,1,0:T(8,128)(2,1)}, u32[]{:S(2)}, u32[]{:S(2)}) collective-permute-start(bf16[8,32,2048]{2,1,0:T(8,128)(2,1)} %copy-done.1), channel_id=1, source_target_pairs={{0,1},{1,0},{2,3},{3,2},{4,5},{5,4},{6,7},{7,6},{8,9},{9,8},{10,11... | collective-permute-start | bytes 3145736 | tf_op jit(solution)/shard_map/ppermute | solution.py:200
  124.6 17.2 %collective-permute-start.24 = (bf16[8,32,2048]{2,1,0:T(8,128)(2,1)}, bf16[8,32,2048]{2,1,0:T(8,128)(2,1)}, u32[]{:S(2)}, u32[]{:S(2)}) collective-permute-start(bf16[8,32,2048]{2,1,0:T(8,128)(2,1)} %collective-permute-done.19), channel_id=1, source_target_pairs={{0,1},{1,0},{2,3},{3,2},{4,5},{5,4},{6,7},{7,6},{8,9},{9,8},{10,11... | collective-permute-start | bytes 3145736 | tf_op jit(solution)/shard_map/ppermute | solution.py:200
  137.2 3.1 %collective-permute-start.26 = (bf16[8,32,2048]{2,1,0:T(8,128)(2,1)}, bf16[8,32,2048]{2,1,0:T(8,128)(2,1)}, u32[]{:S(2)}, u32[]{:S(2)}) collective-permute-start(bf16[8,32,2048]{2,1,0:T(8,128)(2,1)} %collective-permute-done.25), channel_id=1, source_target_pairs={{0,1},{1,0},{2,3},{3,2},{4,5},{5,4},{6,7},{7,6},{8,9},{9,8},{10,11... | collective-permute-start | bytes 3145736 | tf_op jit(solution)/shard_map/ppermute | solution.py:200
  137.6 4.1 %collective-permute-start.30 = (bf16[8,32,2048]{2,1,0:T(8,128)(2,1)}, bf16[8,32,2048]{2,1,0:T(8,128)(2,1)}, u32[]{:S(2)}, u32[]{:S(2)}) collective-permute-start(bf16[8,32,2048]{2,1,0:T(8,128)(2,1)} %collective-permute-done.18), channel_id=1, source_target_pairs={{0,1},{1,0},{2,3},{3,2},{4,5},{5,4},{6,7},{7,6},{8,9},{9,8},{10,11... | collective-permute-start | bytes 3145736 | tf_op jit(solution)/shard_map/ppermute | solution.py:200
  137.7 5.6 %collective-permute-start.28 = (bf16[8,32,2048]{2,1,0:T(8,128)(2,1)}, bf16[8,32,2048]{2,1,0:T(8,128)(2,1)}, u32[]{:S(2)}, u32[]{:S(2)}) collective-permute-start(bf16[8,32,2048]{2,1,0:T(8,128)(2,1)} %collective-permute-done.27), channel_id=1, source_target_pairs={{0,1},{1,0},{2,3},{3,2},{4,5},{5,4},{6,7},{7,6},{8,9},{9,8},{10,11... | collective-permute-start | bytes 3145736 | tf_op jit(solution)/shard_map/ppermute | solution.py:200
  (3 other events, 45.5 us)

commit v3 on v2

--- a/solution.py
+++ b/solution.py
@@ -252,12 +252,18 @@
     steps = [(k, dx) for k in range(4) for dx in range(2)]
     blocks = [(p + (t,), q + (1 - t,)) for t in range(2) for q in steps for p in steps]
     early = [(p, q) for p, q in blocks if p[1] == 0 and q[1] == 0]
-    late = [(p, q) for p, q in blocks if (p, q) not in early]
+    ready = [(p, q) for p, q in blocks if {p[1:], q[1:]} in ({(0, 0), (0, 1)}, {(1, 0), (0, 1)}) and (2, 1) not in (p[:2], q[:2])]
+    middle = [pair for pair in ready if pair not in early]
+    late = [pair for pair in blocks if pair not in ready]
     carry = partial_gram(after(pos, xb), own, mate, early, None, False, total)
     xb3, xb1, carry = tie((xb3, xb1, carry))
     xb2 = ring(xb1, -1)
-    more = {(0, 1, 0): xa, (1, 1, 0): xa1, (2, 1, 0): xa2, (3, 1, 0): xa3}
-    more |= {(0, 1, 1): xb, (1, 1, 1): xb1, (2, 1, 1): xb2, (3, 1, 1): xb3}
+    more = {(0, 1, 0): xa, (1, 1, 0): xa1, (3, 1, 0): xa3}
+    own |= more
+    mate |= {key: mated(x) for key, x in more.items()}
+    carry = partial_gram(pos, own, mate, middle, carry, False, total)
+    xb2, carry = tie((xb2, carry))
+    more = {(2, 1, 0): xa2, (0, 1, 1): xb, (1, 1, 1): xb1, (2, 1, 1): xb2, (3, 1, 1): xb3}
     own |= more
     mate |= {key: mated(x) for key, x in more.items()}
     return partial_gram(pos, own, mate, late, carry, True, total)

time: 168 us -> 163 us (0.970)
  waiting for transfers between devices: 83.1 us -> 69.3 us
  Pallas kernels: 45.3 us -> 54.9 us
    ppermute x31, waiting for transfers between devices: 64.7 us -> 51.2 us  [send(): lax.ppermute(x, AXES, [(device(*p), device(*target(*p))) for p in places()])]
    pallas_call x2 -> x3, Pallas kernels: 35 us -> 44.5 us  [run(): call(pos, *[base[k] for k in base_keys], *[inst[k] for k in inst_keys], *...]
  transfers between devices with their start and end apart: 33 -> 33, of which waited for: 15 -> 12; matrix products, arithmetic and copies ran while one was open for 0% -> 0% of each run, Pallas kernels for 10% -> 18%
where the time goes in v3:
time: 163 us
  waiting for transfers between devices  69.3 us (43%)
  Pallas kernels  54.9 us (34%)
  starting transfers between devices  36.8 us (23%)
    ppermute x31, waiting for transfers between devices, send(): lax.ppermute(x, AXES, [(device(*p), device(*target(*p))) for p in places()])  51.2 us
    pallas_call x3, Pallas kernels, run(): call(pos, *[base[k] for k in base_keys], *[inst[k] for k in inst_keys], *...  44.5 us
    ppermute x31, starting transfers between devices, send(): lax.ppermute(x, AXES, [(device(*p), device(*target(*p))) for p in places()])  23.4 us
    all_to_all x2, waiting for transfers between devices, spread(): return lax.all_to_all(x, AXES, 0, 0, axis_index_groups=groups, tiled=True)  18.1 us
    all_to_all x2, starting transfers between devices, spread(): return lax.all_to_all(x, AXES, 0, 0, axis_index_groups=groups, tiled=True)  13.4 us
    pallas_call x2, Pallas kernels, emphasize(): pl.pallas_call(functools.partial(emphasize_kernel, side), out_shape=jax.S...  10.3 us
  transfers between devices with their start and end apart: 33, of which 12 were waited for; matrix products, arithmetic and copies ran while one was open for 0% of the time, Pallas kernels for 18%

profile of v3, /device:TPU:1, one launch (start us, length us, event | category | flops | bytes accessed | tf_op | source)
XLA Modules:
  0.0 162.8 jit_solution(2864516501860964270)
XLA Ops:
  0.1 5.2 %emphasize.2 = bf16[8,32,2048]{2,1,0:T(8,128)(2,1)} custom-call(s32[5]{0:T(128)S(1)} %stack.23.pos_ref, bf16[32,16384]{1,0:T(8,128)(2,1)} %base_ref.3, bf16[32,16384]{1,0:T(8,128)(2,1)} %inst_ref.3, s32[32,128]{1,0:T(8,128)} %base_sup_ref.3, s32[32,128]{1,0:T(8,128)} %inst_sup_ref.3), custom_call_target="tpu_custom_call" | custom-call | flops 1073741824 | bytes 4194304 | tf_op jit(solution)/shard_map/emphasize/pallas_call | solution.py:65
  5.3 7.5 %all-to-all-start = ((bf16[8,32,2048]{2,1,0:T(8,128)(2,1)}), bf16[8,32,2048]{2,1,0:T(8,128)(2,1)}, u32[]{:S(2)}, u32[]{:S(2)}) async-start(bf16[8,32,2048]{2,1,0:T(8,128)(2,1)} %emphasize.2), calls=%async_computation | async-start | bytes 2097152 | tf_op jit(solution)/shard_map/all_to_all | solution.py:230
  12.8 5.2 %emphasize.3 = bf16[8,32,2048]{2,1,0:T(8,128)(2,1)} custom-call(s32[5]{0:T(128)S(1)} %stack.23.pos_ref, bf16[32,16384]{1,0:T(8,128)(2,1)} %base_ref.3, bf16[32,16384]{1,0:T(8,128)(2,1)} %inst_ref.3, s32[32,128]{1,0:T(8,128)} %base_sup_ref.3, s32[32,128]{1,0:T(8,128)} %inst_sup_ref.3), custom_call_target="tpu_custom_call" | custom-call | flops 1073741824 | bytes 4194304 | tf_op jit(solution)/shard_map/emphasize/pallas_call | solution.py:65
  17.9 12.1 %all-to-all-done = bf16[8,32,2048]{2,1,0:T(8,128)(2,1)} async-done(((bf16[8,32,2048]{2,1,0:T(8,128)(2,1)}), bf16[8,32,2048]{2,1,0:T(8,128)(2,1)}, u32[]{:S(2)}, u32[]{:S(2)}) %all-to-all-start) | async-done | bytes 1048608 | tf_op jit(solution)/shard_map/all_to_all | solution.py:230
  30.1 1.6 %collective-permute-start.6 = (bf16[8,32,2048]{2,1,0:T(8,128)(2,1)}, bf16[8,32,2048]{2,1,0:T(8,128)(2,1)}, u32[]{:S(2)}, u32[]{:S(2)}) collective-permute-start(bf16[8,32,2048]{2,1,0:T(8,128)(2,1)} %all-to-all-done), channel_id=1, source_target_pairs={{0,4},{1,33},{2,6},{3,35},{4,8},{5,37},{6,10},{7,39},{8,12},{9,41}... | collective-permute-start | bytes 3145736 | tf_op jit(solution)/shard_map/ppermute | solution.py:200
  31.7 1.4 collective-permute-done.1
  33.1 5.9 %all-to-all-start.1 = ((bf16[8,32,2048]{2,1,0:T(8,128)(2,1)}), bf16[8,32,2048]{2,1,0:T(8,128)(2,1)S(1)}, u32[]{:S(2)}, u32[]{:S(2)}) async-start(bf16[8,32,2048]{2,1,0:T(8,128)(2,1)} %collective-permute-done.1), calls=%async_computation.1 | async-start | bytes 2097152 | tf_op jit(solution)/shard_map/all_to_all | solution.py:230
  38.9 1.3 collective-permute-start.14
  40.8 9.7 %collective-permute-done.6 = bf16[8,32,2048]{2,1,0:T(8,128)(2,1)} collective-permute-done((bf16[8,32,2048]{2,1,0:T(8,128)(2,1)}, bf16[8,32,2048]{2,1,0:T(8,128)(2,1)}, u32[]{:S(2)}, u32[]{:S(2)}) %collective-permute-start.6) | collective-permute-done | bytes 1048608 | tf_op jit(solution)/shard_map/ppermute | solution.py:200
  50.5 5.9 %all-to-all-done.1 = bf16[8,32,2048]{2,1,0:T(8,128)(2,1)S(1)} async-done(((bf16[8,32,2048]{2,1,0:T(8,128)(2,1)}), bf16[8,32,2048]{2,1,0:T(8,128)(2,1)S(1)}, u32[]{:S(2)}, u32[]{:S(2)}) %all-to-all-start.1) | async-done | bytes 1048608 | tf_op jit(solution)/shard_map/all_to_all | solution.py:230
  56.5 1.0 collective-permute-start.5
  57.9 0.9 collective-permute-done.14
  59.2 14.1 %collective-permute-done.3 = bf16[8,32,2048]{2,1,0:T(8,128)(2,1)} collective-permute-done((bf16[8,32,2048]{2,1,0:T(8,128)(2,1)}, bf16[8,32,2048]{2,1,0:T(8,128)(2,1)}, u32[]{:S(2)}, u32[]{:S(2)}) %collective-permute-start.3) | collective-permute-done | bytes 1048608 | tf_op jit(solution)/shard_map/ppermute | solution.py:200
  73.8 2.5 %collective-permute-start.12 = (bf16[8,32,2048]{2,1,0:T(8,128)(2,1)S(1)}, bf16[8,32,2048]{2,1,0:T(8,128)(2,1)S(1)}, u32[]{:S(2)}, u32[]{:S(2)}) collective-permute-start(bf16[8,32,2048]{2,1,0:T(8,128)(2,1)S(1)} %collective-permute-done.5), channel_id=1, source_target_pairs={{0,12},{1,97},{2,14},{3,99},{4,0},{5,101},{6,2},{7,103},{8,4},{9,1... | collective-permute-start | bytes 3145736 | tf_op jit(solution)/shard_map/ppermute | solution.py:200
  76.2 1.2 collective-permute-done.4
  77.9 1.5 collective-permute-start.11
  79.4 3.4 %collective-permute-start.2 = (bf16[8,32,2048]{2,1,0:T(8,128)(2,1)S(1)}, bf16[8,32,2048]{2,1,0:T(8,128)(2,1)}, u32[]{:S(2)}, u32[]{:S(2)}) collective-permute-start(bf16[8,32,2048]{2,1,0:T(8,128)(2,1)S(1)} %all-to-all-done.1), channel_id=1, source_target_pairs={{0,1},{1,0},{2,3},{3,2},{4,5},{5,4},{6,7},{7,6},{8,9},{9,8},{10,11... | collective-permute-start | bytes 3145736 | tf_op jit(solution)/shard_map/ppermute | solution.py:200
  82.8 5.5 %collective-permute-done.12 = bf16[8,32,2048]{2,1,0:T(8,128)(2,1)S(1)} collective-permute-done((bf16[8,32,2048]{2,1,0:T(8,128)(2,1)S(1)}, bf16[8,32,2048]{2,1,0:T(8,128)(2,1)S(1)}, u32[]{:S(2)}, u32[]{:S(2)}) %collective-permute-start.12) | collective-permute-done | bytes 1048608 | tf_op jit(solution)/shard_map/ppermute | solution.py:200
  88.8 13.7 %collective-permute-done.9 = bf16[8,32,2048]{2,1,0:T(8,128)(2,1)} collective-permute-done((bf16[8,32,2048]{2,1,0:T(8,128)(2,1)S(1)}, bf16[8,32,2048]{2,1,0:T(8,128)(2,1)}, u32[]{:S(2)}, u32[]{:S(2)}) %collective-permute-start.9) | collective-permute-done | bytes 1048608 | tf_op jit(solution)/shard_map/ppermute | solution.py:200
  102.4 1.8 %collective-permute-start.16 = (bf16[8,32,2048]{2,1,0:T(8,128)(2,1)S(1)}, bf16[8,32,2048]{2,1,0:T(8,128)(2,1)}, u32[]{:S(2)}, u32[]{:S(2)}) collective-permute-start(bf16[8,32,2048]{2,1,0:T(8,128)(2,1)S(1)} %collective-permute-done.5), channel_id=1, source_target_pairs={{0,1},{1,0},{2,3},{3,2},{4,5},{5,4},{6,7},{7,6},{8,9},{9,8},{10,11... | collective-permute-start | bytes 3145736 | tf_op jit(solution)/shard_map/ppermute | solution.py:200
  104.9 1.3 collective-permute-start.18
  107.4 1.0 collective-permute-start.8
  108.5 1.1 collective-permute-done.21
  110.0 11.6 %conditional.3 = ((f32[2048,1024]{1,0:T(8,128)}, f32[1,2048]{1,0:T(1,128)S(1)}, f32[1,1024]{1,0:T(1,128)S(1)})) conditional(s32[]{:T(128)} %bitcast.5, (s32[5]{0:T(128)S(1)}, bf16[8,32,2048]{2,1,0:T(8,128)(2,1)}, bf16[8,32,2048]{2,1,0:T(8,128)(2,1)}, bf16[8,32,2048]{2,1,0:T(8,128)(2,1)}, bf16[8,32,2048]{2,1,0:T(8,128)(2,1)}, ...), branch_computations={%region_0.1_spmd, %region_1.2_spmd} | conditional | flops 4294967296 | bytes 23068680 | solution.py:188
  110.0 11.6 %partial_gram.6 = (f32[2048,1024]{1,0:T(8,128)}, f32[1,2048]{1,0:T(1,128)S(1)}, f32[1,1024]{1,0:T(1,128)S(1)}) custom-call(s32[5]{0:T(128)S(1)} %get-tuple-element.292.refs_0_, bf16[8,32,2048]{2,1,0:T(8,128)(2,1)} %get-tuple-element.293.refs_1_, bf16[8,32,2048]{2,1,0:T(8,128)(2,1)} %get-tuple-element.294.refs_2_, ...), custom_call_target="tpu_custom_call" | custom-call | flops 4294967296 | bytes 23068672 | tf_op jit(solution)/shard_map/cond/branch_0_fun/partial_gram/pallas_call | solution.py:184
  121.7 2.7 %collective-permute-start.27 = (bf16[8,32,2048]{2,1,0:T(8,128)(2,1)}, bf16[8,32,2048]{2,1,0:T(8,128)(2,1)}, u32[]{:S(2)}, u32[]{:S(2)}) collective-permute-start(bf16[8,32,2048]{2,1,0:T(8,128)(2,1)} %collective-permute-done.19), channel_id=1, source_target_pairs={{0,12},{1,97},{2,14},{3,99},{4,0},{5,101},{6,2},{7,103},{8,4},{9,1... | collective-permute-start | bytes 3145736 | tf_op jit(solution)/shard_map/ppermute | solution.py:200
  125.0 12.8 %conditional.4 = ((f32[2048,1024]{1,0:T(8,128)}, f32[1,2048]{1,0:T(1,128)S(1)}, f32[1,1024]{1,0:T(1,128)S(1)})) conditional(s32[]{:T(128)} %convert_element_type.10, (s32[5]{0:T(128)S(1)}, bf16[8,32,2048]{2,1,0:T(8,128)(2,1)}, bf16[8,32,2048]{2,1,0:T(8,128)(2,1)}, bf16[8,32,2048]{2,1,0:T(8,128)(2,1)}, bf16[8,32,2048]{2,1,0:T(8,128)(2,1)}, ...), branch_computations={%region_2.3_spmd, %region_3.4_spmd} | conditional | flops 3221225472 | bytes 21495816 | solution.py:188
  125.0 12.8 %partial_gram.8 = (f32[2048,1024]{1,0:T(8,128)}, f32[1,2048]{1,0:T(1,128)S(1)}, f32[1,1024]{1,0:T(1,128)S(1)}) custom-call(s32[5]{0:T(128)S(1)} %get-tuple-element.326.refs_0_, bf16[8,32,2048]{2,1,0:T(8,128)(2,1)} %get-tuple-element.327.refs_1_, bf16[8,32,2048]{2,1,0:T(8,128)(2,1)} %get-tuple-element.328.refs_2_, ...), custom_call_target="tpu_custom_call" | custom-call | flops 3221225472 | bytes 21495808 | tf_op jit(solution)/shard_map/cond/branch_0_fun/partial_gram/pallas_call | solution.py:184
  138.6 2.2 %collective-permute-done.26 = bf16[8,32,2048]{2,1,0:T(8,128)(2,1)S(1)} collective-permute-done((bf16[8,32,2048]{2,1,0:T(8,128)(2,1)}, bf16[8,32,2048]{2,1,0:T(8,128)(2,1)S(1)}, u32[]{:S(2)}, u32[]{:S(2)}) %collective-permute-start.26) | collective-permute-done | bytes 1048608 | tf_op jit(solution)/shard_map/ppermute | solution.py:200
  140.7 1.5 collective-permute-done.29
  142.2 20.4 %conditional.5 = (f32[2048,1024]{1,0:T(8,128)}) conditional(s32[]{:T(128)} %convert_element_type.10, (s32[5]{0:T(128)S(1)}, bf16[8,32,2048]{2,1,0:T(8,128)(2,1)}, bf16[8,32,2048]{2,1,0:T(8,128)(2,1)}, bf16[8,32,2048]{2,1,0:T(8,128)(2,1)}, bf16[8,32,2048]{2,1,0:T(8,128)(2,1)}, /*index=5*/bf16[8,32,2048]{2,1,0:T(8,128)(2,1)}, ...), branch_computations={%region_4.5_spmd, %region_5.6_spmd} | conditional | flops 9663676416 | bytes 30933000 | solution.py:188
  142.2 20.2 %partial_gram.10 = f32[2048,1024]{1,0:T(8,128)} custom-call(s32[5]{0:T(128)S(1)} %get-tuple-element.362.refs_0_, bf16[8,32,2048]{2,1,0:T(8,128)(2,1)} %get-tuple-element.363.refs_1_, bf16[8,32,2048]{2,1,0:T(8,128)(2,1)} %get-tuple-element.364.refs_2_, bf16[8,32,2048]{2,1,0:T(8,128)(2,1)} %get-tuple-element.365.refs_3_, ...), custom_call_target="tpu_custom_call" | custom-call | flops 9663676416 | bytes 30932992 | tf_op jit(solution)/shard_map/cond/branch_0_fun/partial_gram/pallas_call | solution.py:184
  (46 shorter events, 6.2 us)
Async XLA Ops:
  5.3 24.8 %all-to-all-start = ((bf16[8,32,2048]{2,1,0:T(8,128)(2,1)}), bf16[8,32,2048]{2,1,0:T(8,128)(2,1)}, u32[]{:S(2)}, u32[]{:S(2)}) async-start(bf16[8,32,2048]{2,1,0:T(8,128)(2,1)} %emphasize.2), calls=%async_computation | async-start | bytes 2097152 | tf_op jit(solution)/shard_map/all_to_all | solution.py:230
  30.1 3.0 %collective-permute-start.1 = (bf16[8,32,2048]{2,1,0:T(8,128)(2,1)}, bf16[8,32,2048]{2,1,0:T(8,128)(2,1)}, u32[]{:S(2)}, u32[]{:S(2)}) collective-permute-start(bf16[8,32,2048]{2,1,0:T(8,128)(2,1)} %emphasize.3), channel_id=1, source_target_pairs={{0,1},{1,0},{2,3},{3,2},{4,5},{5,4},{6,7},{7,6},{8,9},{9,8},{10,11... | collective-permute-start | bytes 3145736 | tf_op jit(solution)/shard_map/ppermute | solution.py:200
  30.1 20.5 %collective-permute-start.6 = (bf16[8,32,2048]{2,1,0:T(8,128)(2,1)}, bf16[8,32,2048]{2,1,0:T(8,128)(2,1)}, u32[]{:S(2)}, u32[]{:S(2)}) collective-permute-start(bf16[8,32,2048]{2,1,0:T(8,128)(2,1)} %all-to-all-done), channel_id=1, source_target_pairs={{0,4},{1,33},{2,6},{3,35},{4,8},{5,37},{6,10},{7,39},{8,12},{9,41}... | collective-permute-start | bytes 3145736 | tf_op jit(solution)/shard_map/ppermute | solution.py:200
  33.1 23.4 %all-to-all-start.1 = ((bf16[8,32,2048]{2,1,0:T(8,128)(2,1)}), bf16[8,32,2048]{2,1,0:T(8,128)(2,1)S(1)}, u32[]{:S(2)}, u32[]{:S(2)}) async-start(bf16[8,32,2048]{2,1,0:T(8,128)(2,1)} %collective-permute-done.1), calls=%async_computation.1 | async-start | bytes 2097152 | tf_op jit(solution)/shard_map/all_to_all | solution.py:230
  38.9 19.9 %collective-permute-start.14 = (bf16[8,32,2048]{2,1,0:T(8,128)(2,1)}, bf16[8,32,2048]{2,1,0:T(8,128)(2,1)}, u32[]{:S(2)}, u32[]{:S(2)}) collective-permute-start(bf16[8,32,2048]{2,1,0:T(8,128)(2,1)} %all-to-all-done), channel_id=1, source_target_pairs={{0,12},{1,97},{2,14},{3,99},{4,0},{5,101},{6,2},{7,103},{8,4},{9,1... | collective-permute-start | bytes 3145736 | tf_op jit(solution)/shard_map/ppermute | solution.py:200
  40.2 33.1 %collective-permute-start.3 = (bf16[8,32,2048]{2,1,0:T(8,128)(2,1)}, bf16[8,32,2048]{2,1,0:T(8,128)(2,1)}, u32[]{:S(2)}, u32[]{:S(2)}) collective-permute-start(bf16[8,32,2048]{2,1,0:T(8,128)(2,1)} %all-to-all-done), channel_id=1, source_target_pairs={{0,2},{1,17},{2,0},{3,19},{4,6},{5,21},{6,4},{7,23},{8,10},{9,25},... | collective-permute-start | bytes 3145736 | tf_op jit(solution)/shard_map/ppermute | solution.py:200
  50.5 22.9 %collective-permute-start.7 = (bf16[8,32,2048]{2,1,0:T(8,128)(2,1)}, bf16[8,32,2048]{2,1,0:T(8,128)(2,1)}, u32[]{:S(2)}, u32[]{:S(2)}) collective-permute-start(bf16[8,32,2048]{2,1,0:T(8,128)(2,1)} %collective-permute-done.6), channel_id=1, source_target_pairs={{0,4},{1,33},{2,6},{3,35},{4,8},{5,37},{6,10},{7,39},{8,12},{9,41}... | collective-permute-start | bytes 3145736 | tf_op jit(solution)/shard_map/ppermute | solution.py:200
  56.5 17.3 %collective-permute-start.5 = (bf16[8,32,2048]{2,1,0:T(8,128)(2,1)S(1)}, bf16[8,32,2048]{2,1,0:T(8,128)(2,1)S(1)}, u32[]{:S(2)}, u32[]{:S(2)}) collective-permute-start(bf16[8,32,2048]{2,1,0:T(8,128)(2,1)S(1)} %all-to-all-done.1), channel_id=1, source_target_pairs={{0,12},{1,97},{2,14},{3,99},{4,0},{5,101},{6,2},{7,103},{8,4},{9,1... | collective-permute-start | bytes 3145736 | tf_op jit(solution)/shard_map/ppermute | solution.py:200
  57.5 20.0 %collective-permute-start.4 = (bf16[8,32,2048]{2,1,0:T(8,128)(2,1)S(1)}, bf16[8,32,2048]{2,1,0:T(8,128)(2,1)S(1)}, u32[]{:S(2)}, u32[]{:S(2)}) collective-permute-start(bf16[8,32,2048]{2,1,0:T(8,128)(2,1)S(1)} %all-to-all-done.1), channel_id=1, source_target_pairs={{0,4},{1,33},{2,6},{3,35},{4,8},{5,37},{6,10},{7,39},{8,12},{9,41}... | collective-permute-start | bytes 3145736 | tf_op jit(solution)/shard_map/ppermute | solution.py:200
  58.8 19.1 %collective-permute-start = (bf16[8,32,2048]{2,1,0:T(8,128)(2,1)}, bf16[8,32,2048]{2,1,0:T(8,128)(2,1)}, u32[]{:S(2)}, u32[]{:S(2)}) collective-permute-start(bf16[8,32,2048]{2,1,0:T(8,128)(2,1)} %all-to-all-done), channel_id=1, source_target_pairs={{0,1},{1,0},{2,3},{3,2},{4,5},{5,4},{6,7},{7,6},{8,9},{9,8},{10,11... | collective-permute-start | bytes 3145736 | tf_op jit(solution)/shard_map/ppermute | solution.py:200
  73.2 6.2 %collective-permute-start.15 = (bf16[8,32,2048]{2,1,0:T(8,128)(2,1)}, bf16[8,32,2048]{2,1,0:T(8,128)(2,1)}, u32[]{:S(2)}, u32[]{:S(2)}) collective-permute-start(bf16[8,32,2048]{2,1,0:T(8,128)(2,1)} %collective-permute-done.14), channel_id=1, source_target_pairs={{0,1},{1,0},{2,3},{3,2},{4,5},{5,4},{6,7},{7,6},{8,9},{9,8},{10,11... | collective-permute-start | bytes 3145736 | tf_op jit(solution)/shard_map/ppermute | solution.py:200
  73.4 6.0 %collective-permute-start.22 = (bf16[8,32,2048]{2,1,0:T(8,128)(2,1)}, bf16[8,32,2048]{2,1,0:T(8,128)(2,1)}, u32[]{:S(2)}, u32[]{:S(2)}) collective-permute-start(bf16[8,32,2048]{2,1,0:T(8,128)(2,1)} %collective-permute-done.6), channel_id=1, source_target_pairs={{0,1},{1,0},{2,3},{3,2},{4,5},{5,4},{6,7},{7,6},{8,9},{9,8},{10,11... | collective-permute-start | bytes 3145736 | tf_op jit(solution)/shard_map/ppermute | solution.py:200
  73.8 14.6 %collective-permute-start.12 = (bf16[8,32,2048]{2,1,0:T(8,128)(2,1)S(1)}, bf16[8,32,2048]{2,1,0:T(8,128)(2,1)S(1)}, u32[]{:S(2)}, u32[]{:S(2)}) collective-permute-start(bf16[8,32,2048]{2,1,0:T(8,128)(2,1)S(1)} %collective-permute-done.5), channel_id=1, source_target_pairs={{0,12},{1,97},{2,14},{3,99},{4,0},{5,101},{6,2},{7,103},{8,4},{9,1... | collective-permute-start | bytes 3145736 | tf_op jit(solution)/shard_map/ppermute | solution.py:200
  77.5 25.0 %collective-permute-start.9 = (bf16[8,32,2048]{2,1,0:T(8,128)(2,1)S(1)}, bf16[8,32,2048]{2,1,0:T(8,128)(2,1)}, u32[]{:S(2)}, u32[]{:S(2)}) collective-permute-start(bf16[8,32,2048]{2,1,0:T(8,128)(2,1)S(1)} %all-to-all-done.1), channel_id=1, source_target_pairs={{0,2},{1,17},{2,0},{3,19},{4,6},{5,21},{6,4},{7,23},{8,10},{9,25},... | collective-permute-start | bytes 3145736 | tf_op jit(solution)/shard_map/ppermute | solution.py:200
  77.9 26.2 %collective-permute-start.11 = (bf16[8,32,2048]{2,1,0:T(8,128)(2,1)}, bf16[8,32,2048]{2,1,0:T(8,128)(2,1)}, u32[]{:S(2)}, u32[]{:S(2)}) collective-permute-start(bf16[8,32,2048]{2,1,0:T(8,128)(2,1)} %collective-permute-done.3), channel_id=1, source_target_pairs={{0,12},{1,97},{2,14},{3,99},{4,0},{5,101},{6,2},{7,103},{8,4},{9,1... | collective-permute-start | bytes 3145736 | tf_op jit(solution)/shard_map/ppermute | solution.py:200
  79.4 24.8 %collective-permute-start.10 = (bf16[8,32,2048]{2,1,0:T(8,128)(2,1)}, bf16[8,32,2048]{2,1,0:T(8,128)(2,1)}, u32[]{:S(2)}, u32[]{:S(2)}) collective-permute-start(bf16[8,32,2048]{2,1,0:T(8,128)(2,1)} %collective-permute-done.3), channel_id=1, source_target_pairs={{0,4},{1,33},{2,6},{3,35},{4,8},{5,37},{6,10},{7,39},{8,12},{9,41}... | collective-permute-start | bytes 3145736 | tf_op jit(solution)/shard_map/ppermute | solution.py:200
  79.4 25.3 %collective-permute-start.2 = (bf16[8,32,2048]{2,1,0:T(8,128)(2,1)S(1)}, bf16[8,32,2048]{2,1,0:T(8,128)(2,1)}, u32[]{:S(2)}, u32[]{:S(2)}) collective-permute-start(bf16[8,32,2048]{2,1,0:T(8,128)(2,1)S(1)} %all-to-all-done.1), channel_id=1, source_target_pairs={{0,1},{1,0},{2,3},{3,2},{4,5},{5,4},{6,7},{7,6},{8,9},{9,8},{10,11... | collective-permute-start | bytes 3145736 | tf_op jit(solution)/shard_map/ppermute | solution.py:200
  88.3 16.6 %collective-permute-start.20 = (bf16[8,32,2048]{2,1,0:T(8,128)(2,1)}, bf16[8,32,2048]{2,1,0:T(8,128)(2,1)}, u32[]{:S(2)}, u32[]{:S(2)}) collective-permute-start(bf16[8,32,2048]{2,1,0:T(8,128)(2,1)} %collective-permute-done.7), channel_id=1, source_target_pairs={{0,1},{1,0},{2,3},{3,2},{4,5},{5,4},{6,7},{7,6},{8,9},{9,8},{10,11... | collective-permute-start | bytes 3145736 | tf_op jit(solution)/shard_map/ppermute | solution.py:200
  102.4 5.0 %collective-permute-start.16 = (bf16[8,32,2048]{2,1,0:T(8,128)(2,1)S(1)}, bf16[8,32,2048]{2,1,0:T(8,128)(2,1)}, u32[]{:S(2)}, u32[]{:S(2)}) collective-permute-start(bf16[8,32,2048]{2,1,0:T(8,128)(2,1)S(1)} %collective-permute-done.5), channel_id=1, source_target_pairs={{0,1},{1,0},{2,3},{3,2},{4,5},{5,4},{6,7},{7,6},{8,9},{9,8},{10,11... | collective-permute-start | bytes 3145736 | tf_op jit(solution)/shard_map/ppermute | solution.py:200
  104.2 4.3 %collective-permute-start.23 = (bf16[8,32,2048]{2,1,0:T(8,128)(2,1)S(1)}, bf16[8,32,2048]{2,1,0:T(8,128)(2,1)}, u32[]{:S(2)}, u32[]{:S(2)}) collective-permute-start(bf16[8,32,2048]{2,1,0:T(8,128)(2,1)S(1)} %collective-permute-done.4), channel_id=1, source_target_pairs={{0,1},{1,0},{2,3},{3,2},{4,5},{5,4},{6,7},{7,6},{8,9},{9,8},{10,11... | collective-permute-start | bytes 3145736 | tf_op jit(solution)/shard_map/ppermute | solution.py:200
  104.2 5.4 %collective-permute-start.21 = (bf16[8,32,2048]{2,1,0:T(8,128)(2,1)S(1)}, bf16[8,32,2048]{2,1,0:T(8,128)(2,1)}, u32[]{:S(2)}, u32[]{:S(2)}) collective-permute-start(bf16[8,32,2048]{2,1,0:T(8,128)(2,1)S(1)} %collective-permute-done.12), channel_id=1, source_target_pairs={{0,1},{1,0},{2,3},{3,2},{4,5},{5,4},{6,7},{7,6},{8,9},{9,8},{10,11... | collective-permute-start | bytes 3145736 | tf_op jit(solution)/shard_map/ppermute | solution.py:200
  104.7 16.9 %collective-permute-start.19 = (bf16[8,32,2048]{2,1,0:T(8,128)(2,1)}, bf16[8,32,2048]{2,1,0:T(8,128)(2,1)}, u32[]{:S(2)}, u32[]{:S(2)}) collective-permute-start(bf16[8,32,2048]{2,1,0:T(8,128)(2,1)} %collective-permute-done.9), channel_id=1, source_target_pairs={{0,12},{1,97},{2,14},{3,99},{4,0},{5,101},{6,2},{7,103},{8,4},{9,1... | collective-permute-start | bytes 3145736 | tf_op jit(solution)/shard_map/ppermute | solution.py:200
  104.9 16.8 %collective-permute-start.18 = (bf16[8,32,2048]{2,1,0:T(8,128)(2,1)}, bf16[8,32,2048]{2,1,0:T(8,128)(2,1)}, u32[]{:S(2)}, u32[]{:S(2)}) collective-permute-start(bf16[8,32,2048]{2,1,0:T(8,128)(2,1)} %collective-permute-done.9), channel_id=1, source_target_pairs={{0,4},{1,33},{2,6},{3,35},{4,8},{5,37},{6,10},{7,39},{8,12},{9,41}... | collective-permute-start | bytes 3145736 | tf_op jit(solution)/shard_map/ppermute | solution.py:200
  107.4 16.9 %collective-permute-start.8 = (bf16[8,32,2048]{2,1,0:T(8,128)(2,1)}, bf16[8,32,2048]{2,1,0:T(8,128)(2,1)}, u32[]{:S(2)}, u32[]{:S(2)}) collective-permute-start(bf16[8,32,2048]{2,1,0:T(8,128)(2,1)} %collective-permute-done.3), channel_id=1, source_target_pairs={{0,1},{1,0},{2,3},{3,2},{4,5},{5,4},{6,7},{7,6},{8,9},{9,8},{10,11... | collective-permute-start | bytes 3145736 | tf_op jit(solution)/shard_map/ppermute | solution.py:200
  108.4 15.9 %collective-permute-start.17 = (bf16[8,32,2048]{2,1,0:T(8,128)(2,1)}, bf16[8,32,2048]{2,1,0:T(8,128)(2,1)}, u32[]{:S(2)}, u32[]{:S(2)}) collective-permute-start(bf16[8,32,2048]{2,1,0:T(8,128)(2,1)} %collective-permute-done.11), channel_id=1, source_target_pairs={{0,1},{1,0},{2,3},{3,2},{4,5},{5,4},{6,7},{7,6},{8,9},{9,8},{10,11... | collective-permute-start | bytes 3145736 | tf_op jit(solution)/shard_map/ppermute | solution.py:200
  109.6 15.3 %collective-permute-start.28 = (bf16[8,32,2048]{2,1,0:T(8,128)(2,1)}, bf16[8,32,2048]{2,1,0:T(8,128)(2,1)}, u32[]{:S(2)}, u32[]{:S(2)}) collective-permute-start(bf16[8,32,2048]{2,1,0:T(8,128)(2,1)} %collective-permute-done.10), channel_id=1, source_target_pairs={{0,1},{1,0},{2,3},{3,2},{4,5},{5,4},{6,7},{7,6},{8,9},{9,8},{10,11... | collective-permute-start | bytes 3145736 | tf_op jit(solution)/shard_map/ppermute | solution.py:200
  121.6 16.2 %collective-permute-start.25 = (bf16[8,32,2048]{2,1,0:T(8,128)(2,1)}, bf16[8,32,2048]{2,1,0:T(8,128)(2,1)}, u32[]{:S(2)}, u32[]{:S(2)}) collective-permute-start(bf16[8,32,2048]{2,1,0:T(8,128)(2,1)} %collective-permute-done.10), channel_id=1, source_target_pairs={{0,4},{1,33},{2,6},{3,35},{4,8},{5,37},{6,10},{7,39},{8,12},{9,41}... | collective-permute-start | bytes 3145736 | tf_op jit(solution)/shard_map/ppermute | solution.py:200
  121.7 16.2 %collective-permute-start.27 = (bf16[8,32,2048]{2,1,0:T(8,128)(2,1)}, bf16[8,32,2048]{2,1,0:T(8,128)(2,1)}, u32[]{:S(2)}, u32[]{:S(2)}) collective-permute-start(bf16[8,32,2048]{2,1,0:T(8,128)(2,1)} %collective-permute-done.19), channel_id=1, source_target_pairs={{0,12},{1,97},{2,14},{3,99},{4,0},{5,101},{6,2},{7,103},{8,4},{9,1... | collective-permute-start | bytes 3145736 | tf_op jit(solution)/shard_map/ppermute | solution.py:200
  124.3 14.2 %collective-permute-start.13 = (bf16[8,32,2048]{2,1,0:T(8,128)(2,1)}, bf16[8,32,2048]{2,1,0:T(8,128)(2,1)}, u32[]{:S(2)}, u32[]{:S(2)}) collective-permute-start(bf16[8,32,2048]{2,1,0:T(8,128)(2,1)} %collective-permute-done.9), channel_id=1, source_target_pairs={{0,1},{1,0},{2,3},{3,2},{4,5},{5,4},{6,7},{7,6},{8,9},{9,8},{10,11... | collective-permute-start | bytes 3145736 | tf_op jit(solution)/shard_map/ppermute | solution.py:200
  124.4 16.4 %collective-permute-start.24 = (bf16[8,32,2048]{2,1,0:T(8,128)(2,1)}, bf16[8,32,2048]{2,1,0:T(8,128)(2,1)}, u32[]{:S(2)}, u32[]{:S(2)}) collective-permute-start(bf16[8,32,2048]{2,1,0:T(8,128)(2,1)} %collective-permute-done.19), channel_id=1, source_target_pairs={{0,1},{1,0},{2,3},{3,2},{4,5},{5,4},{6,7},{7,6},{8,9},{9,8},{10,11... | collective-permute-start | bytes 3145736 | tf_op jit(solution)/shard_map/ppermute | solution.py:200
  124.9 15.9 %collective-permute-start.30 = (bf16[8,32,2048]{2,1,0:T(8,128)(2,1)}, bf16[8,32,2048]{2,1,0:T(8,128)(2,1)}, u32[]{:S(2)}, u32[]{:S(2)}) collective-permute-start(bf16[8,32,2048]{2,1,0:T(8,128)(2,1)} %collective-permute-done.18), channel_id=1, source_target_pairs={{0,1},{1,0},{2,3},{3,2},{4,5},{5,4},{6,7},{7,6},{8,9},{9,8},{10,11... | collective-permute-start | bytes 3145736 | tf_op jit(solution)/shard_map/ppermute | solution.py:200
  137.9 4.3 %collective-permute-start.29 = (bf16[8,32,2048]{2,1,0:T(8,128)(2,1)}, bf16[8,32,2048]{2,1,0:T(8,128)(2,1)S(1)}, u32[]{:S(2)}, u32[]{:S(2)}) collective-permute-start(bf16[8,32,2048]{2,1,0:T(8,128)(2,1)} %collective-permute-done.27), channel_id=1, source_target_pairs={{0,1},{1,0},{2,3},{3,2},{4,5},{5,4},{6,7},{7,6},{8,9},{9,8},{10,11... | collective-permute-start | bytes 3145736 | tf_op jit(solution)/shard_map/ppermute | solution.py:200
  (2 other events, 24.6 us)

commit v4 on v3

--- a/solution.py
+++ b/solution.py
@@ -21,10 +21,10 @@
     return [(z, xl, y, xh, c) for z in range(4) for xl in range(2) for y in range(4) for xh in range(2) for c in range(2)]
 
 
-def emphasize_kernel(side, pos_ref, base_ref, inst_ref, base_sup_ref, inst_sup_ref, out_ref, pre_ref, support_ref, mask_ref, sem):
+def emphasize_kernel(side, base_ref, inst_ref, base_sup_ref, inst_sup_ref, out_ref, pre_ref, support_ref, mask_ref, sem):
     for own, pre, sup in ((side, base_ref, base_sup_ref), (1 - side, inst_ref, inst_sup_ref)):
 
-        @pl.when(pos_ref[4] == own)
+        @pl.when(lax.axis_index("inst") % 2 == own)
         def _(pre=pre, sup=sup):
             pltpu.make_async_copy(sup, support_ref, sem.at[0]).start()
             pltpu.make_async_copy(pre, pre_ref, sem.at[1]).start()
@@ -46,7 +46,7 @@
         )
         return carry
 
-    lax.fori_loop(0, toks, token, 0, unroll=8)
+    lax.fori_loop(0, toks, token, 0, unroll=32)
     pltpu.make_async_copy(base_ref, pre_ref, sem.at[1]).wait()
     total = jnp.zeros((toks, 128), jnp.float32)
     for g in range(groups):
@@ -60,12 +60,12 @@
         out_ref[block, :, place : place + 128] = (wide * scale * (1.0 + 3.0 * on)).astype(jnp.bfloat16)
 
 
-def emphasize(side, pos, base_pre, inst_pre, base_support, inst_support):
+def emphasize(side, base_pre, inst_pre, base_support, inst_support):
     toks, latents = base_pre.shape
     return pl.pallas_call(
         functools.partial(emphasize_kernel, side),
         out_shape=jax.ShapeDtypeStruct((8, toks, latents // 8), jnp.bfloat16),
-        in_specs=[pl.BlockSpec(memory_space=pltpu.SMEM)] + [pl.BlockSpec(memory_space=pl.ANY)] * 4,
+        in_specs=[pl.BlockSpec(memory_space=pl.ANY)] * 4,
         out_specs=pl.BlockSpec(memory_space=pltpu.VMEM),
         scratch_shapes=[
             pltpu.VMEM(base_pre.shape, base_pre.dtype),
@@ -76,7 +76,7 @@
         compiler_params=pltpu.CompilerParams(vmem_limit_bytes=56 << 20),
         cost_estimate=pl.CostEstimate(flops=1 << 30, bytes_accessed=4 << 20, transcendentals=0),
         name="emphasize",
-    )(pos, base_pre, inst_pre, base_support, inst_support)
+    )(base_pre, inst_pre, base_support, inst_support)
 
 
 def dot_kernel(pairs, base_keys, inst_keys, first, last, total, *refs):
@@ -97,8 +97,8 @@
     def _():
         columns = pl.ds(pl.multiple_of(c * n, n), n)
         copies = []
-        for row, ((dy, dxh, _), key) in enumerate(pairs):
-            source = inst[key].at[((y + dy) & 3) * 2 + (xh ^ dxh), :, columns]
+        for row, ((dy, other, _), key, u) in enumerate(pairs):
+            source = inst[key].at[((y + dy) & 3) * 2 + (u ^ other ^ xl ^ xh), :, columns]
             copies.append(pltpu.make_async_copy(source, rhs_ref.at[pl.ds(row * ROWS, ROWS)], sem))
         for copy in copies:
             copy.start()
@@ -113,8 +113,8 @@
 
     blocks = []
     sums = jnp.zeros((8, TILE), jnp.float32)
-    for key, (dz, dxl, _) in pairs:
-        rows = base[key][((z + dz) & 3) * 2 + (xl ^ dxl)]
+    for key, (dz, _, _), u in pairs:
+        rows = base[key][((z + dz) & 3) * 2 + u]
         blocks.append(rows)
         wide = rows.astype(jnp.float32)
         sums = sums + jnp.sum((wide * wide).reshape(4, 8, -1), axis=0)
@@ -142,8 +142,8 @@
 
 def partial_gram(pos, own, mate, pairs, carry, last, total):
     first = carry is None
-    base_keys = sorted({key for key, _ in pairs})
-    inst_keys = sorted({key for _, key in pairs})
+    base_keys = sorted({pair[0] for pair in pairs})
+    inst_keys = sorted({pair[1] for pair in pairs})
     m = own[base_keys[0]].shape[-1]
     n = m // 2
     carry_specs = [
@@ -223,14 +223,14 @@
     pos = jnp.stack([row // 2, row % 2, column // 4, column // 2 % 2, column % 2]).astype(jnp.int32)
     codes = [base_pre, inst_pre, base_support, inst_support]
     groups = [
-        [device(z, xl, y, xh, 0) for z in range(4) for xl in range(2)] for y in range(4) for xh in range(2)
-    ] + [[device(z, xl, y, xh, 1) for y in range(4) for xh in range(2)] for z in range(4) for xl in range(2)]
+        [device(z, xl, y, xl ^ p, 0) for z in range(4) for xl in range(2)] for y in range(4) for p in range(2)
+    ] + [[device(z, xh ^ p, y, xh, 1) for y in range(4) for xh in range(2)] for z in range(4) for p in range(2)]
 
     def spread(x):
         return lax.all_to_all(x, AXES, 0, 0, axis_index_groups=groups, tiled=True)
 
-    staying = emphasize(0, pos, *codes)
-    leaving = emphasize(1, after(pos, staying), *codes)
+    staying = emphasize(0, *codes)
+    leaving = emphasize(1, *after(codes, staying))
     a = spread(staying)
     leaving, a = tie((leaving, a))
     arriving = mated(leaving)
@@ -240,30 +240,32 @@
     a2 = ring(a3, 1)
     b3, b1 = ring(b, 1), ring(b, -1)
     b2 = ring(b1, -1)
-    xa = after(xa, b3, b1, a2)
     xb = across(after(b, xa))
+    xa = after(xa, a2)
     xa3, xa1 = ring(xa, 1), ring(xa, -1)
-    xb = after(xb, xa3, xa1, b2)
+    xb = after(xb, xa3, xa1)
     xb3, xb1 = ring(xb, 1), ring(xb, -1)
     xa2 = ring(xa3, 1)
     own = {(0, 0, 0): a, (1, 0, 0): a1, (2, 0, 0): a2, (3, 0, 0): a3}
     own |= {(0, 0, 1): b, (1, 0, 1): b1, (2, 0, 1): b2, (3, 0, 1): b3}
     mate = {key: mated(x) for key, x in own.items()}
-    steps = [(k, dx) for k in range(4) for dx in range(2)]
-    blocks = [(p + (t,), q + (1 - t,)) for t in range(2) for q in steps for p in steps]
-    early = [(p, q) for p, q in blocks if p[1] == 0 and q[1] == 0]
-    ready = [(p, q) for p, q in blocks if {p[1:], q[1:]} in ({(0, 0), (0, 1)}, {(1, 0), (0, 1)}) and (2, 1) not in (p[:2], q[:2])]
-    middle = [pair for pair in ready if pair not in early]
-    late = [pair for pair in blocks if pair not in ready]
+    blocks = [
+        ((k, d, t), (q, d, 1 - t), u)
+        for d in range(2) for t in range(2) for q in range(4) for k in range(4) for u in range(2)
+    ]
+    early = [pair for pair in blocks if pair[0][1] == 0]
+    middle = [pair for pair in blocks if pair[0][1] == 1 and 2 not in (pair[0][0], pair[1][0])]
+    late = [pair for pair in blocks if pair not in early + middle]
     carry = partial_gram(after(pos, xb), own, mate, early, None, False, total)
     xb3, xb1, carry = tie((xb3, xb1, carry))
     xb2 = ring(xb1, -1)
     more = {(0, 1, 0): xa, (1, 1, 0): xa1, (3, 1, 0): xa3}
+    more |= {(0, 1, 1): xb, (1, 1, 1): xb1, (3, 1, 1): xb3}
     own |= more
     mate |= {key: mated(x) for key, x in more.items()}
     carry = partial_gram(pos, own, mate, middle, carry, False, total)
-    xb2, carry = tie((xb2, carry))
-    more = {(2, 1, 0): xa2, (0, 1, 1): xb, (1, 1, 1): xb1, (2, 1, 1): xb2, (3, 1, 1): xb3}
+    xb2, xa2, carry = tie((xb2, xa2, carry))
+    more = {(2, 1, 0): xa2, (2, 1, 1): xb2}
     own |= more
     mate |= {key: mated(x) for key, x in more.items()}
     return partial_gram(pos, own, mate, late, carry, True, total)

time: 163 us -> 162 us (level)
  Pallas kernels: 54.9 us -> 51.8 us
    ppermute x31, waiting for transfers between devices: 51.2 us -> 53.7 us  [send(): lax.ppermute(x, AXES, [(device(*p), device(*target(*p))) for p in places()])]
    ppermute x31, starting transfers between devices: 23.4 us -> 25.3 us  [send(): lax.ppermute(x, AXES, [(device(*p), device(*target(*p))) for p in places()])]
    all_to_all x2, starting transfers between devices: 13.4 us -> 11.5 us  [spread(): return lax.all_to_all(x, AXES, 0, 0, axis_index_groups=groups, tiled=True)]
    pallas_call x2, Pallas kernels: 10.3 us -> 8.52 us  [emphasize(): pl.pallas_call(functools.partial(emphasize_kernel, side), out_shape=jax.S...]
  transfers between devices with their start and end apart: 33 -> 33, of which waited for: 12 -> 13; matrix products, arithmetic and copies ran while one was open for 0% -> 0% of each run, Pallas kernels for 18% -> 21%
where the time goes in v4:
time: 162 us; the launch traced here: 161 us
  waiting for transfers between devices  70.3 us (43%)
  Pallas kernels  51.8 us (32%)
  starting transfers between devices  36.8 us (23%)
    ppermute x31, waiting for transfers between devices, send(): lax.ppermute(x, AXES, [(device(*p), device(*target(*p))) for p in places()])  53.7 us
    pallas_call x3, Pallas kernels, run(): call(pos, *[base[k] for k in base_keys], *[inst[k] for k in inst_keys], *...  43.3 us
    ppermute x31, starting transfers between devices, send(): lax.ppermute(x, AXES, [(device(*p), device(*target(*p))) for p in places()])  25.3 us
    all_to_all x2, waiting for transfers between devices, spread(): return lax.all_to_all(x, AXES, 0, 0, axis_index_groups=groups, tiled=True)  16.6 us
    all_to_all x2, starting transfers between devices, spread(): return lax.all_to_all(x, AXES, 0, 0, axis_index_groups=groups, tiled=True)  11.5 us
    pallas_call x2, Pallas kernels, emphasize(): pl.pallas_call(functools.partial(emphasize_kernel, side), out_shape=jax.S...  8.52 us
  transfers between devices with their start and end apart: 33, of which 13 were waited for; matrix products, arithmetic and copies ran while one was open for 0% of the time, Pallas kernels for 21%

profile of v4, /device:TPU:1, one launch (start us, length us, event | category | flops | bytes accessed | tf_op | source)
XLA Modules:
  0.0 161.4 jit_solution(149174231669211174)
XLA Ops:
  0.0 4.3 %emphasize.2 = bf16[8,32,2048]{2,1,0:T(8,128)(2,1)} custom-call(bf16[32,16384]{1,0:T(8,128)(2,1)} %base_ref.2, bf16[32,16384]{1,0:T(8,128)(2,1)} %inst_ref.2, s32[32,128]{1,0:T(8,128)} %base_sup_ref.2, s32[32,128]{1,0:T(8,128)} %inst_sup_ref.2), custom_call_target="tpu_custom_call" | custom-call | flops 1073741824 | bytes 4194304 | tf_op jit(solution)/shard_map/emphasize/pallas_call | solution.py:65
  4.3 7.2 %all-to-all-start = ((bf16[8,32,2048]{2,1,0:T(8,128)(2,1)}), bf16[8,32,2048]{2,1,0:T(8,128)(2,1)S(1)}, u32[]{:S(2)}, u32[]{:S(2)}) async-start(bf16[8,32,2048]{2,1,0:T(8,128)(2,1)} %emphasize.2), calls=%async_computation | async-start | bytes 2097152 | tf_op jit(solution)/shard_map/all_to_all | solution.py:230
  11.5 4.3 %emphasize.3 = bf16[8,32,2048]{2,1,0:T(8,128)(2,1)} custom-call(bf16[32,16384]{1,0:T(8,128)(2,1)} %base_ref.2, bf16[32,16384]{1,0:T(8,128)(2,1)} %inst_ref.2, s32[32,128]{1,0:T(8,128)} %base_sup_ref.2, s32[32,128]{1,0:T(8,128)} %inst_sup_ref.2), custom_call_target="tpu_custom_call" | custom-call | flops 1073741824 | bytes 4194304 | tf_op jit(solution)/shard_map/emphasize/pallas_call | solution.py:65
  15.8 10.2 %all-to-all-done = bf16[8,32,2048]{2,1,0:T(8,128)(2,1)S(1)} async-done(((bf16[8,32,2048]{2,1,0:T(8,128)(2,1)}), bf16[8,32,2048]{2,1,0:T(8,128)(2,1)S(1)}, u32[]{:S(2)}, u32[]{:S(2)}) %all-to-all-start) | async-done | bytes 1048608 | tf_op jit(solution)/shard_map/all_to_all | solution.py:230
  26.0 4.7 %collective-permute-start.4 = (bf16[8,32,2048]{2,1,0:T(8,128)(2,1)}, bf16[8,32,2048]{2,1,0:T(8,128)(2,1)}, u32[]{:S(2)}, u32[]{:S(2)}) collective-permute-start(bf16[8,32,2048]{2,1,0:T(8,128)(2,1)} %emphasize.3), channel_id=1, source_target_pairs={{0,1},{1,0},{2,3},{3,2},{4,5},{5,4},{6,7},{7,6},{8,9},{9,8},{10,11... | collective-permute-start | bytes 3145736 | tf_op jit(solution)/shard_map/ppermute | solution.py:200
  30.7 2.7 %collective-permute-start.14 = (bf16[8,32,2048]{2,1,0:T(8,128)(2,1)S(1)}, bf16[8,32,2048]{2,1,0:T(8,128)(2,1)}, u32[]{:S(2)}, u32[]{:S(2)}) collective-permute-start(bf16[8,32,2048]{2,1,0:T(8,128)(2,1)S(1)} %all-to-all-done), channel_id=1, source_target_pairs={{0,12},{1,97},{2,14},{3,99},{4,0},{5,101},{6,2},{7,103},{8,4},{9,1... | collective-permute-start | bytes 3145736 | tf_op jit(solution)/shard_map/ppermute | solution.py:200
  33.4 4.3 %all-to-all-start.1 = ((bf16[8,32,2048]{2,1,0:T(8,128)(2,1)}), bf16[8,32,2048]{2,1,0:T(8,128)(2,1)}, u32[]{:S(2)}, u32[]{:S(2)}) async-start(bf16[8,32,2048]{2,1,0:T(8,128)(2,1)} %collective-permute-done.4), calls=%async_computation.1 | async-start | bytes 2097152 | tf_op jit(solution)/shard_map/all_to_all | solution.py:230
  38.5 10.3 %collective-permute-done.1 = bf16[8,32,2048]{2,1,0:T(8,128)(2,1)S(1)} collective-permute-done((bf16[8,32,2048]{2,1,0:T(8,128)(2,1)S(1)}, bf16[8,32,2048]{2,1,0:T(8,128)(2,1)S(1)}, u32[]{:S(2)}, u32[]{:S(2)}) %collective-permute-start.1) | collective-permute-done | bytes 1048608 | tf_op jit(solution)/shard_map/ppermute | solution.py:200
  48.8 1.7 %collective-permute-start.21 = (bf16[8,32,2048]{2,1,0:T(8,128)(2,1)S(1)}, bf16[8,32,2048]{2,1,0:T(8,128)(2,1)}, u32[]{:S(2)}, u32[]{:S(2)}) collective-permute-start(bf16[8,32,2048]{2,1,0:T(8,128)(2,1)S(1)} %collective-permute-done.1), channel_id=1, source_target_pairs={{0,1},{1,0},{2,3},{3,2},{4,5},{5,4},{6,7},{7,6},{8,9},{9,8},{10,11... | collective-permute-start | bytes 3145736 | tf_op jit(solution)/shard_map/ppermute | solution.py:200
  50.5 6.7 %collective-permute-done = bf16[8,32,2048]{2,1,0:T(8,128)(2,1)S(1)} collective-permute-done((bf16[8,32,2048]{2,1,0:T(8,128)(2,1)S(1)}, bf16[8,32,2048]{2,1,0:T(8,128)(2,1)S(1)}, u32[]{:S(2)}, u32[]{:S(2)}) %collective-permute-start) | collective-permute-done | bytes 1048608 | tf_op jit(solution)/shard_map/ppermute | solution.py:200
  57.3 6.4 %all-to-all-done.1 = bf16[8,32,2048]{2,1,0:T(8,128)(2,1)} async-done(((bf16[8,32,2048]{2,1,0:T(8,128)(2,1)}), bf16[8,32,2048]{2,1,0:T(8,128)(2,1)}, u32[]{:S(2)}, u32[]{:S(2)}) %all-to-all-start.1) | async-done | bytes 1048608 | tf_op jit(solution)/shard_map/all_to_all | solution.py:230
  63.8 2.7 %collective-permute-done.2 = bf16[8,32,2048]{2,1,0:T(8,128)(2,1)} collective-permute-done((bf16[8,32,2048]{2,1,0:T(8,128)(2,1)S(1)}, bf16[8,32,2048]{2,1,0:T(8,128)(2,1)}, u32[]{:S(2)}, u32[]{:S(2)}) %collective-permute-start.2) | collective-permute-done | bytes 1048608 | tf_op jit(solution)/shard_map/ppermute | solution.py:200
  66.6 2.7 %collective-permute-start.7 = (bf16[8,32,2048]{2,1,0:T(8,128)(2,1)S(1)}, bf16[8,32,2048]{2,1,0:T(8,128)(2,1)S(1)}, u32[]{:S(2)}, u32[]{:S(2)}) collective-permute-start(bf16[8,32,2048]{2,1,0:T(8,128)(2,1)S(1)} %collective-permute-done), channel_id=1, source_target_pairs={{0,12},{1,97},{2,14},{3,99},{4,0},{5,101},{6,2},{7,103},{8,4},{9,1... | collective-permute-start | bytes 3145736 | tf_op jit(solution)/shard_map/ppermute | solution.py:200
  69.3 8.6 %collective-permute-done.16 = bf16[8,32,2048]{2,1,0:T(8,128)(2,1)S(1)} collective-permute-done((bf16[8,32,2048]{2,1,0:T(8,128)(2,1)}, bf16[8,32,2048]{2,1,0:T(8,128)(2,1)S(1)}, u32[]{:S(2)}, u32[]{:S(2)}) %collective-permute-start.16) | collective-permute-done | bytes 1048608 | tf_op jit(solution)/shard_map/ppermute | solution.py:200
  77.8 1.2 collective-permute-start.19
  79.0 9.8 %collective-permute-done.5 = bf16[8,32,2048]{2,1,0:T(8,128)(2,1)S(1)} collective-permute-done((bf16[8,32,2048]{2,1,0:T(8,128)(2,1)}, bf16[8,32,2048]{2,1,0:T(8,128)(2,1)S(1)}, u32[]{:S(2)}, u32[]{:S(2)}) %collective-permute-start.5) | collective-permute-done | bytes 1048608 | tf_op jit(solution)/shard_map/ppermute | solution.py:200
  89.3 3.8 %collective-permute-done.6 = bf16[8,32,2048]{2,1,0:T(8,128)(2,1)S(1)} collective-permute-done((bf16[8,32,2048]{2,1,0:T(8,128)(2,1)S(1)}, bf16[8,32,2048]{2,1,0:T(8,128)(2,1)S(1)}, u32[]{:S(2)}, u32[]{:S(2)}) %collective-permute-start.6) | collective-permute-done | bytes 1048608 | tf_op jit(solution)/shard_map/ppermute | solution.py:200
  93.1 1.6 %collective-permute-start.17 = (bf16[8,32,2048]{2,1,0:T(8,128)(2,1)S(1)}, bf16[8,32,2048]{2,1,0:T(8,128)(2,1)S(1)}, u32[]{:S(2)}, u32[]{:S(2)}) collective-permute-start(bf16[8,32,2048]{2,1,0:T(8,128)(2,1)S(1)} %collective-permute-done.16), channel_id=1, source_target_pairs={{0,1},{1,0},{2,3},{3,2},{4,5},{5,4},{6,7},{7,6},{8,9},{9,8},{10,11... | collective-permute-start | bytes 3145736 | tf_op jit(solution)/shard_map/ppermute | solution.py:200
  94.8 5.5 %collective-permute-done.19 = bf16[8,32,2048]{2,1,0:T(8,128)(2,1)S(1)} collective-permute-done((bf16[8,32,2048]{2,1,0:T(8,128)(2,1)S(1)}, bf16[8,32,2048]{2,1,0:T(8,128)(2,1)S(1)}, u32[]{:S(2)}, u32[]{:S(2)}) %collective-permute-start.19) | collective-permute-done | bytes 1048608 | tf_op jit(solution)/shard_map/ppermute | solution.py:200
  100.3 1.0 collective-permute-start.20
  101.9 2.1 %collective-permute-start.11 = (bf16[8,32,2048]{2,1,0:T(8,128)(2,1)S(1)}, bf16[8,32,2048]{2,1,0:T(8,128)(2,1)}, u32[]{:S(2)}, u32[]{:S(2)}) collective-permute-start(bf16[8,32,2048]{2,1,0:T(8,128)(2,1)S(1)} %collective-permute-done.5), channel_id=1, source_target_pairs={{0,12},{1,97},{2,14},{3,99},{4,0},{5,101},{6,2},{7,103},{8,4},{9,1... | collective-permute-start | bytes 3145736 | tf_op jit(solution)/shard_map/ppermute | solution.py:200
  107.3 15.8 %conditional.3 = ((f32[2048,1024]{1,0:T(8,128)}, f32[1,2048]{1,0:T(1,128)S(1)}, f32[1,1024]{1,0:T(1,128)S(1)})) conditional(s32[]{:T(128)} %bitcast.5, (s32[5]{0:T(128)S(1)}, bf16[8,32,2048]{2,1,0:T(8,128)(2,1)}, bf16[8,32,2048]{2,1,0:T(8,128)(2,1)}, bf16[8,32,2048]{2,1,0:T(8,128)(2,1)}, bf16[8,32,2048]{2,1,0:T(8,128)(2,1)}, ...), branch_computations={%region_0.1_spmd, %region_1.2_spmd} | conditional | flops 8589934592 | bytes 29360136 | solution.py:188
  107.3 15.8 %partial_gram.6 = (f32[2048,1024]{1,0:T(8,128)}, f32[1,2048]{1,0:T(1,128)S(1)}, f32[1,1024]{1,0:T(1,128)S(1)}) custom-call(s32[5]{0:T(128)S(1)} %get-tuple-element.220.refs_0_, bf16[8,32,2048]{2,1,0:T(8,128)(2,1)} %get-tuple-element.221.refs_1_, bf16[8,32,2048]{2,1,0:T(8,128)(2,1)} %get-tuple-element.222.refs_2_, ...), custom_call_target="tpu_custom_call" | custom-call | flops 8589934592 | bytes 29360128 | tf_op jit(solution)/shard_map/cond/branch_0_fun/partial_gram/pallas_call | solution.py:184
  125.0 1.7 %collective-permute-start.25 = (bf16[8,32,2048]{2,1,0:T(8,128)(2,1)}, bf16[8,32,2048]{2,1,0:T(8,128)(2,1)}, u32[]{:S(2)}, u32[]{:S(2)}) collective-permute-start(bf16[8,32,2048]{2,1,0:T(8,128)(2,1)} %collective-permute-done.11), channel_id=1, source_target_pairs={{0,12},{1,97},{2,14},{3,99},{4,0},{5,101},{6,2},{7,103},{8,4},{9,1... | collective-permute-start | bytes 3145736 | tf_op jit(solution)/shard_map/ppermute | solution.py:200
  126.8 1.0 collective-permute-done.24
  127.7 1.5 collective-permute-done.28
  129.2 14.0 %conditional.4 = ((f32[2048,1024]{1,0:T(8,128)}, f32[1,2048]{1,0:T(1,128)S(1)}, f32[1,1024]{1,0:T(1,128)S(1)})) conditional(s32[]{:T(128)} %convert_element_type.10, (s32[5]{0:T(128)S(1)}, bf16[8,32,2048]{2,1,0:T(8,128)(2,1)}, bf16[8,32,2048]{2,1,0:T(8,128)(2,1)}, bf16[8,32,2048]{2,1,0:T(8,128)(2,1)}, bf16[8,32,2048]{2,1,0:T(8,128)(2,1)}, ...), branch_computations={%region_2.3_spmd, %region_3.4_spmd} | conditional | flops 4831838208 | bytes 23855112 | solution.py:188
  129.2 14.0 %partial_gram.8 = (f32[2048,1024]{1,0:T(8,128)}, f32[1,2048]{1,0:T(1,128)S(1)}, f32[1,1024]{1,0:T(1,128)S(1)}) custom-call(s32[5]{0:T(128)S(1)} %get-tuple-element.254.refs_0_, bf16[8,32,2048]{2,1,0:T(8,128)(2,1)} %get-tuple-element.255.refs_1_, bf16[8,32,2048]{2,1,0:T(8,128)(2,1)} %get-tuple-element.256.refs_2_, ...), custom_call_target="tpu_custom_call" | custom-call | flops 4831838208 | bytes 23855104 | tf_op jit(solution)/shard_map/cond/branch_0_fun/partial_gram/pallas_call | solution.py:184
  143.9 2.4 %collective-permute-done.29 = bf16[8,32,2048]{2,1,0:T(8,128)(2,1)S(1)} collective-permute-done((bf16[8,32,2048]{2,1,0:T(8,128)(2,1)}, bf16[8,32,2048]{2,1,0:T(8,128)(2,1)S(1)}, u32[]{:S(2)}, u32[]{:S(2)}) %collective-permute-start.29) | collective-permute-done | bytes 1048608 | tf_op jit(solution)/shard_map/ppermute | solution.py:200
  146.2 1.5 collective-permute-done.30
  147.7 13.5 %conditional.5 = (f32[2048,1024]{1,0:T(8,128)}) conditional(s32[]{:T(128)} %convert_element_type.10, (s32[5]{0:T(128)S(1)}, bf16[8,32,2048]{2,1,0:T(8,128)(2,1)}, bf16[8,32,2048]{2,1,0:T(8,128)(2,1)}, bf16[8,32,2048]{2,1,0:T(8,128)(2,1)}, bf16[8,32,2048]{2,1,0:T(8,128)(2,1)}, /*index=5*/bf16[8,32,2048]{2,1,0:T(8,128)(2,1)S(1)}, ...), branch_computations={%region_4.5_spmd, %region_5.6_spmd} | conditional | flops 3758096384 | bytes 22282248 | solution.py:188
  147.7 13.5 %partial_gram.10 = f32[2048,1024]{1,0:T(8,128)} custom-call(s32[5]{0:T(128)S(1)} %get-tuple-element.286.refs_0_, bf16[8,32,2048]{2,1,0:T(8,128)(2,1)} %get-tuple-element.287.refs_1_, bf16[8,32,2048]{2,1,0:T(8,128)(2,1)} %get-tuple-element.288.refs_2_, bf16[8,32,2048]{2,1,0:T(8,128)(2,1)} %get-tuple-element.289.refs_3_, ...), custom_call_target="tpu_custom_call" | custom-call | flops 3758096384 | bytes 22282240 | tf_op jit(solution)/shard_map/cond/branch_0_fun/partial_gram/pallas_call | solution.py:184
  (66 shorter events, 7.4 us)
Async XLA Ops:
  4.3 21.7 %all-to-all-start = ((bf16[8,32,2048]{2,1,0:T(8,128)(2,1)}), bf16[8,32,2048]{2,1,0:T(8,128)(2,1)S(1)}, u32[]{:S(2)}, u32[]{:S(2)}) async-start(bf16[8,32,2048]{2,1,0:T(8,128)(2,1)} %emphasize.2), calls=%async_computation | async-start | bytes 2097152 | tf_op jit(solution)/shard_map/all_to_all | solution.py:230
  26.0 7.4 %collective-permute-start.4 = (bf16[8,32,2048]{2,1,0:T(8,128)(2,1)}, bf16[8,32,2048]{2,1,0:T(8,128)(2,1)}, u32[]{:S(2)}, u32[]{:S(2)}) collective-permute-start(bf16[8,32,2048]{2,1,0:T(8,128)(2,1)} %emphasize.3), channel_id=1, source_target_pairs={{0,1},{1,0},{2,3},{3,2},{4,5},{5,4},{6,7},{7,6},{8,9},{9,8},{10,11... | collective-permute-start | bytes 3145736 | tf_op jit(solution)/shard_map/ppermute | solution.py:200
  30.7 18.1 %collective-permute-start.1 = (bf16[8,32,2048]{2,1,0:T(8,128)(2,1)S(1)}, bf16[8,32,2048]{2,1,0:T(8,128)(2,1)S(1)}, u32[]{:S(2)}, u32[]{:S(2)}) collective-permute-start(bf16[8,32,2048]{2,1,0:T(8,128)(2,1)S(1)} %all-to-all-done), channel_id=1, source_target_pairs={{0,4},{1,33},{2,6},{3,35},{4,8},{5,37},{6,10},{7,39},{8,12},{9,41}... | collective-permute-start | bytes 3145736 | tf_op jit(solution)/shard_map/ppermute | solution.py:200
  30.7 19.8 %collective-permute-start.14 = (bf16[8,32,2048]{2,1,0:T(8,128)(2,1)S(1)}, bf16[8,32,2048]{2,1,0:T(8,128)(2,1)}, u32[]{:S(2)}, u32[]{:S(2)}) collective-permute-start(bf16[8,32,2048]{2,1,0:T(8,128)(2,1)S(1)} %all-to-all-done), channel_id=1, source_target_pairs={{0,12},{1,97},{2,14},{3,99},{4,0},{5,101},{6,2},{7,103},{8,4},{9,1... | collective-permute-start | bytes 3145736 | tf_op jit(solution)/shard_map/ppermute | solution.py:200
  33.4 23.9 %collective-permute-start = (bf16[8,32,2048]{2,1,0:T(8,128)(2,1)S(1)}, bf16[8,32,2048]{2,1,0:T(8,128)(2,1)S(1)}, u32[]{:S(2)}, u32[]{:S(2)}) collective-permute-start(bf16[8,32,2048]{2,1,0:T(8,128)(2,1)S(1)} %all-to-all-done), channel_id=1, source_target_pairs={{0,2},{1,17},{2,0},{3,19},{4,6},{5,21},{6,4},{7,23},{8,10},{9,25},... | collective-permute-start | bytes 3145736 | tf_op jit(solution)/shard_map/ppermute | solution.py:200
  33.4 30.3 %all-to-all-start.1 = ((bf16[8,32,2048]{2,1,0:T(8,128)(2,1)}), bf16[8,32,2048]{2,1,0:T(8,128)(2,1)}, u32[]{:S(2)}, u32[]{:S(2)}) async-start(bf16[8,32,2048]{2,1,0:T(8,128)(2,1)} %collective-permute-done.4), calls=%async_computation.1 | async-start | bytes 2097152 | tf_op jit(solution)/shard_map/all_to_all | solution.py:230
  37.7 26.0 %collective-permute-start.12 = (bf16[8,32,2048]{2,1,0:T(8,128)(2,1)S(1)}, bf16[8,32,2048]{2,1,0:T(8,128)(2,1)}, u32[]{:S(2)}, u32[]{:S(2)}) collective-permute-start(bf16[8,32,2048]{2,1,0:T(8,128)(2,1)S(1)} %all-to-all-done), channel_id=1, source_target_pairs={{0,1},{1,0},{2,3},{3,2},{4,5},{5,4},{6,7},{7,6},{8,9},{9,8},{10,11... | collective-permute-start | bytes 3145736 | tf_op jit(solution)/shard_map/ppermute | solution.py:200
  48.8 17.7 %collective-permute-start.2 = (bf16[8,32,2048]{2,1,0:T(8,128)(2,1)S(1)}, bf16[8,32,2048]{2,1,0:T(8,128)(2,1)}, u32[]{:S(2)}, u32[]{:S(2)}) collective-permute-start(bf16[8,32,2048]{2,1,0:T(8,128)(2,1)S(1)} %collective-permute-done.1), channel_id=1, source_target_pairs={{0,4},{1,33},{2,6},{3,35},{4,8},{5,37},{6,10},{7,39},{8,12},{9,41}... | collective-permute-start | bytes 3145736 | tf_op jit(solution)/shard_map/ppermute | solution.py:200
  48.8 17.7 %collective-permute-start.21 = (bf16[8,32,2048]{2,1,0:T(8,128)(2,1)S(1)}, bf16[8,32,2048]{2,1,0:T(8,128)(2,1)}, u32[]{:S(2)}, u32[]{:S(2)}) collective-permute-start(bf16[8,32,2048]{2,1,0:T(8,128)(2,1)S(1)} %collective-permute-done.1), channel_id=1, source_target_pairs={{0,1},{1,0},{2,3},{3,2},{4,5},{5,4},{6,7},{7,6},{8,9},{9,8},{10,11... | collective-permute-start | bytes 3145736 | tf_op jit(solution)/shard_map/ppermute | solution.py:200
  50.5 16.1 %collective-permute-start.15 = (bf16[8,32,2048]{2,1,0:T(8,128)(2,1)}, bf16[8,32,2048]{2,1,0:T(8,128)(2,1)}, u32[]{:S(2)}, u32[]{:S(2)}) collective-permute-start(bf16[8,32,2048]{2,1,0:T(8,128)(2,1)} %collective-permute-done.14), channel_id=1, source_target_pairs={{0,1},{1,0},{2,3},{3,2},{4,5},{5,4},{6,7},{7,6},{8,9},{9,8},{10,11... | collective-permute-start | bytes 3145736 | tf_op jit(solution)/shard_map/ppermute | solution.py:200
  63.7 14.2 %collective-permute-start.16 = (bf16[8,32,2048]{2,1,0:T(8,128)(2,1)}, bf16[8,32,2048]{2,1,0:T(8,128)(2,1)S(1)}, u32[]{:S(2)}, u32[]{:S(2)}) collective-permute-start(bf16[8,32,2048]{2,1,0:T(8,128)(2,1)} %all-to-all-done.1), channel_id=1, source_target_pairs={{0,12},{1,97},{2,14},{3,99},{4,0},{5,101},{6,2},{7,103},{8,4},{9,1... | collective-permute-start | bytes 3145736 | tf_op jit(solution)/shard_map/ppermute | solution.py:200
  63.7 25.1 %collective-permute-start.5 = (bf16[8,32,2048]{2,1,0:T(8,128)(2,1)}, bf16[8,32,2048]{2,1,0:T(8,128)(2,1)S(1)}, u32[]{:S(2)}, u32[]{:S(2)}) collective-permute-start(bf16[8,32,2048]{2,1,0:T(8,128)(2,1)} %all-to-all-done.1), channel_id=1, source_target_pairs={{0,2},{1,17},{2,0},{3,19},{4,6},{5,21},{6,4},{7,23},{8,10},{9,25},... | collective-permute-start | bytes 3145736 | tf_op jit(solution)/shard_map/ppermute | solution.py:200
  66.5 22.3 %collective-permute-start.22 = (bf16[8,32,2048]{2,1,0:T(8,128)(2,1)}, bf16[8,32,2048]{2,1,0:T(8,128)(2,1)S(1)}, u32[]{:S(2)}, u32[]{:S(2)}) collective-permute-start(bf16[8,32,2048]{2,1,0:T(8,128)(2,1)} %all-to-all-done.1), channel_id=1, source_target_pairs={{0,4},{1,33},{2,6},{3,35},{4,8},{5,37},{6,10},{7,39},{8,12},{9,41}... | collective-permute-start | bytes 3145736 | tf_op jit(solution)/shard_map/ppermute | solution.py:200
  66.5 26.6 %collective-permute-start.6 = (bf16[8,32,2048]{2,1,0:T(8,128)(2,1)S(1)}, bf16[8,32,2048]{2,1,0:T(8,128)(2,1)S(1)}, u32[]{:S(2)}, u32[]{:S(2)}) collective-permute-start(bf16[8,32,2048]{2,1,0:T(8,128)(2,1)S(1)} %collective-permute-done), channel_id=1, source_target_pairs={{0,4},{1,33},{2,6},{3,35},{4,8},{5,37},{6,10},{7,39},{8,12},{9,41}... | collective-permute-start | bytes 3145736 | tf_op jit(solution)/shard_map/ppermute | solution.py:200
  66.6 28.1 %collective-permute-start.7 = (bf16[8,32,2048]{2,1,0:T(8,128)(2,1)S(1)}, bf16[8,32,2048]{2,1,0:T(8,128)(2,1)S(1)}, u32[]{:S(2)}, u32[]{:S(2)}) collective-permute-start(bf16[8,32,2048]{2,1,0:T(8,128)(2,1)S(1)} %collective-permute-done), channel_id=1, source_target_pairs={{0,12},{1,97},{2,14},{3,99},{4,0},{5,101},{6,2},{7,103},{8,4},{9,1... | collective-permute-start | bytes 3145736 | tf_op jit(solution)/shard_map/ppermute | solution.py:200
  77.8 22.5 %collective-permute-start.19 = (bf16[8,32,2048]{2,1,0:T(8,128)(2,1)S(1)}, bf16[8,32,2048]{2,1,0:T(8,128)(2,1)S(1)}, u32[]{:S(2)}, u32[]{:S(2)}) collective-permute-start(bf16[8,32,2048]{2,1,0:T(8,128)(2,1)S(1)} %collective-permute-done.16), channel_id=1, source_target_pairs={{0,12},{1,97},{2,14},{3,99},{4,0},{5,101},{6,2},{7,103},{8,4},{9,1... | collective-permute-start | bytes 3145736 | tf_op jit(solution)/shard_map/ppermute | solution.py:200
  88.8 12.5 %collective-permute-start.13 = (bf16[8,32,2048]{2,1,0:T(8,128)(2,1)}, bf16[8,32,2048]{2,1,0:T(8,128)(2,1)S(1)}, u32[]{:S(2)}, u32[]{:S(2)}) collective-permute-start(bf16[8,32,2048]{2,1,0:T(8,128)(2,1)} %all-to-all-done.1), channel_id=1, source_target_pairs={{0,1},{1,0},{2,3},{3,2},{4,5},{5,4},{6,7},{7,6},{8,9},{9,8},{10,11... | collective-permute-start | bytes 3145736 | tf_op jit(solution)/shard_map/ppermute | solution.py:200
  88.8 13.1 %collective-permute-start.18 = (bf16[8,32,2048]{2,1,0:T(8,128)(2,1)}, bf16[8,32,2048]{2,1,0:T(8,128)(2,1)S(1)}, u32[]{:S(2)}, u32[]{:S(2)}) collective-permute-start(bf16[8,32,2048]{2,1,0:T(8,128)(2,1)} %collective-permute-done.2), channel_id=1, source_target_pairs={{0,1},{1,0},{2,3},{3,2},{4,5},{5,4},{6,7},{7,6},{8,9},{9,8},{10,11... | collective-permute-start | bytes 3145736 | tf_op jit(solution)/shard_map/ppermute | solution.py:200
  93.1 10.9 %collective-permute-start.17 = (bf16[8,32,2048]{2,1,0:T(8,128)(2,1)S(1)}, bf16[8,32,2048]{2,1,0:T(8,128)(2,1)S(1)}, u32[]{:S(2)}, u32[]{:S(2)}) collective-permute-start(bf16[8,32,2048]{2,1,0:T(8,128)(2,1)S(1)} %collective-permute-done.16), channel_id=1, source_target_pairs={{0,1},{1,0},{2,3},{3,2},{4,5},{5,4},{6,7},{7,6},{8,9},{9,8},{10,11... | collective-permute-start | bytes 3145736 | tf_op jit(solution)/shard_map/ppermute | solution.py:200
  94.7 9.9 %collective-permute-start.23 = (bf16[8,32,2048]{2,1,0:T(8,128)(2,1)S(1)}, bf16[8,32,2048]{2,1,0:T(8,128)(2,1)S(1)}, u32[]{:S(2)}, u32[]{:S(2)}) collective-permute-start(bf16[8,32,2048]{2,1,0:T(8,128)(2,1)S(1)} %collective-permute-done.22), channel_id=1, source_target_pairs={{0,1},{1,0},{2,3},{3,2},{4,5},{5,4},{6,7},{7,6},{8,9},{9,8},{10,11... | collective-permute-start | bytes 3145736 | tf_op jit(solution)/shard_map/ppermute | solution.py:200
  100.3 4.5 %collective-permute-start.20 = (bf16[8,32,2048]{2,1,0:T(8,128)(2,1)S(1)}, bf16[8,32,2048]{2,1,0:T(8,128)(2,1)S(1)}, u32[]{:S(2)}, u32[]{:S(2)}) collective-permute-start(bf16[8,32,2048]{2,1,0:T(8,128)(2,1)S(1)} %collective-permute-done.19), channel_id=1, source_target_pairs={{0,1},{1,0},{2,3},{3,2},{4,5},{5,4},{6,7},{7,6},{8,9},{9,8},{10,11... | collective-permute-start | bytes 3145736 | tf_op jit(solution)/shard_map/ppermute | solution.py:200
  101.3 21.8 %collective-permute-start.10 = (bf16[8,32,2048]{2,1,0:T(8,128)(2,1)S(1)}, bf16[8,32,2048]{2,1,0:T(8,128)(2,1)}, u32[]{:S(2)}, u32[]{:S(2)}) collective-permute-start(bf16[8,32,2048]{2,1,0:T(8,128)(2,1)S(1)} %collective-permute-done.5), channel_id=1, source_target_pairs={{0,4},{1,33},{2,6},{3,35},{4,8},{5,37},{6,10},{7,39},{8,12},{9,41}... | collective-permute-start | bytes 3145736 | tf_op jit(solution)/shard_map/ppermute | solution.py:200
  101.9 21.6 %collective-permute-start.11 = (bf16[8,32,2048]{2,1,0:T(8,128)(2,1)S(1)}, bf16[8,32,2048]{2,1,0:T(8,128)(2,1)}, u32[]{:S(2)}, u32[]{:S(2)}) collective-permute-start(bf16[8,32,2048]{2,1,0:T(8,128)(2,1)S(1)} %collective-permute-done.5), channel_id=1, source_target_pairs={{0,12},{1,97},{2,14},{3,99},{4,0},{5,101},{6,2},{7,103},{8,4},{9,1... | collective-permute-start | bytes 3145736 | tf_op jit(solution)/shard_map/ppermute | solution.py:200
  104.0 19.8 %collective-permute-start.3 = (bf16[8,32,2048]{2,1,0:T(8,128)(2,1)S(1)}, bf16[8,32,2048]{2,1,0:T(8,128)(2,1)}, u32[]{:S(2)}, u32[]{:S(2)}) collective-permute-start(bf16[8,32,2048]{2,1,0:T(8,128)(2,1)S(1)} %collective-permute-done), channel_id=1, source_target_pairs={{0,1},{1,0},{2,3},{3,2},{4,5},{5,4},{6,7},{7,6},{8,9},{9,8},{10,11... | collective-permute-start | bytes 3145736 | tf_op jit(solution)/shard_map/ppermute | solution.py:200
  104.6 19.4 %collective-permute-start.8 = (bf16[8,32,2048]{2,1,0:T(8,128)(2,1)S(1)}, bf16[8,32,2048]{2,1,0:T(8,128)(2,1)}, u32[]{:S(2)}, u32[]{:S(2)}) collective-permute-start(bf16[8,32,2048]{2,1,0:T(8,128)(2,1)S(1)} %collective-permute-done.5), channel_id=1, source_target_pairs={{0,1},{1,0},{2,3},{3,2},{4,5},{5,4},{6,7},{7,6},{8,9},{9,8},{10,11... | collective-permute-start | bytes 3145736 | tf_op jit(solution)/shard_map/ppermute | solution.py:200
  104.8 20.3 %collective-permute-start.27 = (bf16[8,32,2048]{2,1,0:T(8,128)(2,1)S(1)}, bf16[8,32,2048]{2,1,0:T(8,128)(2,1)}, u32[]{:S(2)}, u32[]{:S(2)}) collective-permute-start(bf16[8,32,2048]{2,1,0:T(8,128)(2,1)S(1)} %collective-permute-done.6), channel_id=1, source_target_pairs={{0,1},{1,0},{2,3},{3,2},{4,5},{5,4},{6,7},{7,6},{8,9},{9,8},{10,11... | collective-permute-start | bytes 3145736 | tf_op jit(solution)/shard_map/ppermute | solution.py:200
  123.2 3.6 %collective-permute-start.9 = (bf16[8,32,2048]{2,1,0:T(8,128)(2,1)}, bf16[8,32,2048]{2,1,0:T(8,128)(2,1)}, u32[]{:S(2)}, u32[]{:S(2)}) collective-permute-start(bf16[8,32,2048]{2,1,0:T(8,128)(2,1)} %copy-done), channel_id=1, source_target_pairs={{0,1},{1,0},{2,3},{3,2},{4,5},{5,4},{6,7},{7,6},{8,9},{9,8},{10,11... | collective-permute-start | bytes 3145736 | tf_op jit(solution)/shard_map/ppermute | solution.py:200
  123.5 4.2 %collective-permute-start.24 = (bf16[8,32,2048]{2,1,0:T(8,128)(2,1)}, bf16[8,32,2048]{2,1,0:T(8,128)(2,1)}, u32[]{:S(2)}, u32[]{:S(2)}) collective-permute-start(bf16[8,32,2048]{2,1,0:T(8,128)(2,1)} %collective-permute-done.11), channel_id=1, source_target_pairs={{0,1},{1,0},{2,3},{3,2},{4,5},{5,4},{6,7},{7,6},{8,9},{9,8},{10,11... | collective-permute-start | bytes 3145736 | tf_op jit(solution)/shard_map/ppermute | solution.py:200
  123.8 5.5 %collective-permute-start.28 = (bf16[8,32,2048]{2,1,0:T(8,128)(2,1)}, bf16[8,32,2048]{2,1,0:T(8,128)(2,1)}, u32[]{:S(2)}, u32[]{:S(2)}) collective-permute-start(bf16[8,32,2048]{2,1,0:T(8,128)(2,1)} %collective-permute-done.10), channel_id=1, source_target_pairs={{0,1},{1,0},{2,3},{3,2},{4,5},{5,4},{6,7},{7,6},{8,9},{9,8},{10,11... | collective-permute-start | bytes 3145736 | tf_op jit(solution)/shard_map/ppermute | solution.py:200
  124.1 19.2 %collective-permute-start.26 = (bf16[8,32,2048]{2,1,0:T(8,128)(2,1)S(1)}, bf16[8,32,2048]{2,1,0:T(8,128)(2,1)}, u32[]{:S(2)}, u32[]{:S(2)}) collective-permute-start(bf16[8,32,2048]{2,1,0:T(8,128)(2,1)S(1)} %collective-permute-done.6), channel_id=1, source_target_pairs={{0,4},{1,33},{2,6},{3,35},{4,8},{5,37},{6,10},{7,39},{8,12},{9,41}... | collective-permute-start | bytes 3145736 | tf_op jit(solution)/shard_map/ppermute | solution.py:200
  125.0 18.3 %collective-permute-start.25 = (bf16[8,32,2048]{2,1,0:T(8,128)(2,1)}, bf16[8,32,2048]{2,1,0:T(8,128)(2,1)}, u32[]{:S(2)}, u32[]{:S(2)}) collective-permute-start(bf16[8,32,2048]{2,1,0:T(8,128)(2,1)} %collective-permute-done.11), channel_id=1, source_target_pairs={{0,12},{1,97},{2,14},{3,99},{4,0},{5,101},{6,2},{7,103},{8,4},{9,1... | collective-permute-start | bytes 3145736 | tf_op jit(solution)/shard_map/ppermute | solution.py:200
  143.4 4.4 %collective-permute-start.30 = (bf16[8,32,2048]{2,1,0:T(8,128)(2,1)}, bf16[8,32,2048]{2,1,0:T(8,128)(2,1)S(1)}, u32[]{:S(2)}, u32[]{:S(2)}) collective-permute-start(bf16[8,32,2048]{2,1,0:T(8,128)(2,1)} %collective-permute-done.25), channel_id=1, source_target_pairs={{0,1},{1,0},{2,3},{3,2},{4,5},{5,4},{6,7},{7,6},{8,9},{9,8},{10,11... | collective-permute-start | bytes 3145736 | tf_op jit(solution)/shard_map/ppermute | solution.py:200
  (12 other events, 127.5 us)

commit v5 on v4

--- a/solution.py
+++ b/solution.py
@@ -114,7 +114,7 @@
     blocks = []
     sums = jnp.zeros((8, TILE), jnp.float32)
     for key, (dz, _, _), u in pairs:
-        rows = base[key][((z + dz) & 3) * 2 + u]
+        rows = base[key][u if base[key].shape[0] == 2 else ((z + dz) & 3) * 2 + u]
         blocks.append(rows)
         wide = rows.astype(jnp.float32)
         sums = sums + jnp.sum((wide * wide).reshape(4, 8, -1), axis=0)
@@ -156,13 +156,21 @@
         jax.ShapeDtypeStruct((1, m), jnp.float32),
         jax.ShapeDtypeStruct((1, n), jnp.float32),
     ]
+    base_specs = []
+    for key in base_keys:
+        steps = {pair[1][0] for pair in pairs if pair[0] == key}
+        if len(steps) == 1:
+            index = lambda i, p, dz=min(steps): ((p[0] + dz) & 3, 0, i)
+            base_specs.append(pl.BlockSpec((2, ROWS, TILE), index))
+        else:
+            base_specs.append(pl.BlockSpec((8, ROWS, TILE), lambda i, p: (0, 0, i)))
     depth = len(pairs) * ROWS
     call = pl.pallas_call(
         functools.partial(dot_kernel, pairs, base_keys, inst_keys, first, last, total),
         grid_spec=pltpu.PrefetchScalarGridSpec(
             num_scalar_prefetch=1,
             grid=(m // TILE,),
-            in_specs=[pl.BlockSpec((8, ROWS, TILE), lambda i, p: (0, 0, i))] * len(base_keys)
+            in_specs=base_specs
             + [pl.BlockSpec(memory_space=pl.ANY)] * len(inst_keys)
             + ([] if first else carry_specs),
             out_specs=carry_specs[0] if last else carry_specs,

time: 162 us -> 161 us (level)
  no operation moved by 1% of the time
where the time goes in v5:
time: 161 us; the launch traced here: 160 us
  waiting for transfers between devices  70.3 us (44%)
  Pallas kernels  50.7 us (31%)
  starting transfers between devices  36.8 us (23%)
    ppermute x31, waiting for transfers between devices, send(): lax.ppermute(x, AXES, [(device(*p), device(*target(*p))) for p in places()])  53.7 us
    pallas_call x3, Pallas kernels, run(): call(pos, *[base[k] for k in base_keys], *[inst[k] for k in inst_keys], *...  42.2 us
    ppermute x31, starting transfers between devices, send(): lax.ppermute(x, AXES, [(device(*p), device(*target(*p))) for p in places()])  25.3 us
    all_to_all x2, waiting for transfers between devices, spread(): return lax.all_to_all(x, AXES, 0, 0, axis_index_groups=groups, tiled=True)  16.6 us
    all_to_all x2, starting transfers between devices, spread(): return lax.all_to_all(x, AXES, 0, 0, axis_index_groups=groups, tiled=True)  11.5 us
    pallas_call x2, Pallas kernels, emphasize(): pl.pallas_call(functools.partial(emphasize_kernel, side), out_shape=jax.S...  8.52 us
  transfers between devices with their start and end apart: 33, of which 13 were waited for; matrix products, arithmetic and copies ran while one was open for 0% of the time, Pallas kernels for 21%

profile of v5, /device:TPU:1, one launch (start us, length us, event | category | flops | bytes accessed | tf_op | source)
XLA Modules:
  0.0 160.3 jit_solution(16699086495686791050)
XLA Ops:
  0.0 4.3 %emphasize.2 = bf16[8,32,2048]{2,1,0:T(8,128)(2,1)} custom-call(bf16[32,16384]{1,0:T(8,128)(2,1)} %base_ref.2, bf16[32,16384]{1,0:T(8,128)(2,1)} %inst_ref.2, s32[32,128]{1,0:T(8,128)} %base_sup_ref.2, s32[32,128]{1,0:T(8,128)} %inst_sup_ref.2), custom_call_target="tpu_custom_call" | custom-call | flops 1073741824 | bytes 4194304 | tf_op jit(solution)/shard_map/emphasize/pallas_call | solution.py:65
  4.3 7.2 %all-to-all-start = ((bf16[8,32,2048]{2,1,0:T(8,128)(2,1)}), bf16[8,32,2048]{2,1,0:T(8,128)(2,1)S(1)}, u32[]{:S(2)}, u32[]{:S(2)}) async-start(bf16[8,32,2048]{2,1,0:T(8,128)(2,1)} %emphasize.2), calls=%async_computation | async-start | bytes 2097152 | tf_op jit(solution)/shard_map/all_to_all | solution.py:238
  11.5 4.3 %emphasize.3 = bf16[8,32,2048]{2,1,0:T(8,128)(2,1)} custom-call(bf16[32,16384]{1,0:T(8,128)(2,1)} %base_ref.2, bf16[32,16384]{1,0:T(8,128)(2,1)} %inst_ref.2, s32[32,128]{1,0:T(8,128)} %base_sup_ref.2, s32[32,128]{1,0:T(8,128)} %inst_sup_ref.2), custom_call_target="tpu_custom_call" | custom-call | flops 1073741824 | bytes 4194304 | tf_op jit(solution)/shard_map/emphasize/pallas_call | solution.py:65
  15.8 10.2 %all-to-all-done = bf16[8,32,2048]{2,1,0:T(8,128)(2,1)S(1)} async-done(((bf16[8,32,2048]{2,1,0:T(8,128)(2,1)}), bf16[8,32,2048]{2,1,0:T(8,128)(2,1)S(1)}, u32[]{:S(2)}, u32[]{:S(2)}) %all-to-all-start) | async-done | bytes 1048608 | tf_op jit(solution)/shard_map/all_to_all | solution.py:238
  26.0 4.7 %collective-permute-start.4 = (bf16[8,32,2048]{2,1,0:T(8,128)(2,1)}, bf16[8,32,2048]{2,1,0:T(8,128)(2,1)}, u32[]{:S(2)}, u32[]{:S(2)}) collective-permute-start(bf16[8,32,2048]{2,1,0:T(8,128)(2,1)} %emphasize.3), channel_id=1, source_target_pairs={{0,1},{1,0},{2,3},{3,2},{4,5},{5,4},{6,7},{7,6},{8,9},{9,8},{10,11... | collective-permute-start | bytes 3145736 | tf_op jit(solution)/shard_map/ppermute | solution.py:208
  30.7 2.7 %collective-permute-start.14 = (bf16[8,32,2048]{2,1,0:T(8,128)(2,1)S(1)}, bf16[8,32,2048]{2,1,0:T(8,128)(2,1)}, u32[]{:S(2)}, u32[]{:S(2)}) collective-permute-start(bf16[8,32,2048]{2,1,0:T(8,128)(2,1)S(1)} %all-to-all-done), channel_id=1, source_target_pairs={{0,12},{1,97},{2,14},{3,99},{4,0},{5,101},{6,2},{7,103},{8,4},{9,1... | collective-permute-start | bytes 3145736 | tf_op jit(solution)/shard_map/ppermute | solution.py:208
  33.4 4.3 %all-to-all-start.1 = ((bf16[8,32,2048]{2,1,0:T(8,128)(2,1)}), bf16[8,32,2048]{2,1,0:T(8,128)(2,1)}, u32[]{:S(2)}, u32[]{:S(2)}) async-start(bf16[8,32,2048]{2,1,0:T(8,128)(2,1)} %collective-permute-done.4), calls=%async_computation.1 | async-start | bytes 2097152 | tf_op jit(solution)/shard_map/all_to_all | solution.py:238
  38.5 10.3 %collective-permute-done.1 = bf16[8,32,2048]{2,1,0:T(8,128)(2,1)S(1)} collective-permute-done((bf16[8,32,2048]{2,1,0:T(8,128)(2,1)S(1)}, bf16[8,32,2048]{2,1,0:T(8,128)(2,1)S(1)}, u32[]{:S(2)}, u32[]{:S(2)}) %collective-permute-start.1) | collective-permute-done | bytes 1048608 | tf_op jit(solution)/shard_map/ppermute | solution.py:208
  48.8 1.7 %collective-permute-start.21 = (bf16[8,32,2048]{2,1,0:T(8,128)(2,1)S(1)}, bf16[8,32,2048]{2,1,0:T(8,128)(2,1)}, u32[]{:S(2)}, u32[]{:S(2)}) collective-permute-start(bf16[8,32,2048]{2,1,0:T(8,128)(2,1)S(1)} %collective-permute-done.1), channel_id=1, source_target_pairs={{0,1},{1,0},{2,3},{3,2},{4,5},{5,4},{6,7},{7,6},{8,9},{9,8},{10,11... | collective-permute-start | bytes 3145736 | tf_op jit(solution)/shard_map/ppermute | solution.py:208
  50.5 6.7 %collective-permute-done = bf16[8,32,2048]{2,1,0:T(8,128)(2,1)S(1)} collective-permute-done((bf16[8,32,2048]{2,1,0:T(8,128)(2,1)S(1)}, bf16[8,32,2048]{2,1,0:T(8,128)(2,1)S(1)}, u32[]{:S(2)}, u32[]{:S(2)}) %collective-permute-start) | collective-permute-done | bytes 1048608 | tf_op jit(solution)/shard_map/ppermute | solution.py:208
  57.3 6.4 %all-to-all-done.1 = bf16[8,32,2048]{2,1,0:T(8,128)(2,1)} async-done(((bf16[8,32,2048]{2,1,0:T(8,128)(2,1)}), bf16[8,32,2048]{2,1,0:T(8,128)(2,1)}, u32[]{:S(2)}, u32[]{:S(2)}) %all-to-all-start.1) | async-done | bytes 1048608 | tf_op jit(solution)/shard_map/all_to_all | solution.py:238
  63.8 2.7 %collective-permute-done.2 = bf16[8,32,2048]{2,1,0:T(8,128)(2,1)} collective-permute-done((bf16[8,32,2048]{2,1,0:T(8,128)(2,1)S(1)}, bf16[8,32,2048]{2,1,0:T(8,128)(2,1)}, u32[]{:S(2)}, u32[]{:S(2)}) %collective-permute-start.2) | collective-permute-done | bytes 1048608 | tf_op jit(solution)/shard_map/ppermute | solution.py:208
  66.6 2.7 %collective-permute-start.7 = (bf16[8,32,2048]{2,1,0:T(8,128)(2,1)S(1)}, bf16[8,32,2048]{2,1,0:T(8,128)(2,1)S(1)}, u32[]{:S(2)}, u32[]{:S(2)}) collective-permute-start(bf16[8,32,2048]{2,1,0:T(8,128)(2,1)S(1)} %collective-permute-done), channel_id=1, source_target_pairs={{0,12},{1,97},{2,14},{3,99},{4,0},{5,101},{6,2},{7,103},{8,4},{9,1... | collective-permute-start | bytes 3145736 | tf_op jit(solution)/shard_map/ppermute | solution.py:208
  69.3 8.6 %collective-permute-done.16 = bf16[8,32,2048]{2,1,0:T(8,128)(2,1)S(1)} collective-permute-done((bf16[8,32,2048]{2,1,0:T(8,128)(2,1)}, bf16[8,32,2048]{2,1,0:T(8,128)(2,1)S(1)}, u32[]{:S(2)}, u32[]{:S(2)}) %collective-permute-start.16) | collective-permute-done | bytes 1048608 | tf_op jit(solution)/shard_map/ppermute | solution.py:208
  77.8 1.2 collective-permute-start.19
  79.0 9.8 %collective-permute-done.5 = bf16[8,32,2048]{2,1,0:T(8,128)(2,1)S(1)} collective-permute-done((bf16[8,32,2048]{2,1,0:T(8,128)(2,1)}, bf16[8,32,2048]{2,1,0:T(8,128)(2,1)S(1)}, u32[]{:S(2)}, u32[]{:S(2)}) %collective-permute-start.5) | collective-permute-done | bytes 1048608 | tf_op jit(solution)/shard_map/ppermute | solution.py:208
  89.3 3.8 %collective-permute-done.6 = bf16[8,32,2048]{2,1,0:T(8,128)(2,1)S(1)} collective-permute-done((bf16[8,32,2048]{2,1,0:T(8,128)(2,1)S(1)}, bf16[8,32,2048]{2,1,0:T(8,128)(2,1)S(1)}, u32[]{:S(2)}, u32[]{:S(2)}) %collective-permute-start.6) | collective-permute-done | bytes 1048608 | tf_op jit(solution)/shard_map/ppermute | solution.py:208
  93.1 1.6 %collective-permute-start.17 = (bf16[8,32,2048]{2,1,0:T(8,128)(2,1)S(1)}, bf16[8,32,2048]{2,1,0:T(8,128)(2,1)S(1)}, u32[]{:S(2)}, u32[]{:S(2)}) collective-permute-start(bf16[8,32,2048]{2,1,0:T(8,128)(2,1)S(1)} %collective-permute-done.16), channel_id=1, source_target_pairs={{0,1},{1,0},{2,3},{3,2},{4,5},{5,4},{6,7},{7,6},{8,9},{9,8},{10,11... | collective-permute-start | bytes 3145736 | tf_op jit(solution)/shard_map/ppermute | solution.py:208
  94.8 5.5 %collective-permute-done.19 = bf16[8,32,2048]{2,1,0:T(8,128)(2,1)S(1)} collective-permute-done((bf16[8,32,2048]{2,1,0:T(8,128)(2,1)S(1)}, bf16[8,32,2048]{2,1,0:T(8,128)(2,1)S(1)}, u32[]{:S(2)}, u32[]{:S(2)}) %collective-permute-start.19) | collective-permute-done | bytes 1048608 | tf_op jit(solution)/shard_map/ppermute | solution.py:208
  100.3 1.0 collective-permute-start.20
  101.9 2.1 %collective-permute-start.11 = (bf16[8,32,2048]{2,1,0:T(8,128)(2,1)S(1)}, bf16[8,32,2048]{2,1,0:T(8,128)(2,1)}, u32[]{:S(2)}, u32[]{:S(2)}) collective-permute-start(bf16[8,32,2048]{2,1,0:T(8,128)(2,1)S(1)} %collective-permute-done.5), channel_id=1, source_target_pairs={{0,12},{1,97},{2,14},{3,99},{4,0},{5,101},{6,2},{7,103},{8,4},{9,1... | collective-permute-start | bytes 3145736 | tf_op jit(solution)/shard_map/ppermute | solution.py:208
  107.3 15.8 %conditional.3 = ((f32[2048,1024]{1,0:T(8,128)}, f32[1,2048]{1,0:T(1,128)S(1)}, f32[1,1024]{1,0:T(1,128)S(1)})) conditional(s32[]{:T(128)} %bitcast.5, (s32[5]{0:T(128)S(1)}, bf16[8,32,2048]{2,1,0:T(8,128)(2,1)}, bf16[8,32,2048]{2,1,0:T(8,128)(2,1)}, bf16[8,32,2048]{2,1,0:T(8,128)(2,1)}, bf16[8,32,2048]{2,1,0:T(8,128)(2,1)}, ...), branch_computations={%region_0.1_spmd, %region_1.2_spmd} | conditional | flops 8589934592 | bytes 29360136 | solution.py:196
  107.3 15.8 %partial_gram.6 = (f32[2048,1024]{1,0:T(8,128)}, f32[1,2048]{1,0:T(1,128)S(1)}, f32[1,1024]{1,0:T(1,128)S(1)}) custom-call(s32[5]{0:T(128)S(1)} %get-tuple-element.220.refs_0_, bf16[8,32,2048]{2,1,0:T(8,128)(2,1)} %get-tuple-element.221.refs_1_, bf16[8,32,2048]{2,1,0:T(8,128)(2,1)} %get-tuple-element.222.refs_2_, ...), custom_call_target="tpu_custom_call" | custom-call | flops 8589934592 | bytes 29360128 | tf_op jit(solution)/shard_map/cond/branch_0_fun/partial_gram/pallas_call | solution.py:192
  125.0 1.7 %collective-permute-start.25 = (bf16[8,32,2048]{2,1,0:T(8,128)(2,1)}, bf16[8,32,2048]{2,1,0:T(8,128)(2,1)}, u32[]{:S(2)}, u32[]{:S(2)}) collective-permute-start(bf16[8,32,2048]{2,1,0:T(8,128)(2,1)} %collective-permute-done.11), channel_id=1, source_target_pairs={{0,12},{1,97},{2,14},{3,99},{4,0},{5,101},{6,2},{7,103},{8,4},{9,1... | collective-permute-start | bytes 3145736 | tf_op jit(solution)/shard_map/ppermute | solution.py:208
  126.8 1.0 collective-permute-done.24
  127.7 1.5 collective-permute-done.28
  129.2 14.0 %conditional.4 = ((f32[2048,1024]{1,0:T(8,128)}, f32[1,2048]{1,0:T(1,128)S(1)}, f32[1,1024]{1,0:T(1,128)S(1)})) conditional(s32[]{:T(128)} %convert_element_type.10, (s32[5]{0:T(128)S(1)}, bf16[8,32,2048]{2,1,0:T(8,128)(2,1)}, bf16[8,32,2048]{2,1,0:T(8,128)(2,1)}, bf16[8,32,2048]{2,1,0:T(8,128)(2,1)}, bf16[8,32,2048]{2,1,0:T(8,128)(2,1)}, ...), branch_computations={%region_2.3_spmd, %region_3.4_spmd} | conditional | flops 4831838208 | bytes 23855112 | solution.py:196
  129.2 14.0 %partial_gram.8 = (f32[2048,1024]{1,0:T(8,128)}, f32[1,2048]{1,0:T(1,128)S(1)}, f32[1,1024]{1,0:T(1,128)S(1)}) custom-call(s32[5]{0:T(128)S(1)} %get-tuple-element.254.refs_0_, bf16[8,32,2048]{2,1,0:T(8,128)(2,1)} %get-tuple-element.255.refs_1_, bf16[8,32,2048]{2,1,0:T(8,128)(2,1)} %get-tuple-element.256.refs_2_, ...), custom_call_target="tpu_custom_call" | custom-call | flops 4831838208 | bytes 23855104 | tf_op jit(solution)/shard_map/cond/branch_0_fun/partial_gram/pallas_call | solution.py:192
  143.9 2.4 %collective-permute-done.29 = bf16[8,32,2048]{2,1,0:T(8,128)(2,1)S(1)} collective-permute-done((bf16[8,32,2048]{2,1,0:T(8,128)(2,1)}, bf16[8,32,2048]{2,1,0:T(8,128)(2,1)S(1)}, u32[]{:S(2)}, u32[]{:S(2)}) %collective-permute-start.29) | collective-permute-done | bytes 1048608 | tf_op jit(solution)/shard_map/ppermute | solution.py:208
  146.2 1.5 collective-permute-done.30
  147.7 12.3 %conditional.5 = (f32[2048,1024]{1,0:T(8,128)}) conditional(s32[]{:T(128)} %convert_element_type.10, (s32[5]{0:T(128)S(1)}, bf16[8,32,2048]{2,1,0:T(8,128)(2,1)}, bf16[8,32,2048]{2,1,0:T(8,128)(2,1)}, bf16[8,32,2048]{2,1,0:T(8,128)(2,1)}, bf16[8,32,2048]{2,1,0:T(8,128)(2,1)}, /*index=5*/bf16[8,32,2048]{2,1,0:T(8,128)(2,1)S(1)}, ...), branch_computations={%region_4.5_spmd, %region_5.6_spmd} | conditional | flops 3758096384 | bytes 22282248 | solution.py:196
  147.7 12.3 %partial_gram.10 = f32[2048,1024]{1,0:T(8,128)} custom-call(s32[5]{0:T(128)S(1)} %get-tuple-element.286.refs_0_, bf16[8,32,2048]{2,1,0:T(8,128)(2,1)} %get-tuple-element.287.refs_1_, bf16[8,32,2048]{2,1,0:T(8,128)(2,1)} %get-tuple-element.288.refs_2_, bf16[8,32,2048]{2,1,0:T(8,128)(2,1)} %get-tuple-element.289.refs_3_, ...), custom_call_target="tpu_custom_call" | custom-call | flops 3758096384 | bytes 22282240 | tf_op jit(solution)/shard_map/cond/branch_0_fun/partial_gram/pallas_call | solution.py:192
  (66 shorter events, 7.4 us)
Async XLA Ops:
  4.3 21.7 %all-to-all-start = ((bf16[8,32,2048]{2,1,0:T(8,128)(2,1)}), bf16[8,32,2048]{2,1,0:T(8,128)(2,1)S(1)}, u32[]{:S(2)}, u32[]{:S(2)}) async-start(bf16[8,32,2048]{2,1,0:T(8,128)(2,1)} %emphasize.2), calls=%async_computation | async-start | bytes 2097152 | tf_op jit(solution)/shard_map/all_to_all | solution.py:238
  26.0 7.4 %collective-permute-start.4 = (bf16[8,32,2048]{2,1,0:T(8,128)(2,1)}, bf16[8,32,2048]{2,1,0:T(8,128)(2,1)}, u32[]{:S(2)}, u32[]{:S(2)}) collective-permute-start(bf16[8,32,2048]{2,1,0:T(8,128)(2,1)} %emphasize.3), channel_id=1, source_target_pairs={{0,1},{1,0},{2,3},{3,2},{4,5},{5,4},{6,7},{7,6},{8,9},{9,8},{10,11... | collective-permute-start | bytes 3145736 | tf_op jit(solution)/shard_map/ppermute | solution.py:208
  30.7 18.1 %collective-permute-start.1 = (bf16[8,32,2048]{2,1,0:T(8,128)(2,1)S(1)}, bf16[8,32,2048]{2,1,0:T(8,128)(2,1)S(1)}, u32[]{:S(2)}, u32[]{:S(2)}) collective-permute-start(bf16[8,32,2048]{2,1,0:T(8,128)(2,1)S(1)} %all-to-all-done), channel_id=1, source_target_pairs={{0,4},{1,33},{2,6},{3,35},{4,8},{5,37},{6,10},{7,39},{8,12},{9,41}... | collective-permute-start | bytes 3145736 | tf_op jit(solution)/shard_map/ppermute | solution.py:208
  30.7 19.8 %collective-permute-start.14 = (bf16[8,32,2048]{2,1,0:T(8,128)(2,1)S(1)}, bf16[8,32,2048]{2,1,0:T(8,128)(2,1)}, u32[]{:S(2)}, u32[]{:S(2)}) collective-permute-start(bf16[8,32,2048]{2,1,0:T(8,128)(2,1)S(1)} %all-to-all-done), channel_id=1, source_target_pairs={{0,12},{1,97},{2,14},{3,99},{4,0},{5,101},{6,2},{7,103},{8,4},{9,1... | collective-permute-start | bytes 3145736 | tf_op jit(solution)/shard_map/ppermute | solution.py:208
  33.4 23.9 %collective-permute-start = (bf16[8,32,2048]{2,1,0:T(8,128)(2,1)S(1)}, bf16[8,32,2048]{2,1,0:T(8,128)(2,1)S(1)}, u32[]{:S(2)}, u32[]{:S(2)}) collective-permute-start(bf16[8,32,2048]{2,1,0:T(8,128)(2,1)S(1)} %all-to-all-done), channel_id=1, source_target_pairs={{0,2},{1,17},{2,0},{3,19},{4,6},{5,21},{6,4},{7,23},{8,10},{9,25},... | collective-permute-start | bytes 3145736 | tf_op jit(solution)/shard_map/ppermute | solution.py:208
  33.4 30.3 %all-to-all-start.1 = ((bf16[8,32,2048]{2,1,0:T(8,128)(2,1)}), bf16[8,32,2048]{2,1,0:T(8,128)(2,1)}, u32[]{:S(2)}, u32[]{:S(2)}) async-start(bf16[8,32,2048]{2,1,0:T(8,128)(2,1)} %collective-permute-done.4), calls=%async_computation.1 | async-start | bytes 2097152 | tf_op jit(solution)/shard_map/all_to_all | solution.py:238
  37.7 26.0 %collective-permute-start.12 = (bf16[8,32,2048]{2,1,0:T(8,128)(2,1)S(1)}, bf16[8,32,2048]{2,1,0:T(8,128)(2,1)}, u32[]{:S(2)}, u32[]{:S(2)}) collective-permute-start(bf16[8,32,2048]{2,1,0:T(8,128)(2,1)S(1)} %all-to-all-done), channel_id=1, source_target_pairs={{0,1},{1,0},{2,3},{3,2},{4,5},{5,4},{6,7},{7,6},{8,9},{9,8},{10,11... | collective-permute-start | bytes 3145736 | tf_op jit(solution)/shard_map/ppermute | solution.py:208
  48.8 17.7 %collective-permute-start.2 = (bf16[8,32,2048]{2,1,0:T(8,128)(2,1)S(1)}, bf16[8,32,2048]{2,1,0:T(8,128)(2,1)}, u32[]{:S(2)}, u32[]{:S(2)}) collective-permute-start(bf16[8,32,2048]{2,1,0:T(8,128)(2,1)S(1)} %collective-permute-done.1), channel_id=1, source_target_pairs={{0,4},{1,33},{2,6},{3,35},{4,8},{5,37},{6,10},{7,39},{8,12},{9,41}... | collective-permute-start | bytes 3145736 | tf_op jit(solution)/shard_map/ppermute | solution.py:208
  48.8 17.7 %collective-permute-start.21 = (bf16[8,32,2048]{2,1,0:T(8,128)(2,1)S(1)}, bf16[8,32,2048]{2,1,0:T(8,128)(2,1)}, u32[]{:S(2)}, u32[]{:S(2)}) collective-permute-start(bf16[8,32,2048]{2,1,0:T(8,128)(2,1)S(1)} %collective-permute-done.1), channel_id=1, source_target_pairs={{0,1},{1,0},{2,3},{3,2},{4,5},{5,4},{6,7},{7,6},{8,9},{9,8},{10,11... | collective-permute-start | bytes 3145736 | tf_op jit(solution)/shard_map/ppermute | solution.py:208
  50.5 16.1 %collective-permute-start.15 = (bf16[8,32,2048]{2,1,0:T(8,128)(2,1)}, bf16[8,32,2048]{2,1,0:T(8,128)(2,1)}, u32[]{:S(2)}, u32[]{:S(2)}) collective-permute-start(bf16[8,32,2048]{2,1,0:T(8,128)(2,1)} %collective-permute-done.14), channel_id=1, source_target_pairs={{0,1},{1,0},{2,3},{3,2},{4,5},{5,4},{6,7},{7,6},{8,9},{9,8},{10,11... | collective-permute-start | bytes 3145736 | tf_op jit(solution)/shard_map/ppermute | solution.py:208
  63.7 14.2 %collective-permute-start.16 = (bf16[8,32,2048]{2,1,0:T(8,128)(2,1)}, bf16[8,32,2048]{2,1,0:T(8,128)(2,1)S(1)}, u32[]{:S(2)}, u32[]{:S(2)}) collective-permute-start(bf16[8,32,2048]{2,1,0:T(8,128)(2,1)} %all-to-all-done.1), channel_id=1, source_target_pairs={{0,12},{1,97},{2,14},{3,99},{4,0},{5,101},{6,2},{7,103},{8,4},{9,1... | collective-permute-start | bytes 3145736 | tf_op jit(solution)/shard_map/ppermute | solution.py:208
  63.7 25.1 %collective-permute-start.5 = (bf16[8,32,2048]{2,1,0:T(8,128)(2,1)}, bf16[8,32,2048]{2,1,0:T(8,128)(2,1)S(1)}, u32[]{:S(2)}, u32[]{:S(2)}) collective-permute-start(bf16[8,32,2048]{2,1,0:T(8,128)(2,1)} %all-to-all-done.1), channel_id=1, source_target_pairs={{0,2},{1,17},{2,0},{3,19},{4,6},{5,21},{6,4},{7,23},{8,10},{9,25},... | collective-permute-start | bytes 3145736 | tf_op jit(solution)/shard_map/ppermute | solution.py:208
  66.5 22.3 %collective-permute-start.22 = (bf16[8,32,2048]{2,1,0:T(8,128)(2,1)}, bf16[8,32,2048]{2,1,0:T(8,128)(2,1)S(1)}, u32[]{:S(2)}, u32[]{:S(2)}) collective-permute-start(bf16[8,32,2048]{2,1,0:T(8,128)(2,1)} %all-to-all-done.1), channel_id=1, source_target_pairs={{0,4},{1,33},{2,6},{3,35},{4,8},{5,37},{6,10},{7,39},{8,12},{9,41}... | collective-permute-start | bytes 3145736 | tf_op jit(solution)/shard_map/ppermute | solution.py:208
  66.5 26.6 %collective-permute-start.6 = (bf16[8,32,2048]{2,1,0:T(8,128)(2,1)S(1)}, bf16[8,32,2048]{2,1,0:T(8,128)(2,1)S(1)}, u32[]{:S(2)}, u32[]{:S(2)}) collective-permute-start(bf16[8,32,2048]{2,1,0:T(8,128)(2,1)S(1)} %collective-permute-done), channel_id=1, source_target_pairs={{0,4},{1,33},{2,6},{3,35},{4,8},{5,37},{6,10},{7,39},{8,12},{9,41}... | collective-permute-start | bytes 3145736 | tf_op jit(solution)/shard_map/ppermute | solution.py:208
  66.6 28.1 %collective-permute-start.7 = (bf16[8,32,2048]{2,1,0:T(8,128)(2,1)S(1)}, bf16[8,32,2048]{2,1,0:T(8,128)(2,1)S(1)}, u32[]{:S(2)}, u32[]{:S(2)}) collective-permute-start(bf16[8,32,2048]{2,1,0:T(8,128)(2,1)S(1)} %collective-permute-done), channel_id=1, source_target_pairs={{0,12},{1,97},{2,14},{3,99},{4,0},{5,101},{6,2},{7,103},{8,4},{9,1... | collective-permute-start | bytes 3145736 | tf_op jit(solution)/shard_map/ppermute | solution.py:208
  77.8 22.5 %collective-permute-start.19 = (bf16[8,32,2048]{2,1,0:T(8,128)(2,1)S(1)}, bf16[8,32,2048]{2,1,0:T(8,128)(2,1)S(1)}, u32[]{:S(2)}, u32[]{:S(2)}) collective-permute-start(bf16[8,32,2048]{2,1,0:T(8,128)(2,1)S(1)} %collective-permute-done.16), channel_id=1, source_target_pairs={{0,12},{1,97},{2,14},{3,99},{4,0},{5,101},{6,2},{7,103},{8,4},{9,1... | collective-permute-start | bytes 3145736 | tf_op jit(solution)/shard_map/ppermute | solution.py:208
  88.8 12.5 %collective-permute-start.13 = (bf16[8,32,2048]{2,1,0:T(8,128)(2,1)}, bf16[8,32,2048]{2,1,0:T(8,128)(2,1)S(1)}, u32[]{:S(2)}, u32[]{:S(2)}) collective-permute-start(bf16[8,32,2048]{2,1,0:T(8,128)(2,1)} %all-to-all-done.1), channel_id=1, source_target_pairs={{0,1},{1,0},{2,3},{3,2},{4,5},{5,4},{6,7},{7,6},{8,9},{9,8},{10,11... | collective-permute-start | bytes 3145736 | tf_op jit(solution)/shard_map/ppermute | solution.py:208
  88.8 13.1 %collective-permute-start.18 = (bf16[8,32,2048]{2,1,0:T(8,128)(2,1)}, bf16[8,32,2048]{2,1,0:T(8,128)(2,1)S(1)}, u32[]{:S(2)}, u32[]{:S(2)}) collective-permute-start(bf16[8,32,2048]{2,1,0:T(8,128)(2,1)} %collective-permute-done.2), channel_id=1, source_target_pairs={{0,1},{1,0},{2,3},{3,2},{4,5},{5,4},{6,7},{7,6},{8,9},{9,8},{10,11... | collective-permute-start | bytes 3145736 | tf_op jit(solution)/shard_map/ppermute | solution.py:208
  93.1 10.9 %collective-permute-start.17 = (bf16[8,32,2048]{2,1,0:T(8,128)(2,1)S(1)}, bf16[8,32,2048]{2,1,0:T(8,128)(2,1)S(1)}, u32[]{:S(2)}, u32[]{:S(2)}) collective-permute-start(bf16[8,32,2048]{2,1,0:T(8,128)(2,1)S(1)} %collective-permute-done.16), channel_id=1, source_target_pairs={{0,1},{1,0},{2,3},{3,2},{4,5},{5,4},{6,7},{7,6},{8,9},{9,8},{10,11... | collective-permute-start | bytes 3145736 | tf_op jit(solution)/shard_map/ppermute | solution.py:208
  94.7 9.9 %collective-permute-start.23 = (bf16[8,32,2048]{2,1,0:T(8,128)(2,1)S(1)}, bf16[8,32,2048]{2,1,0:T(8,128)(2,1)S(1)}, u32[]{:S(2)}, u32[]{:S(2)}) collective-permute-start(bf16[8,32,2048]{2,1,0:T(8,128)(2,1)S(1)} %collective-permute-done.22), channel_id=1, source_target_pairs={{0,1},{1,0},{2,3},{3,2},{4,5},{5,4},{6,7},{7,6},{8,9},{9,8},{10,11... | collective-permute-start | bytes 3145736 | tf_op jit(solution)/shard_map/ppermute | solution.py:208
  100.3 4.5 %collective-permute-start.20 = (bf16[8,32,2048]{2,1,0:T(8,128)(2,1)S(1)}, bf16[8,32,2048]{2,1,0:T(8,128)(2,1)S(1)}, u32[]{:S(2)}, u32[]{:S(2)}) collective-permute-start(bf16[8,32,2048]{2,1,0:T(8,128)(2,1)S(1)} %collective-permute-done.19), channel_id=1, source_target_pairs={{0,1},{1,0},{2,3},{3,2},{4,5},{5,4},{6,7},{7,6},{8,9},{9,8},{10,11... | collective-permute-start | bytes 3145736 | tf_op jit(solution)/shard_map/ppermute | solution.py:208
  101.3 21.8 %collective-permute-start.10 = (bf16[8,32,2048]{2,1,0:T(8,128)(2,1)S(1)}, bf16[8,32,2048]{2,1,0:T(8,128)(2,1)}, u32[]{:S(2)}, u32[]{:S(2)}) collective-permute-start(bf16[8,32,2048]{2,1,0:T(8,128)(2,1)S(1)} %collective-permute-done.5), channel_id=1, source_target_pairs={{0,4},{1,33},{2,6},{3,35},{4,8},{5,37},{6,10},{7,39},{8,12},{9,41}... | collective-permute-start | bytes 3145736 | tf_op jit(solution)/shard_map/ppermute | solution.py:208
  101.9 21.6 %collective-permute-start.11 = (bf16[8,32,2048]{2,1,0:T(8,128)(2,1)S(1)}, bf16[8,32,2048]{2,1,0:T(8,128)(2,1)}, u32[]{:S(2)}, u32[]{:S(2)}) collective-permute-start(bf16[8,32,2048]{2,1,0:T(8,128)(2,1)S(1)} %collective-permute-done.5), channel_id=1, source_target_pairs={{0,12},{1,97},{2,14},{3,99},{4,0},{5,101},{6,2},{7,103},{8,4},{9,1... | collective-permute-start | bytes 3145736 | tf_op jit(solution)/shard_map/ppermute | solution.py:208
  104.0 19.8 %collective-permute-start.3 = (bf16[8,32,2048]{2,1,0:T(8,128)(2,1)S(1)}, bf16[8,32,2048]{2,1,0:T(8,128)(2,1)}, u32[]{:S(2)}, u32[]{:S(2)}) collective-permute-start(bf16[8,32,2048]{2,1,0:T(8,128)(2,1)S(1)} %collective-permute-done), channel_id=1, source_target_pairs={{0,1},{1,0},{2,3},{3,2},{4,5},{5,4},{6,7},{7,6},{8,9},{9,8},{10,11... | collective-permute-start | bytes 3145736 | tf_op jit(solution)/shard_map/ppermute | solution.py:208
  104.6 19.4 %collective-permute-start.8 = (bf16[8,32,2048]{2,1,0:T(8,128)(2,1)S(1)}, bf16[8,32,2048]{2,1,0:T(8,128)(2,1)}, u32[]{:S(2)}, u32[]{:S(2)}) collective-permute-start(bf16[8,32,2048]{2,1,0:T(8,128)(2,1)S(1)} %collective-permute-done.5), channel_id=1, source_target_pairs={{0,1},{1,0},{2,3},{3,2},{4,5},{5,4},{6,7},{7,6},{8,9},{9,8},{10,11... | collective-permute-start | bytes 3145736 | tf_op jit(solution)/shard_map/ppermute | solution.py:208
  104.8 20.3 %collective-permute-start.27 = (bf16[8,32,2048]{2,1,0:T(8,128)(2,1)S(1)}, bf16[8,32,2048]{2,1,0:T(8,128)(2,1)}, u32[]{:S(2)}, u32[]{:S(2)}) collective-permute-start(bf16[8,32,2048]{2,1,0:T(8,128)(2,1)S(1)} %collective-permute-done.6), channel_id=1, source_target_pairs={{0,1},{1,0},{2,3},{3,2},{4,5},{5,4},{6,7},{7,6},{8,9},{9,8},{10,11... | collective-permute-start | bytes 3145736 | tf_op jit(solution)/shard_map/ppermute | solution.py:208
  123.2 3.6 %collective-permute-start.9 = (bf16[8,32,2048]{2,1,0:T(8,128)(2,1)}, bf16[8,32,2048]{2,1,0:T(8,128)(2,1)}, u32[]{:S(2)}, u32[]{:S(2)}) collective-permute-start(bf16[8,32,2048]{2,1,0:T(8,128)(2,1)} %copy-done), channel_id=1, source_target_pairs={{0,1},{1,0},{2,3},{3,2},{4,5},{5,4},{6,7},{7,6},{8,9},{9,8},{10,11... | collective-permute-start | bytes 3145736 | tf_op jit(solution)/shard_map/ppermute | solution.py:208
  123.5 4.2 %collective-permute-start.24 = (bf16[8,32,2048]{2,1,0:T(8,128)(2,1)}, bf16[8,32,2048]{2,1,0:T(8,128)(2,1)}, u32[]{:S(2)}, u32[]{:S(2)}) collective-permute-start(bf16[8,32,2048]{2,1,0:T(8,128)(2,1)} %collective-permute-done.11), channel_id=1, source_target_pairs={{0,1},{1,0},{2,3},{3,2},{4,5},{5,4},{6,7},{7,6},{8,9},{9,8},{10,11... | collective-permute-start | bytes 3145736 | tf_op jit(solution)/shard_map/ppermute | solution.py:208
  123.8 5.5 %collective-permute-start.28 = (bf16[8,32,2048]{2,1,0:T(8,128)(2,1)}, bf16[8,32,2048]{2,1,0:T(8,128)(2,1)}, u32[]{:S(2)}, u32[]{:S(2)}) collective-permute-start(bf16[8,32,2048]{2,1,0:T(8,128)(2,1)} %collective-permute-done.10), channel_id=1, source_target_pairs={{0,1},{1,0},{2,3},{3,2},{4,5},{5,4},{6,7},{7,6},{8,9},{9,8},{10,11... | collective-permute-start | bytes 3145736 | tf_op jit(solution)/shard_map/ppermute | solution.py:208
  124.1 19.2 %collective-permute-start.26 = (bf16[8,32,2048]{2,1,0:T(8,128)(2,1)S(1)}, bf16[8,32,2048]{2,1,0:T(8,128)(2,1)}, u32[]{:S(2)}, u32[]{:S(2)}) collective-permute-start(bf16[8,32,2048]{2,1,0:T(8,128)(2,1)S(1)} %collective-permute-done.6), channel_id=1, source_target_pairs={{0,4},{1,33},{2,6},{3,35},{4,8},{5,37},{6,10},{7,39},{8,12},{9,41}... | collective-permute-start | bytes 3145736 | tf_op jit(solution)/shard_map/ppermute | solution.py:208
  125.0 18.3 %collective-permute-start.25 = (bf16[8,32,2048]{2,1,0:T(8,128)(2,1)}, bf16[8,32,2048]{2,1,0:T(8,128)(2,1)}, u32[]{:S(2)}, u32[]{:S(2)}) collective-permute-start(bf16[8,32,2048]{2,1,0:T(8,128)(2,1)} %collective-permute-done.11), channel_id=1, source_target_pairs={{0,12},{1,97},{2,14},{3,99},{4,0},{5,101},{6,2},{7,103},{8,4},{9,1... | collective-permute-start | bytes 3145736 | tf_op jit(solution)/shard_map/ppermute | solution.py:208
  143.4 4.4 %collective-permute-start.30 = (bf16[8,32,2048]{2,1,0:T(8,128)(2,1)}, bf16[8,32,2048]{2,1,0:T(8,128)(2,1)S(1)}, u32[]{:S(2)}, u32[]{:S(2)}) collective-permute-start(bf16[8,32,2048]{2,1,0:T(8,128)(2,1)} %collective-permute-done.25), channel_id=1, source_target_pairs={{0,1},{1,0},{2,3},{3,2},{4,5},{5,4},{6,7},{7,6},{8,9},{9,8},{10,11... | collective-permute-start | bytes 3145736 | tf_op jit(solution)/shard_map/ppermute | solution.py:208
  (12 other events, 127.5 us)
